TPU v7x, 128 devices: a whole 4x4x4 slice. The times are simulated.
128 devices in a mesh: slab: 32 (over z, x, core), face: 4 (over y).
Axes of the slice: x: 4, y: 4, z: 4, core: 2. Of those that a mesh axis runs over, the one named last changes fastest.
Arguments:
- displacement: float32 [6, 8192, 1024], P(None, 'slab', 'face'), may hold values from -6 to 6
- load: float32 [6, 8192, 1024], P(None, 'slab', 'face'), may hold values from -6 to 6
- stiffness: float32 [8192, 1024], P('slab', 'face'), may hold values from 0.02 to 0.5
- slave_row: int32 [16384], P(('slab', 'face')), may hold values from 0 to 255
- master_dev: int32 [16384, 1], P(('slab', 'face')), may hold values from 0 to 127; in each aligned block of 128 rows (0 to 127, 128 to 255, ...) at most 4 rows name the same one
- master_row: int32 [16384], P(('slab', 'face')), may hold values from 0 to 255
- seg_count: int32 [16384], P(('slab', 'face')), may hold values from 16 to 24
- quad_coords: float32 [16384, 4, 384], P(('slab', 'face')), may hold values from -0.98 to 0.98
- quad_weights: float32 [16384, 384], P(('slab', 'face')), may hold values from 0.002 to 0.02
Outputs:
- relaxed: float32 [6, 8192, 1024], P(None, 'slab', 'face')
- contact_gap: float32 [16384, 3, 256], P(('slab', 'face'))
Inputs may be any that keep to these rules, and one draw needn't show every extreme that they name: `master_dev`: among the 128 pairs of one device no owner device is named more than 4 times, and in some device one owner is named exactly 4 times.
All inputs are finite; a program needn't handle non-finite values.
Results may differ from a plain program's by a relative error of at most 0.0003.
Values sent between devices are 32-bit elements; how exact they have to be, the bound alone decides.
No kernel may reach another device: no remote copies, remote signals or barrier semaphores. Data moves between devices by JAX's collectives and lax.ppermute only.
A program may use at most 128 MiB of HBM per device.

v0:
```python
import math

import jax
import jax.numpy as jnp
from jax import lax
from jax.sharding import PartitionSpec as P

MODES = 16
QPTS = 16
CAP = 4
SWEEPS = 2


PENALTY = 0.5
RELAX = 0.8


def extended(cells, sides, width):
    for axis, dim in sides:
        count = lax.axis_size(axis)
        ends = count - 1
        head = lax.slice_in_dim(cells, 0, width, axis=dim)
        tail = lax.slice_in_dim(cells, cells.shape[dim] - width, cells.shape[dim], axis=dim)
        cells = jnp.concatenate(
            [
                lax.ppermute(tail, axis, [(i, (i + 1) % count) for i in range(ends)]),
                cells,
                lax.ppermute(head, axis, [((i + 1) % count, i) for i in range(ends)]),
            ],
            axis=dim,
        )
    return cells


def mode_table(coord_s, coord_t, mode_count):
    degree = jnp.arange(mode_count).astype(jnp.float32)
    along_s = jnp.cos(degree[:, None] * jnp.arccos(coord_s)[..., None, :])
    across = jnp.cos(degree[:, None] * jnp.arccos(coord_t)[..., None, :])
    tensor = along_s[..., :, None, :] * across[..., None, :, :]
    return tensor.reshape(tensor.shape[:-3] + (mode_count * mode_count, tensor.shape[-1]))


def mortar(slave_u, master_u, coords, weights):
    pair_total = slave_u.shape[0]
    block_size = math.gcd(pair_total, 32)
    highest = lax.Precision.HIGHEST

    def one_block(inputs):
        slave_part, master_part, coord_part, weight_part = inputs
        slave_tab = (
            mode_table(coord_part[:, 0], coord_part[:, 1], MODES) * weight_part[:, None, :]
        ).astype(jnp.bfloat16)
        master_tab = mode_table(coord_part[:, 2], coord_part[:, 3], MODES).astype(jnp.bfloat16)
        coupling = jnp.einsum(
            "bik,bjk->bij", slave_tab, master_tab, preferred_element_type=jnp.float32
        )
        pulled = jnp.einsum("bij,bcj->bci", coupling, master_part, precision=highest)
        gap_block = slave_part - pulled
        pushed_back = jnp.einsum("bci,bij->bcj", PENALTY * gap_block, coupling, precision=highest)
        return (gap_block, pushed_back)

    def blocked(array):
        return array.reshape((pair_total // block_size, block_size) + array.shape[1:])

    gap_all, pushed_all = lax.map(
        one_block, (blocked(slave_u), blocked(master_u), blocked(coords), blocked(weights))
    )
    return (gap_all.reshape(slave_u.shape), pushed_all.reshape(slave_u.shape))


def body(
    displacement,
    load,
    stiffness,
    slave_row,
    master_dev,
    master_row,
    seg_count,
    quad_coords,
    quad_weights,
):
    slab_count = lax.axis_size("slab")
    face_count = lax.axis_size("face")
    devices = slab_count * face_count
    components, row_count, node_count = displacement.shape
    pair_count = slave_row.shape[0]
    slot_count = devices * CAP
    highest = lax.Precision.HIGHEST
    target = master_dev[:, 0]
    dest_hits = (target[:, None] == jnp.arange(devices, dtype=jnp.int32)[None, :]).astype(jnp.int32)
    slot_rank = jnp.sum(jnp.cumsum(dest_hits, axis=0) * dest_hits, axis=1) - 1
    slot_index = target * CAP + slot_rank
    slot_hits = slot_index[None, :] == jnp.arange(slot_count, dtype=jnp.int32)[:, None]
    filled = jnp.any(slot_hits, axis=1)
    pair_of_slot = jnp.sum(
        jnp.where(slot_hits, jnp.arange(pair_count, dtype=jnp.int32)[None, :], 0), axis=1
    )
    active = jnp.arange(quad_weights.shape[1])[None, :] < (seg_count * QPTS)[:, None]
    weights = jnp.where(active, quad_weights, 0.0)
    slave_u = jnp.take(displacement[0:3], slave_row, axis=1).transpose(1, 0, 2)
    row_grid = jnp.arange(row_count, dtype=jnp.int32)[:, None]
    request = jnp.where(filled, jnp.take(master_row, pair_of_slot), -1)
    asked_rows = lax.all_to_all(request, ("slab", "face"), split_axis=0, concat_axis=0, tiled=True)
    served = jnp.take(displacement[3:6], jnp.maximum(asked_rows, 0), axis=1).transpose(1, 0, 2)
    served = jnp.where((asked_rows >= 0)[:, None, None], served, 0.0)
    arrived = lax.all_to_all(served, ("slab", "face"), split_axis=0, concat_axis=0, tiled=True)
    master_u = jnp.take(arrived, slot_index, axis=0)
    contact_gap, pushed_back = mortar(slave_u, master_u, quad_coords, weights)
    outgoing = jnp.where(filled[:, None, None], jnp.take(pushed_back, pair_of_slot, axis=0), 0.0)
    incoming = lax.all_to_all(outgoing, ("slab", "face"), split_axis=0, concat_axis=0, tiled=True)
    master_hits = (asked_rows[None, :] == row_grid).astype(jnp.float32)
    master_force = jnp.einsum("rs,scn->crn", master_hits, incoming, precision=highest)
    slave_hits = (slave_row[None, :] == row_grid).astype(jnp.float32)
    slave_force = jnp.einsum("rp,pcn->crn", slave_hits, -PENALTY * contact_gap, precision=highest)
    right_side = load + jnp.concatenate((slave_force, master_force), axis=0)
    diagonal = 4.0 + stiffness
    current = displacement
    for sweep_index in range(SWEEPS):
        padded = extended(current, (("slab", 1), ("face", 2)), 1)
        beside = (
            padded[:, 2:, 1:-1] + padded[:, :-2, 1:-1] + padded[:, 1:-1, 2:] + padded[:, 1:-1, :-2]
        )
        residual = right_side - (diagonal * current - beside)
        current = current + RELAX * residual / diagonal
    return (current, contact_gap)


def solution(mesh):
    return jax.shard_map(
        body,
        mesh=mesh,
        in_specs=(
            P(None, "slab", "face"),
            P(None, "slab", "face"),
            P("slab", "face"),
            P(("slab", "face")),
            P(("slab", "face"), None),
            P(("slab", "face")),
            P(("slab", "face")),
            P(("slab", "face"), None, None),
            P(("slab", "face"), None),
        ),
        out_specs=(P(None, "slab", "face"), P(("slab", "face"), None, None)),
        check_vma=False,
    )
```

profile of v0, /device:TPU:56, one launch (start us, length us, event | category | flops | bytes accessed | tf_op | source)
XLA Modules:
  0.0 371.2 jit_solution(16478715812362569087)
XLA Ops:
  3.6 3.3 gather_fusion.1
  7.9 10.1 %all-to-all-start = ((s32[128,4,1]{1,2,0:T(1,128)}), s32[128,4,1]{1,2,0:T(1,128)S(1)}, u32[]{:S(2)}, u32[]{:S(2)}) async-start(s32[128,4,1]{1,2,0:T(1,128)} %bitcast.17), calls=%async_computation | async-start | bytes 131072 | tf_op jit(solution)/shard_map/all_to_all | solution.py:103
  21.1 2.6 copy.59
  26.9 3.3 gather_fusion.2
  30.2 5.6 %select_select_fusion = f32[512,3,256]{2,1,0:T(4,128)} fusion(f32[512,3,256]{2,1,0:T(4,128)} %gather_fusion.2, pred[512]{0:T(512)(128)(4,1)S(1)} %get-tuple-element.100, pred[512]{0:T(512)(128)(4,1)S(1)} %get-tuple-element.99), kind=kLoop, calls=%fused_computation.31 | loop fusion | flops 786432 | bytes 3146752 | tf_op jit(solution)/shard_map/jit(_where)/select_n | solution.py:105
  35.9 8.8 %all-to-all-start.1 = ((f32[512,3,256]{2,1,0:T(4,128)}), f32[512,3,256]{2,1,0:T(4,128)}, u32[]{:S(2)}, u32[]{:S(2)}) async-start(f32[512,3,256]{2,1,0:T(4,128)} %select_select_fusion), calls=%async_computation.1 | async-start | bytes 4194304 | tf_op jit(solution)/shard_map/all_to_all | solution.py:106
  47.2 25.1 %all-to-all-done.1 = f32[512,3,256]{2,1,0:T(4,128)} async-done(((f32[512,3,256]{2,1,0:T(4,128)}), f32[512,3,256]{2,1,0:T(4,128)}, u32[]{:S(2)}, u32[]{:S(2)}) %all-to-all-start.1) | async-done | bytes 1572896 | tf_op jit(solution)/shard_map/all_to_all | solution.py:106
  72.3 3.2 gather_fusion.3
  76.8 204.4 %while.12 = (s32[]{:T(128)}, f32[4,32,3,256]{3,1,0,2:T(8,128)}, f32[4,32,3,256]{3,2,1,0:T(4,128)S(1)}, f32[4,32,3,256]{3,2,1,0:T(4,128)S(1)}, f32[4,32,3,256]{3,...) while((s32[]{:T(128)}, f32[4,32,3,256]{3,1,0,2:T(8,128)}, ...), condition=%wide.region_5.6_spmd, body=%wide.region_4.5_spmd.sunk | while | flops 1778319360 | bytes 84133592 | solution.py:65
  95.1 10.0 %multiply_cosine_fusion.5 = (f32[32,16,384]{2,1,0:T(8,128)S(1)}, f32[32,16,384]{2,1,0:T(8,128)S(1)}, f32[32,16,384]{2,1,0:T(8,128)S(1)}, f32[32,16,384]{2,1,0:T(8,128)S(1)}) fusion(f32[32,384]{1,0:T(8,128)S(1)} %get-tuple-element.154, f32[16]{0:T(128)S(1)} %iota_convert_fusion.2, f32[32,384]{1,0:T(8,128)S(1)} %get-tuple-element.155, ...), kind=kLoop, calls=%fused_computation.13.clone.1 | loop fusion | flops 786432 | bytes 3342400 | tf_op jit(solution)/shard_map/while/body/eval_jaxpr/cos | solution.py:37
  105.1 7.9 %multiply_convert_fusion.2 = (bf16[32,16,16,384]{3,2,1,0:T(8,128)(2,1)}, f32[32,16,16,384]{3,2,1,0:T(8,128)}) fusion(f32[32,16,384]{2,1,0:T(8,128)S(1)} %get-tuple-element.158, f32[32,16,384]{2,1,0:T(8,128)S(1)} %get-tuple-element.159, f32[32,16,384]{2,1,0:T(8,128)S(1)} %get-tuple-element.160, f32[32,16,384]{2,1,0:T(8,128)S(1)} %get-tuple-element.161), kind=kLoop, calls=%fused_computation.7.clone.1 | loop fusion | flops 9437184 | bytes 22020096 | tf_op jit(solution)/shard_map/while/body/eval_jaxpr/convert_element_type | solution.py:53
  113.1 8.8 %fusion.66 = bf16[32,256,384]{2,1,0:T(8,128)(2,1)} fusion(f32[32,16,16,384]{3,2,1,0:T(8,128)} %get-tuple-element.162, f32[32,384]{1,0:T(8,128)S(1)} %dynamic-slice_bitcast_fusion.2), kind=kLoop, calls=%fused_computation.6.clone.1 | loop fusion | flops 6291456 | bytes 18923520 | tf_op jit(solution)/shard_map/while/body/eval_jaxpr/convert_element_type | solution.py:52
  121.9 7.0 %fusion.67 = f32[32,256,256]{2,1,0:T(8,128)S(1)} fusion(bf16[32,256,384]{2,1,0:T(8,128)(2,1)} %fusion.66, bf16[32,256,384]{2,1,0:T(8,128)(2,1)} %bitcast.89), kind=kOutput, calls=%fused_computation.116.clone.1 | convolution fusion | flops 1610612736 | bytes 20971520 | tf_op jit(solution)/shard_map/while/body/eval_jaxpr/bik,bjk->bij/dot_general | solution.py:54
  128.9 7.0 %convolution_subtract_fusion.2 = f32[32,3,256]{2,1,0:T(4,128)S(1)} fusion(f32[32,256,256]{2,1,0:T(8,128)S(1)} %fusion.67, f32[4,32,3,256]{3,2,1,0:T(4,128)S(1)} %get-tuple-element.184, s32[]{:T(128)} %get-tuple-element.172, f32[4,32,3,256]{3,2,1,0:T(4,128)S(1)} %get-tuple-element.183), kind=kOutput, calls=%fused_computation.11.clone.1 | convolution fusion | flops 75522048 | bytes 8750080 | tf_op jit(solution)/shard_map/while/body/eval_jaxpr/bij,bcj->bci/dot_general | solution.py:57
  135.9 4.1 %fusion.68 = f32[4,32,3,256]{3,2,1,0:T(4,128)S(1)} fusion(f32[4,32,3,256]{3,2,1,0:T(4,128)S(1)} %get-tuple-element.174, s32[]{:T(128)} %get-tuple-element.172, f32[32,256,256]{2,1,0:T(8,128)S(1)} %fusion.67, f32[32,3,256]{2,1,0:T(4,128)S(1)} %convolution_subtract_fusion.2), kind=kOutput, calls=%fused_computation.10.clone.1 | convolution fusion | flops 75522048 | bytes 8650756 | tf_op jit(solution)/shard_map/while/body/eval_jaxpr/bci,bij->bcj/dot_general | solution.py:59
  142.0 10.0 %multiply_cosine_fusion.5 = (f32[32,16,384]{2,1,0:T(8,128)S(1)}, f32[32,16,384]{2,1,0:T(8,128)S(1)}, f32[32,16,384]{2,1,0:T(8,128)S(1)}, f32[32,16,384]{2,1,0:T(8,128)S(1)}) fusion(f32[32,384]{1,0:T(8,128)S(1)} %get-tuple-element.154, f32[16]{0:T(128)S(1)} %iota_convert_fusion.2, f32[32,384]{1,0:T(8,128)S(1)} %get-tuple-element.155, ...), kind=kLoop, calls=%fused_computation.13.clone.1 | loop fusion | flops 786432 | bytes 3342400 | tf_op jit(solution)/shard_map/while/body/eval_jaxpr/cos | solution.py:37
  152.0 7.9 %multiply_convert_fusion.2 = (bf16[32,16,16,384]{3,2,1,0:T(8,128)(2,1)}, f32[32,16,16,384]{3,2,1,0:T(8,128)}) fusion(f32[32,16,384]{2,1,0:T(8,128)S(1)} %get-tuple-element.158, f32[32,16,384]{2,1,0:T(8,128)S(1)} %get-tuple-element.159, f32[32,16,384]{2,1,0:T(8,128)S(1)} %get-tuple-element.160, f32[32,16,384]{2,1,0:T(8,128)S(1)} %get-tuple-element.161), kind=kLoop, calls=%fused_computation.7.clone.1 | loop fusion | flops 9437184 | bytes 22020096 | tf_op jit(solution)/shard_map/while/body/eval_jaxpr/convert_element_type | solution.py:53
  159.9 8.8 %fusion.66 = bf16[32,256,384]{2,1,0:T(8,128)(2,1)} fusion(f32[32,16,16,384]{3,2,1,0:T(8,128)} %get-tuple-element.162, f32[32,384]{1,0:T(8,128)S(1)} %dynamic-slice_bitcast_fusion.2), kind=kLoop, calls=%fused_computation.6.clone.1 | loop fusion | flops 6291456 | bytes 18923520 | tf_op jit(solution)/shard_map/while/body/eval_jaxpr/convert_element_type | solution.py:52
  168.7 7.0 %fusion.67 = f32[32,256,256]{2,1,0:T(8,128)S(1)} fusion(bf16[32,256,384]{2,1,0:T(8,128)(2,1)} %fusion.66, bf16[32,256,384]{2,1,0:T(8,128)(2,1)} %bitcast.89), kind=kOutput, calls=%fused_computation.116.clone.1 | convolution fusion | flops 1610612736 | bytes 20971520 | tf_op jit(solution)/shard_map/while/body/eval_jaxpr/bik,bjk->bij/dot_general | solution.py:54
  175.7 7.0 %convolution_subtract_fusion.2 = f32[32,3,256]{2,1,0:T(4,128)S(1)} fusion(f32[32,256,256]{2,1,0:T(8,128)S(1)} %fusion.67, f32[4,32,3,256]{3,2,1,0:T(4,128)S(1)} %get-tuple-element.184, s32[]{:T(128)} %get-tuple-element.172, f32[4,32,3,256]{3,2,1,0:T(4,128)S(1)} %get-tuple-element.183), kind=kOutput, calls=%fused_computation.11.clone.1 | convolution fusion | flops 75522048 | bytes 8750080 | tf_op jit(solution)/shard_map/while/body/eval_jaxpr/bij,bcj->bci/dot_general | solution.py:57
  182.7 4.1 %fusion.68 = f32[4,32,3,256]{3,2,1,0:T(4,128)S(1)} fusion(f32[4,32,3,256]{3,2,1,0:T(4,128)S(1)} %get-tuple-element.174, s32[]{:T(128)} %get-tuple-element.172, f32[32,256,256]{2,1,0:T(8,128)S(1)} %fusion.67, f32[32,3,256]{2,1,0:T(4,128)S(1)} %convolution_subtract_fusion.2), kind=kOutput, calls=%fused_computation.10.clone.1 | convolution fusion | flops 75522048 | bytes 8650756 | tf_op jit(solution)/shard_map/while/body/eval_jaxpr/bci,bij->bcj/dot_general | solution.py:59
  188.8 10.0 %multiply_cosine_fusion.5 = (f32[32,16,384]{2,1,0:T(8,128)S(1)}, f32[32,16,384]{2,1,0:T(8,128)S(1)}, f32[32,16,384]{2,1,0:T(8,128)S(1)}, f32[32,16,384]{2,1,0:T(8,128)S(1)}) fusion(f32[32,384]{1,0:T(8,128)S(1)} %get-tuple-element.154, f32[16]{0:T(128)S(1)} %iota_convert_fusion.2, f32[32,384]{1,0:T(8,128)S(1)} %get-tuple-element.155, ...), kind=kLoop, calls=%fused_computation.13.clone.1 | loop fusion | flops 786432 | bytes 3342400 | tf_op jit(solution)/shard_map/while/body/eval_jaxpr/cos | solution.py:37
  198.8 7.9 %multiply_convert_fusion.2 = (bf16[32,16,16,384]{3,2,1,0:T(8,128)(2,1)}, f32[32,16,16,384]{3,2,1,0:T(8,128)}) fusion(f32[32,16,384]{2,1,0:T(8,128)S(1)} %get-tuple-element.158, f32[32,16,384]{2,1,0:T(8,128)S(1)} %get-tuple-element.159, f32[32,16,384]{2,1,0:T(8,128)S(1)} %get-tuple-element.160, f32[32,16,384]{2,1,0:T(8,128)S(1)} %get-tuple-element.161), kind=kLoop, calls=%fused_computation.7.clone.1 | loop fusion | flops 9437184 | bytes 22020096 | tf_op jit(solution)/shard_map/while/body/eval_jaxpr/convert_element_type | solution.py:53
  206.8 8.8 %fusion.66 = bf16[32,256,384]{2,1,0:T(8,128)(2,1)} fusion(f32[32,16,16,384]{3,2,1,0:T(8,128)} %get-tuple-element.162, f32[32,384]{1,0:T(8,128)S(1)} %dynamic-slice_bitcast_fusion.2), kind=kLoop, calls=%fused_computation.6.clone.1 | loop fusion | flops 6291456 | bytes 18923520 | tf_op jit(solution)/shard_map/while/body/eval_jaxpr/convert_element_type | solution.py:52
  215.6 7.0 %fusion.67 = f32[32,256,256]{2,1,0:T(8,128)S(1)} fusion(bf16[32,256,384]{2,1,0:T(8,128)(2,1)} %fusion.66, bf16[32,256,384]{2,1,0:T(8,128)(2,1)} %bitcast.89), kind=kOutput, calls=%fused_computation.116.clone.1 | convolution fusion | flops 1610612736 | bytes 20971520 | tf_op jit(solution)/shard_map/while/body/eval_jaxpr/bik,bjk->bij/dot_general | solution.py:54
  222.6 7.0 %convolution_subtract_fusion.2 = f32[32,3,256]{2,1,0:T(4,128)S(1)} fusion(f32[32,256,256]{2,1,0:T(8,128)S(1)} %fusion.67, f32[4,32,3,256]{3,2,1,0:T(4,128)S(1)} %get-tuple-element.184, s32[]{:T(128)} %get-tuple-element.172, f32[4,32,3,256]{3,2,1,0:T(4,128)S(1)} %get-tuple-element.183), kind=kOutput, calls=%fused_computation.11.clone.1 | convolution fusion | flops 75522048 | bytes 8750080 | tf_op jit(solution)/shard_map/while/body/eval_jaxpr/bij,bcj->bci/dot_general | solution.py:57
  229.6 4.1 %fusion.68 = f32[4,32,3,256]{3,2,1,0:T(4,128)S(1)} fusion(f32[4,32,3,256]{3,2,1,0:T(4,128)S(1)} %get-tuple-element.174, s32[]{:T(128)} %get-tuple-element.172, f32[32,256,256]{2,1,0:T(8,128)S(1)} %fusion.67, f32[32,3,256]{2,1,0:T(4,128)S(1)} %convolution_subtract_fusion.2), kind=kOutput, calls=%fused_computation.10.clone.1 | convolution fusion | flops 75522048 | bytes 8650756 | tf_op jit(solution)/shard_map/while/body/eval_jaxpr/bci,bij->bcj/dot_general | solution.py:59
  235.7 10.0 %multiply_cosine_fusion.5 = (f32[32,16,384]{2,1,0:T(8,128)S(1)}, f32[32,16,384]{2,1,0:T(8,128)S(1)}, f32[32,16,384]{2,1,0:T(8,128)S(1)}, f32[32,16,384]{2,1,0:T(8,128)S(1)}) fusion(f32[32,384]{1,0:T(8,128)S(1)} %get-tuple-element.154, f32[16]{0:T(128)S(1)} %iota_convert_fusion.2, f32[32,384]{1,0:T(8,128)S(1)} %get-tuple-element.155, ...), kind=kLoop, calls=%fused_computation.13.clone.1 | loop fusion | flops 786432 | bytes 3342400 | tf_op jit(solution)/shard_map/while/body/eval_jaxpr/cos | solution.py:37
  245.7 7.9 %multiply_convert_fusion.2 = (bf16[32,16,16,384]{3,2,1,0:T(8,128)(2,1)}, f32[32,16,16,384]{3,2,1,0:T(8,128)}) fusion(f32[32,16,384]{2,1,0:T(8,128)S(1)} %get-tuple-element.158, f32[32,16,384]{2,1,0:T(8,128)S(1)} %get-tuple-element.159, f32[32,16,384]{2,1,0:T(8,128)S(1)} %get-tuple-element.160, f32[32,16,384]{2,1,0:T(8,128)S(1)} %get-tuple-element.161), kind=kLoop, calls=%fused_computation.7.clone.1 | loop fusion | flops 9437184 | bytes 22020096 | tf_op jit(solution)/shard_map/while/body/eval_jaxpr/convert_element_type | solution.py:53
  253.6 8.8 %fusion.66 = bf16[32,256,384]{2,1,0:T(8,128)(2,1)} fusion(f32[32,16,16,384]{3,2,1,0:T(8,128)} %get-tuple-element.162, f32[32,384]{1,0:T(8,128)S(1)} %dynamic-slice_bitcast_fusion.2), kind=kLoop, calls=%fused_computation.6.clone.1 | loop fusion | flops 6291456 | bytes 18923520 | tf_op jit(solution)/shard_map/while/body/eval_jaxpr/convert_element_type | solution.py:52
  262.4 7.0 %fusion.67 = f32[32,256,256]{2,1,0:T(8,128)S(1)} fusion(bf16[32,256,384]{2,1,0:T(8,128)(2,1)} %fusion.66, bf16[32,256,384]{2,1,0:T(8,128)(2,1)} %bitcast.89), kind=kOutput, calls=%fused_computation.116.clone.1 | convolution fusion | flops 1610612736 | bytes 20971520 | tf_op jit(solution)/shard_map/while/body/eval_jaxpr/bik,bjk->bij/dot_general | solution.py:54
  269.4 7.0 %convolution_subtract_fusion.2 = f32[32,3,256]{2,1,0:T(4,128)S(1)} fusion(f32[32,256,256]{2,1,0:T(8,128)S(1)} %fusion.67, f32[4,32,3,256]{3,2,1,0:T(4,128)S(1)} %get-tuple-element.184, s32[]{:T(128)} %get-tuple-element.172, f32[4,32,3,256]{3,2,1,0:T(4,128)S(1)} %get-tuple-element.183), kind=kOutput, calls=%fused_computation.11.clone.1 | convolution fusion | flops 75522048 | bytes 8750080 | tf_op jit(solution)/shard_map/while/body/eval_jaxpr/bij,bcj->bci/dot_general | solution.py:57
  276.4 4.1 %fusion.68 = f32[4,32,3,256]{3,2,1,0:T(4,128)S(1)} fusion(f32[4,32,3,256]{3,2,1,0:T(4,128)S(1)} %get-tuple-element.174, s32[]{:T(128)} %get-tuple-element.172, f32[32,256,256]{2,1,0:T(8,128)S(1)} %fusion.67, f32[32,3,256]{2,1,0:T(4,128)S(1)} %convolution_subtract_fusion.2), kind=kOutput, calls=%fused_computation.10.clone.1 | convolution fusion | flops 75522048 | bytes 8650756 | tf_op jit(solution)/shard_map/while/body/eval_jaxpr/bci,bij->bcj/dot_general | solution.py:59
  281.2 3.3 gather_fusion.4
  284.5 5.6 %select_select_fusion.1 = f32[512,3,256]{2,1,0:T(4,128)} fusion(f32[512,3,256]{2,1,0:T(4,128)} %gather_fusion.4, pred[512]{0:T(512)(128)(4,1)S(1)} %compare_and_fusion, pred[512]{0:T(512)(128)(4,1)S(1)} %fusion.33), kind=kLoop, calls=%fused_computation.32 | loop fusion | flops 786432 | bytes 3146752 | tf_op jit(solution)/shard_map/jit(_where)/select_n | solution.py:109
  290.1 7.5 %all-to-all-start.2 = ((f32[512,3,256]{2,1,0:T(4,128)}), f32[512,3,256]{2,1,0:T(4,128)}, u32[]{:S(2)}, u32[]{:S(2)}) async-start(f32[512,3,256]{2,1,0:T(4,128)} %select_select_fusion.1), calls=%async_computation.2 | async-start | bytes 4194304 | tf_op jit(solution)/shard_map/all_to_all | solution.py:110
  297.7 4.1 %collective-permute-start = (f32[6,1,256]{2,1,0:T(1,128)S(1)}, f32[6,1,256]{2,1,0:T(1,128)S(1)}, u32[]{:S(2)}, u32[]{:S(2)}) collective-permute-start(f32[6,1,256]{2,1,0:T(1,128)S(1)} %get-tuple-element.98), channel_id=1, source_target_pairs={{4,0},{8,4},{12,8},{16,12},{20,16},{24,20},{28,24},{32,28},{36,32}... | collective-permute-start | bytes 18440 | tf_op jit(solution)/shard_map/ppermute | solution.py:28
  303.7 14.7 %collective-permute-done = f32[6,1,256]{2,1,0:T(1,128)S(1)} collective-permute-done((f32[6,1,256]{2,1,0:T(1,128)S(1)}, f32[6,1,256]{2,1,0:T(1,128)S(1)}, u32[]{:S(2)}, u32[]{:S(2)}) %collective-permute-start) | collective-permute-done | bytes 6176 | tf_op jit(solution)/shard_map/ppermute | solution.py:28
  318.4 3.7 collective-permute-done.1
  322.9 2.7 collective-permute-start.2
  332.7 2.4 convolution_bitcast_fusion.1
  335.2 2.7 fusion.26
  337.9 4.3 %fusion.21 = f32[6,256,256]{2,1,0:T(8,128)S(1)} fusion(f32[6,256,256]{2,1,0:T(8,128)S(1)} %copy-done.2, f32[6,258,1]{2,1,0:T(8,128)} %copy.49, f32[6,1,256]{2,1,0:T(1,128)S(1)} %collective-permute-done, f32[6,1,256]{2,1,0:T(1,128)S(1)} %collective-permute-done.1, f32[6,258,1]{2,1,0:T(8,128)} %copy.47, f32[256,256]{1,0:T(8,128)S(1)} %broadcast_add_fusion, ...), kind=kLoop, calls=%fused_computation.57 | loop fusion | flops 7471104 | bytes 6578272 | tf_op jit(solution)/shard_map/add | solution.py:124
  344.2 2.4 collective-permute-start.5
  346.6 4.6 %collective-permute-done.5 = f32[6,1,256]{2,1,0:T(1,128)S(1)} collective-permute-done((f32[6,1,256]{2,1,0:T(1,128)S(1)}, f32[6,1,256]{2,1,0:T(1,128)S(1)}, u32[]{:S(2)}, u32[]{:S(2)}) %collective-permute-start.5) | collective-permute-done | bytes 6176 | tf_op jit(solution)/shard_map/ppermute | solution.py:26
  354.4 3.1 collective-permute-start.6
  361.6 3.0 collective-permute-done.7
  365.8 5.0 %fusion.13 = f32[6,256,256]{2,1,0:T(8,128)} fusion(f32[6,256,256]{2,1,0:T(8,128)S(1)} %fusion.21, f32[6,258,1]{2,1,0:T(8,128)} %copy.53, f32[6,1,256]{2,1,0:T(1,128)S(1)} %collective-permute-done.4, f32[6,1,256]{2,1,0:T(1,128)S(1)} %collective-permute-done.5, f32[6,258,1]{2,1,0:T(8,128)} %copy.51, f32[256,256]{1,0:T(8,128)S(1)} %broadcast_add_fusion, ...), kind=kLoop, calls=%fused_computation.41 | loop fusion | flops 7471104 | bytes 6578272 | tf_op jit(solution)/shard_map/add | solution.py:124
  (106 shorter events, 42.0 us)
Async XLA Ops:
  0.6 3.0 copy-start
  0.6 17.3 %copy-start.2 = (f32[6,256,256]{2,1,0:T(8,128)S(1)}, f32[6,256,256]{2,1,0:T(8,128)}, u32[]{:S(2)}) copy-start(f32[6,256,256]{2,1,0:T(8,128)} %param.11) | copy-start | bytes 4718596
  7.9 17.3 %all-to-all-start = ((s32[128,4,1]{1,2,0:T(1,128)}), s32[128,4,1]{1,2,0:T(1,128)S(1)}, u32[]{:S(2)}, u32[]{:S(2)}) async-start(s32[128,4,1]{1,2,0:T(1,128)} %bitcast.17), calls=%async_computation | async-start | bytes 131072 | tf_op jit(solution)/shard_map/all_to_all | solution.py:103
  18.0 1.4 copy-start.8
  35.9 8.8 %copy-start.9 = (s32[128]{0:T(128)S(1)}, s32[128]{0:T(128)}, u32[]{:S(2)}) copy-start(s32[128]{0:T(128)} %param.14) | copy-start | bytes 1540
  35.9 11.0 %copy-start.10 = (s32[128]{0:T(128)S(1)}, s32[128]{0:T(128)}, u32[]{:S(2)}) copy-start(s32[128]{0:T(128)} %param.17) | copy-start | bytes 1540
  35.9 11.0 %copy-start.7 = (f32[128,384]{1,0:T(8,128)S(1)}, f32[128,384]{1,0:T(8,128)}, u32[]{:S(2)}) copy-start(f32[128,384]{1,0:T(8,128)} %param.19) | copy-start | bytes 589828
  35.9 36.4 %all-to-all-start.1 = ((f32[512,3,256]{2,1,0:T(4,128)}), f32[512,3,256]{2,1,0:T(4,128)}, u32[]{:S(2)}, u32[]{:S(2)}) async-start(f32[512,3,256]{2,1,0:T(4,128)} %select_select_fusion), calls=%async_computation.1 | async-start | bytes 4194304 | tf_op jit(solution)/shard_map/all_to_all | solution.py:106
  290.1 45.0 %all-to-all-start.2 = ((f32[512,3,256]{2,1,0:T(4,128)}), f32[512,3,256]{2,1,0:T(4,128)}, u32[]{:S(2)}, u32[]{:S(2)}) async-start(f32[512,3,256]{2,1,0:T(4,128)} %select_select_fusion.1), calls=%async_computation.2 | async-start | bytes 4194304 | tf_op jit(solution)/shard_map/all_to_all | solution.py:110
  297.7 20.7 %collective-permute-start = (f32[6,1,256]{2,1,0:T(1,128)S(1)}, f32[6,1,256]{2,1,0:T(1,128)S(1)}, u32[]{:S(2)}, u32[]{:S(2)}) collective-permute-start(f32[6,1,256]{2,1,0:T(1,128)S(1)} %get-tuple-element.98), channel_id=1, source_target_pairs={{4,0},{8,4},{12,8},{16,12},{20,16},{24,20},{28,24},{32,28},{36,32}... | collective-permute-start | bytes 18440 | tf_op jit(solution)/shard_map/ppermute | solution.py:28
  301.8 20.3 %collective-permute-start.1 = (f32[6,1,256]{2,1,0:T(1,128)S(1)}, f32[6,1,256]{2,1,0:T(1,128)S(1)}, u32[]{:S(2)}, u32[]{:S(2)}) collective-permute-start(f32[6,1,256]{2,1,0:T(1,128)S(1)} %get-tuple-element.97), channel_id=1, source_target_pairs={{0,4},{4,8},{8,12},{12,16},{16,20},{20,24},{24,28},{28,32},{32,36}... | collective-permute-start | bytes 18440 | tf_op jit(solution)/shard_map/ppermute | solution.py:26
  322.9 5.4 %collective-permute-start.2 = (f32[6,258,1]{1,2,0:T(1,128)S(1)}, f32[6,258,1]{1,2,0:T(1,128)S(1)}, u32[]{:S(2)}, u32[]{:S(2)}) collective-permute-start(f32[6,258,1]{1,2,0:T(1,128)S(1)} %copy.46), channel_id=1, source_target_pairs={{1,0},{2,1},{3,2},{5,4},{6,5},{7,6},{9,8},{10,9},{11,10},{13,12},{... | collective-permute-start | bytes 18584 | tf_op jit(solution)/shard_map/ppermute | solution.py:28
  326.0 5.6 %collective-permute-start.3 = (f32[6,258,1]{1,2,0:T(1,128)S(1)}, f32[6,258,1]{1,2,0:T(1,128)S(1)}, u32[]{:S(2)}, u32[]{:S(2)}) collective-permute-start(f32[6,258,1]{1,2,0:T(1,128)S(1)} %copy.48), channel_id=1, source_target_pairs={{0,1},{1,2},{2,3},{4,5},{5,6},{6,7},{8,9},{9,10},{10,11},{12,13},{... | collective-permute-start | bytes 18584 | tf_op jit(solution)/shard_map/ppermute | solution.py:26
  335.2 2.7 copy-start.3
  337.9 4.4 %copy-start.5 = (f32[3,256,256]{2,1,0:T(8,128)}, f32[3,256,256]{2,1,0:T(8,128)S(1)}, u32[]{:S(2)}) copy-start(f32[3,256,256]{2,1,0:T(8,128)S(1)} %fusion.26) | copy-start | bytes 2359300
  342.3 4.3 %collective-permute-start.4 = (f32[6,1,256]{2,1,0:T(1,128)S(1)}, f32[6,1,256]{2,1,0:T(1,128)S(1)}, u32[]{:S(2)}, u32[]{:S(2)}) collective-permute-start(f32[6,1,256]{2,1,0:T(1,128)S(1)} %get-tuple-element.94), channel_id=1, source_target_pairs={{4,0},{8,4},{12,8},{16,12},{20,16},{24,20},{28,24},{32,28},{36,32}... | collective-permute-start | bytes 18440 | tf_op jit(solution)/shard_map/ppermute | solution.py:28
  344.2 7.1 %collective-permute-start.5 = (f32[6,1,256]{2,1,0:T(1,128)S(1)}, f32[6,1,256]{2,1,0:T(1,128)S(1)}, u32[]{:S(2)}, u32[]{:S(2)}) collective-permute-start(f32[6,1,256]{2,1,0:T(1,128)S(1)} %get-tuple-element.93), channel_id=1, source_target_pairs={{0,4},{4,8},{8,12},{12,16},{16,20},{20,24},{24,28},{28,32},{32,36}... | collective-permute-start | bytes 18440 | tf_op jit(solution)/shard_map/ppermute | solution.py:26
  352.8 13.0 %copy-start.4 = (f32[3,256,256]{2,1,0:T(8,128)S(1)}, f32[3,256,256]{2,1,0:T(8,128)}, u32[]{:S(2)}) copy-start(f32[3,256,256]{2,1,0:T(8,128)} %convolution_bitcast_fusion.1) | copy-start | bytes 2359300
  352.8 13.0 %copy-start.6 = (f32[3,256,256]{2,1,0:T(8,128)S(1)}, f32[3,256,256]{2,1,0:T(8,128)}, u32[]{:S(2)}) copy-start(f32[3,256,256]{2,1,0:T(8,128)} %copy-done.5) | copy-start | bytes 2359300
  354.4 5.9 %collective-permute-start.6 = (f32[6,258,1]{1,2,0:T(1,128)S(1)}, f32[6,258,1]{1,2,0:T(1,128)S(1)}, u32[]{:S(2)}, u32[]{:S(2)}) collective-permute-start(f32[6,258,1]{1,2,0:T(1,128)S(1)} %copy.50), channel_id=1, source_target_pairs={{1,0},{2,1},{3,2},{5,4},{6,5},{7,6},{9,8},{10,9},{11,10},{13,12},{... | collective-permute-start | bytes 18584 | tf_op jit(solution)/shard_map/ppermute | solution.py:28
  359.0 5.6 %collective-permute-start.7 = (f32[6,258,1]{1,2,0:T(1,128)S(1)}, f32[6,258,1]{1,2,0:T(1,128)S(1)}, u32[]{:S(2)}, u32[]{:S(2)}) collective-permute-start(f32[6,258,1]{1,2,0:T(1,128)S(1)} %copy.52), channel_id=1, source_target_pairs={{0,1},{1,2},{2,3},{4,5},{5,6},{6,7},{8,9},{9,10},{10,11},{12,13},{... | collective-permute-start | bytes 18584 | tf_op jit(solution)/shard_map/ppermute | solution.py:26
  365.8 5.0 %copy-start.1 = (s32[128]{0:T(128)S(1)}, s32[128]{0:T(128)}, u32[]{:S(2)}) copy-start(s32[128]{0:T(128)} %param.16) | copy-start | bytes 1540
where the time goes:
time: 378 us; the launch traced here: 371 us
  other arithmetic  136 us (36%)
  matrix products  77.4 us (20%)
  waiting for transfers between devices  54.6 us (14%)
  starting transfers between devices  45.2 us (12%)
  local copies, waits for them, and re-layouts  39.3 us (10%)
  loops' own time  17.1 us (5%)
    cos x4, other arithmetic, mode_table(): along_s = jnp.cos(degree[:, None] * jnp.arccos(coord_s)[..., None, :])  40 us
    convert_element_type x4, other arithmetic, one_block(): slave_tab = (mode_table(coord_part[:, 0], coord_part[:, 1], MODES) * weig...  35.3 us
    convert_element_type x4, other arithmetic, one_block(): mode_table(coord_part[:, 2], coord_part[:, 3], MODES).astype(jnp.bfloat16)  31.7 us
    dot_general x4, matrix products, one_block(): jnp.einsum('bij,bcj->bci', coupling, master_part, precision=highest)  27.9 us
    dot_general x4, matrix products, one_block(): jnp.einsum('bik,bjk->bij', slave_tab, master_tab, preferred_element_type=...  27.9 us
    all_to_all x1, waiting for transfers between devices, body(): lax.all_to_all(served, ('slab', 'face'), split_axis=0, concat_axis=0, til...  25.1 us
    another operation x1, loops' own time, mortar(): lax.map(one_block, (blocked(slave_u), blocked(master_u), blocked(coords),...  17.1 us
    dot_general x4, matrix products, one_block(): jnp.einsum('bci,bij->bcj', PENALTY * gap_block, coupling, precision=highest)  16.4 us
  transfers between devices with their start and end apart: 11, of which 7 were waited for; matrix products, arithmetic and copies ran while one was open for 5% of the time, Pallas kernels for 0%

commit v1 on v0

v1 whole, which is shorter than its diff:
```python
import functools

import jax
import jax.numpy as jnp
from jax import lax
from jax.experimental import pallas as pl
from jax.experimental.pallas import tpu as pltpu
from jax.sharding import PartitionSpec as P

MODES = 16
QPTS = 16
CAP = 4
PENALTY = 0.5
RELAX = 0.8
DEVICES = 128
PAIRS = 128
NODES = 256
ROWS = 256
PARTS = 6
SLOT_ROWS = DEVICES * CAP * PARTS
PAIR_BLOCK = 8

f32 = jnp.float32
bf16 = jnp.bfloat16
AXES = ("slab", "face")


def vmem():
    return pl.BlockSpec(memory_space=pltpu.VMEM)


def smem():
    return pl.BlockSpec(memory_space=pltpu.SMEM)


def params():
    return pltpu.CompilerParams(vmem_limit_bytes=48 << 20)


def slots_kernel(dev_ref, row_ref, request_ref, slot_ref):
    dev = dev_ref[...]
    row = row_ref[...]
    spread = jnp.broadcast_to(dev, (PAIRS, PAIRS))
    across = jnp.transpose(spread)
    first = lax.broadcasted_iota(jnp.int32, (PAIRS, PAIRS), 0)
    second = lax.broadcasted_iota(jnp.int32, (PAIRS, PAIRS), 1)
    same = jnp.where((spread == across) & (first < second), 1.0, 0.0)
    rank = jnp.sum(same, axis=0, keepdims=True).astype(jnp.int32)
    slot_ref[...] = dev * CAP + rank
    hits = spread == first
    result = jnp.full((DEVICES, 128), -1, jnp.int32)
    for k in range(CAP):
        chosen = jnp.where(hits & (rank == k), (row + 1).astype(f32), 0.0)
        found = jnp.sum(chosen, axis=1, keepdims=True).astype(jnp.int32) - 1
        result = jnp.where(second == k, found, result)
    request_ref[...] = result.reshape(DEVICES, 1, 128)


def slots(dev, row):
    return pl.pallas_call(
        slots_kernel,
        out_shape=[
            jax.ShapeDtypeStruct((DEVICES, 1, 128), jnp.int32),
            jax.ShapeDtypeStruct((1, PAIRS), jnp.int32),
        ],
        in_specs=[vmem(), vmem()],
        out_specs=[vmem(), vmem()],
        name="slots",
    )(dev, row)


def serve_kernel(asked_ref, field_ref, out_ref):
    def one(s, carry):
        for k in range(CAP):
            r = jnp.maximum(asked_ref[s * 128 + k], 0)
            for c in range(3):
                line = field_ref[c, pl.ds(r, 1), :]
                out_ref[s, pl.ds(k * PARTS + c, 1), :] = line[:, 0:128]
                out_ref[s, pl.ds(k * PARTS + 3 + c, 1), :] = line[:, 128:256]
        return carry

    lax.fori_loop(0, DEVICES, one, 0, unroll=4)


def serve(asked, field):
    return pl.pallas_call(
        serve_kernel,
        grid=(1,),
        out_shape=jax.ShapeDtypeStruct((DEVICES, CAP * PARTS, 128), f32),
        in_specs=[smem(), pl.BlockSpec((3, ROWS, NODES), lambda i: (1, 0, 0))],
        out_specs=pl.BlockSpec((DEVICES, CAP * PARTS, 128), lambda i: (0, 0, 0)),
        compiler_params=params(),
        name="serve",
    )(asked, field)


def two_pieces(u):
    high = u.astype(bf16)
    low = u - high.astype(f32)
    return jnp.concatenate([high.astype(f32), low], axis=0).astype(bf16)


def times(pieces, table):
    both = lax.dot_general(pieces, table, (((1,), (0,)), ((), ())), preferred_element_type=f32)
    return both[0:8] + both[8:16]


def times_transposed(pieces, table):
    both = lax.dot_general(pieces, table, (((1,), (1,)), ((), ())), preferred_element_type=f32)
    return both[0:8] + both[8:16]


def mortar_kernel(
    slot_ref, row_ref, coords_ref, weights_ref, field_ref, load_ref, arrived_ref,
    gap_ref, outgoing_ref, right_ref, modes, slave_tab, master_tab,
):
    step = pl.program_id(0)

    @pl.when(step == 0)
    def _():
        outgoing_ref[...] = jnp.zeros_like(outgoing_ref)
        right_ref[...] = load_ref[...]

    for k in range(4):
        x = coords_ref[k]
        now = weights_ref[...] if k == 0 else jnp.ones_like(x)
        later = now * x
        twice = x + x
        for n in range(MODES):
            modes[k, :, n, :] = now
            now, later = later, twice * later - now
    for p in range(PAIR_BLOCK):
        for table, along, across in ((master_tab, 2, 3), (slave_tab, 0, 1)):
            inner = modes[across, p]
            for a in range(MODES):
                outer = modes[along, p, a : a + 1, :]
                table[p, a * MODES : (a + 1) * MODES, :] = (inner * outer).astype(bf16)
    rest = jnp.zeros((5, NODES), f32)
    master = []
    for p in range(PAIR_BLOCK):
        start = slot_ref[step * PAIR_BLOCK + p] * PARTS
        both = arrived_ref[pl.ds(start, PARTS), :]
        u = jnp.concatenate([both[0:3], both[3:6]], axis=1)
        master.append(two_pieces(jnp.concatenate([u, rest], axis=0)))
    projected = [two_pieces(times(master[p], master_tab[p])) for p in range(PAIR_BLOCK)]
    pulled = [times_transposed(projected[p], slave_tab[p]) for p in range(PAIR_BLOCK)]
    half_gaps = []
    for p in range(PAIR_BLOCK):
        r = row_ref[step * PAIR_BLOCK + p]
        lines = [field_ref[c, pl.ds(r, 1), :] for c in range(3)]
        gap = jnp.concatenate(lines + [rest], axis=0) - pulled[p]
        gap_ref[p] = gap[0:3]
        half = PENALTY * gap
        half_gaps.append(half)
    pushed = [two_pieces(times(two_pieces(half_gaps[p]), slave_tab[p])) for p in range(PAIR_BLOCK)]
    back = [times_transposed(pushed[p], master_tab[p]) for p in range(PAIR_BLOCK)]
    for p in range(PAIR_BLOCK):
        start = slot_ref[step * PAIR_BLOCK + p] * PARTS
        outgoing_ref[pl.ds(start, PARTS), :] = jnp.concatenate(
            [back[p][0:3, 0:128], back[p][0:3, 128:256]], axis=0
        )
        r = row_ref[step * PAIR_BLOCK + p]
        for c in range(3):
            right_ref[c, pl.ds(r, 1), :] = right_ref[c, pl.ds(r, 1), :] - half_gaps[p][c : c + 1]


def mortar(slot, slave_row, coords, weights, field, load, arrived):
    points = weights.shape[1]
    whole = lambda i, *_: (0, 0, 0)
    return pl.pallas_call(
        mortar_kernel,
        grid_spec=pltpu.PrefetchScalarGridSpec(
            num_scalar_prefetch=2,
            grid=(PAIRS // PAIR_BLOCK,),
            in_specs=[
                pl.BlockSpec((4, PAIR_BLOCK, points), lambda i, *_: (0, i, 0)),
                pl.BlockSpec((PAIR_BLOCK, points), lambda i, *_: (i, 0)),
                pl.BlockSpec((3, ROWS, NODES), whole),
                pl.BlockSpec((3, ROWS, NODES), whole),
                pl.BlockSpec((SLOT_ROWS, 128), lambda i, *_: (0, 0)),
            ],
            out_specs=[
                pl.BlockSpec((PAIR_BLOCK, 3, NODES), lambda i, *_: (i, 0, 0)),
                pl.BlockSpec((SLOT_ROWS, 128), lambda i, *_: (0, 0)),
                pl.BlockSpec((3, ROWS, NODES), whole),
            ],
            scratch_shapes=[
                pltpu.VMEM((4, PAIR_BLOCK, MODES, points), f32),
                pltpu.VMEM((PAIR_BLOCK, NODES, points), bf16),
                pltpu.VMEM((PAIR_BLOCK, NODES, points), bf16),
            ],
        ),
        out_shape=[
            jax.ShapeDtypeStruct((PAIRS, 3, NODES), f32),
            jax.ShapeDtypeStruct((SLOT_ROWS, 128), f32),
            jax.ShapeDtypeStruct((3, ROWS, NODES), f32),
        ],
        compiler_params=params(),
        name="mortar",
    )(slot, slave_row, coords, weights, field, load, arrived)


def as_column(line):
    tall = jnp.transpose(jnp.broadcast_to(line, (128, ROWS)))
    return jnp.concatenate([tall, tall], axis=1)


def swept(u, right, stiffness, above, below, left, right_side):
    row = lax.broadcasted_iota(jnp.int32, (ROWS, NODES), 0)
    col = lax.broadcasted_iota(jnp.int32, (ROWS, NODES), 1)
    up = jnp.where(row == 0, above, pltpu.roll(u, 1, 0))
    down = jnp.where(row == ROWS - 1, below, pltpu.roll(u, ROWS - 1, 0))
    west = jnp.where(col == 0, as_column(left), pltpu.roll(u, 1, 1))
    east = jnp.where(col == NODES - 1, as_column(right_side), pltpu.roll(u, NODES - 1, 1))
    diagonal = 4.0 + stiffness
    residual = right - (diagonal * u - (down + up + east + west))
    return u + RELAX * residual / diagonal


def put_edges(c, u, edges):
    top, bottom, left, right = edges
    top[c : c + 1, :] = u[0:1]
    bottom[c : c + 1, :] = u[ROWS - 1 : ROWS]
    left[c : c + 1, :] = jnp.transpose(u[:, 0:128])[0:1]
    right[c : c + 1, :] = jnp.transpose(u[:, 128:256])[127:128]


def slave_sweep_kernel(u_ref, right_ref, stiff_ref, ha, hb, hl, hr, out_ref, *edges):
    for c in range(3):
        u = swept(
            u_ref[c], right_ref[c], stiff_ref[...],
            ha[c : c + 1, :], hb[c : c + 1, :], hl[c : c + 1, :], hr[c : c + 1, :],
        )
        out_ref[c] = u
        put_edges(c, u, edges)


EDGES = [jax.ShapeDtypeStruct((3, 256), f32)] * 4
FIELD = jax.ShapeDtypeStruct((3, ROWS, NODES), f32)


def slave_sweep(displacement, right, stiffness, halos):
    return pl.pallas_call(
        slave_sweep_kernel,
        grid=(1,),
        out_shape=[FIELD] + EDGES,
        in_specs=[pl.BlockSpec((3, ROWS, NODES), lambda i: (0, 0, 0))] + [vmem()] * 6,
        out_specs=[vmem()] * 5,
        compiler_params=params(),
        name="slave_sweep",
    )(displacement, right, stiffness, *halos)


def master_sweep_kernel(
    asked_ref, incoming_ref, u_ref, load_ref, stiff_ref, ha, hb, hl, hr, out_ref, right_ref, *edges
):
    asked = jnp.transpose(asked_ref[...].reshape(DEVICES, 128))
    row = lax.broadcasted_iota(jnp.int32, (ROWS, DEVICES), 0)
    hits = jnp.concatenate(
        [jnp.where(row == asked[k : k + 1], 1.0, 0.0) for k in range(CAP)], axis=1
    ).astype(bf16)

    def force(part):
        lines = jnp.concatenate(
            [
                incoming_ref[pl.ds(k * PARTS + part, DEVICES, stride=CAP * PARTS), :]
                for k in range(CAP)
            ],
            axis=0,
        )
        high = lines.astype(bf16)
        low = (lines - high.astype(f32)).astype(bf16)
        dims = (((1,), (0,)), ((), ()))
        return lax.dot_general(hits, high, dims, preferred_element_type=f32) + lax.dot_general(
            hits, low, dims, preferred_element_type=f32
        )

    for c in range(3):
        right = load_ref[c] + jnp.concatenate([force(c), force(3 + c)], axis=1)
        right_ref[c] = right
        d = 3 + c
        u = swept(
            u_ref[c], right, stiff_ref[...],
            ha[d : d + 1, :], hb[d : d + 1, :], hl[d : d + 1, :], hr[d : d + 1, :],
        )
        out_ref[c] = u
        put_edges(c, u, edges)


def master_sweep(asked, incoming, displacement, load, stiffness, halos):
    second = pl.BlockSpec((3, ROWS, NODES), lambda i: (1, 0, 0))
    return pl.pallas_call(
        master_sweep_kernel,
        grid=(1,),
        out_shape=[FIELD, FIELD] + EDGES,
        in_specs=[vmem(), vmem(), second, second] + [vmem()] * 5,
        out_specs=[vmem()] * 6,
        compiler_params=params(),
        name="master_sweep",
    )(asked, incoming, displacement, load, stiffness, *halos)


def last_sweep_kernel(u_ref, right_ref, stiff_ref, ha, hb, hl, hr, *rest):
    out_ref = rest[-1]
    for c in range(3):
        out_ref[c] = swept(
            u_ref[c], right_ref[c], stiff_ref[...],
            ha[c : c + 1, :], hb[c : c + 1, :], hl[c : c + 1, :], hr[c : c + 1, :],
        )


def last_sweep(half, u, right, stiffness, halos, earlier):
    more = [] if earlier is None else [earlier]
    return pl.pallas_call(
        last_sweep_kernel,
        grid=(1,),
        out_shape=jax.ShapeDtypeStruct((6, ROWS, NODES), f32),
        in_specs=[vmem()] * 7 + [pl.BlockSpec(memory_space=pl.ANY)] * len(more),
        out_specs=pl.BlockSpec((3, ROWS, NODES), lambda i: (half, 0, 0)),
        input_output_aliases={7: 0} if more else {},
        compiler_params=params(),
        name="last_sweep",
    )(u, right, stiffness, *halos, *more)


def exchange(top, bottom, left, right):
    slabs, faces = lax.axis_size("slab"), lax.axis_size("face")
    onward = lambda n: [(i, i + 1) for i in range(n - 1)]
    back = lambda n: [(i + 1, i) for i in range(n - 1)]
    return (
        lax.ppermute(bottom, "slab", onward(slabs)),
        lax.ppermute(top, "slab", back(slabs)),
        lax.ppermute(right, "face", onward(faces)),
        lax.ppermute(left, "face", back(faces)),
    )


def all_to_all(x):
    return lax.all_to_all(x, AXES, split_axis=0, concat_axis=0, tiled=True)


def body(
    displacement,
    load,
    stiffness,
    slave_row,
    master_dev,
    master_row,
    seg_count,
    quad_coords,
    quad_weights,
):
    request, slot = slots(master_dev.reshape(1, PAIRS), master_row.reshape(1, PAIRS))
    slot = slot.reshape(PAIRS)
    asked = all_to_all(request)
    first_halos = exchange(
        displacement[:, 0, :],
        displacement[:, ROWS - 1, :],
        displacement[:, :, 0],
        displacement[:, :, NODES - 1],
    )
    active = jnp.arange(quad_weights.shape[1])[None, :] < (seg_count * QPTS)[:, None]
    weights = jnp.where(active, quad_weights, 0.0)
    coords = quad_coords.transpose(1, 0, 2)
    served = serve(asked.reshape(DEVICES * 128), displacement)
    arrived = all_to_all(served).reshape(SLOT_ROWS, 128)
    gap, outgoing, slave_right = mortar(
        slot, slave_row, coords, weights, displacement, load, arrived
    )
    incoming = all_to_all(outgoing.reshape(DEVICES, CAP * PARTS, 128)).reshape(SLOT_ROWS, 128)
    slave_u, *slave_edges = slave_sweep(displacement, slave_right, stiffness, first_halos)
    slave_done = last_sweep(0, slave_u, slave_right, stiffness, exchange(*slave_edges), None)
    master_u, master_right, *master_edges = master_sweep(
        asked, incoming, displacement, load, stiffness, first_halos
    )
    relaxed = last_sweep(
        1, master_u, master_right, stiffness, exchange(*master_edges), slave_done
    )
    return relaxed, gap


def solution(mesh):
    pairs = P(AXES)
    field = P(None, "slab", "face")
    return jax.shard_map(
        body,
        mesh=mesh,
        in_specs=(
            field,
            field,
            P("slab", "face"),
            pairs,
            P(AXES, None),
            pairs,
            pairs,
            P(AXES, None, None),
            P(AXES, None),
        ),
        out_specs=(field, P(AXES, None, None)),
        check_vma=False,
    )
```

time: 378 us -> 154 us (0.41)
  the two profiles are of different devices: /device:TPU:56 before, /device:TPU:32 now
where the time goes in v1:
time: 154 us
  starting transfers between devices  49.7 us (32%)
  Pallas kernels  45 us (29%)
  waiting for transfers between devices  26.4 us (17%)
  blocking collectives  18.9 us (12%)
  local copies, waits for them, and re-layouts  11.5 us (7%)
    pallas_call x1, Pallas kernels, mortar(): pl.pallas_call(mortar_kernel, grid_spec=pltpu.PrefetchScalarGridSpec(num_...  31.5 us
    all_to_all x2, waiting for transfers between devices, all_to_all(): return lax.all_to_all(x, AXES, split_axis=0, concat_axis=0, tiled=True)  22.5 us
    all_to_all x1, blocking collectives, all_to_all(): return lax.all_to_all(x, AXES, split_axis=0, concat_axis=0, tiled=True)  18.9 us
    ppermute x3, starting transfers between devices, exchange(): lax.ppermute(top, 'slab', back(slabs))  17.3 us
    ppermute x3, starting transfers between devices, exchange(): lax.ppermute(right, 'face', onward(faces))  11.6 us
    all_to_all x2, starting transfers between devices, all_to_all(): return lax.all_to_all(x, AXES, split_axis=0, concat_axis=0, tiled=True)  11.2 us
    unnamed x36, local copies, waits for them, and re-layouts  10.2 us
    ppermute x3, starting transfers between devices, exchange(): lax.ppermute(bottom, 'slab', onward(slabs))  5.77 us
  transfers between devices with their start and end apart: 14, of which 3 were waited for; matrix products, arithmetic and copies ran while one was open for 4% of the time, Pallas kernels for 4%

profile of v1, /device:TPU:32, one launch (start us, length us, event | category | flops | bytes accessed | tf_op | source)
XLA Modules:
  0.0 153.6 jit_solution(10630310628312317283)
XLA Ops:
  0.6 1.6 %slots.1 = (s32[128,1,128]{2,1,0:T(1,128)}, s32[1,128]{1,0:T(1,128)}) custom-call(s32[1,128]{1,0:T(1,128)} %bitcast.27, s32[1,128]{1,0:T(1,128)} %bitcast.28), custom_call_target="tpu_custom_call" | custom-call | tf_op jit(solution)/shard_map/slots/pallas_call | solution.py:60
  2.2 18.9 %all_to_all.15.asked_ref = s32[128,1,128]{2,1,0:T(1,128)S(1)} all-to-all(s32[128,1,128]{2,1,0:T(1,128)} %get-tuple-element.18), channel_id=1, replica_groups=mesh['slab'=32,'face'=4] {'slab','face'}, dimensions={0} | all-to-all | bytes 131072 | tf_op jit(solution)/shard_map/all_to_all | solution.py:339
  21.1 1.4 copy-done
  22.5 4.7 %serve.1 = f32[128,24,128]{2,1,0:T(8,128)} custom-call(s32[16384]{0:T(1024)S(1)} %bitcast.21, f32[6,256,256]{2,1,0:T(8,128)S(1)} %copy-done), custom_call_target="tpu_custom_call" | custom-call | tf_op jit(solution)/shard_map/serve/pallas_call | solution.py:86
  27.2 6.3 %all-to-all-start.1 = ((f32[128,24,128]{2,1,0:T(8,128)}), f32[128,24,128]{2,1,0:T(8,128)}, u32[]{:S(2)}, u32[]{:S(2)}) async-start(f32[128,24,128]{2,1,0:T(8,128)} %serve.1), calls=%async_computation.1 | async-start | bytes 3145728 | tf_op jit(solution)/shard_map/all_to_all | solution.py:339
  33.6 0.0 copy-start.1
  33.6 0.0 copy-start.11
  33.6 0.1 copy.25
  33.7 1.1 fusion.weights_ref
  34.8 22.5 %all-to-all-done.1 = f32[128,24,128]{2,1,0:T(8,128)} async-done(((f32[128,24,128]{2,1,0:T(8,128)}), f32[128,24,128]{2,1,0:T(8,128)}, u32[]{:S(2)}, u32[]{:S(2)}) %all-to-all-start.1) | async-done | bytes 1572896 | tf_op jit(solution)/shard_map/all_to_all | solution.py:339
  57.3 31.5 %mortar.1 = (f32[128,3,256]{2,1,0:T(4,128)S(1)}, f32[3072,128]{1,0:T(8,128)S(1)}, f32[3,256,256]{2,1,0:T(8,128)S(1)}) custom-call(s32[128]{0:T(128)S(1)} %bitcast.22, s32[128]{0:T(128)S(1)} %copy-done.11, f32[4,128,384]{2,1,0:T(8,128)S(1)} %bitcast.19, f32[128,384]{1,0:T(8,128)S(1)} %fusion.weights_ref, f32[6,256,256]{2,1,0:T(8,128)S(1)} %copy-done.1, ...), custom_call_target="tpu_custom_call" | custom-call | tf_op jit(solution)/shard_map/mortar/pallas_call | solution.py:170
  88.8 0.9 copy-done.3
  89.7 1.1 copy-done.6
  90.9 0.8 copy-done.9
  91.7 4.9 %all-to-all-start.2 = ((f32[128,24,128]{2,1,0:T(8,128)}), f32[128,24,128]{2,1,0:T(8,128)S(1)}, u32[]{:S(2)}, u32[]{:S(2)}) async-start(f32[128,24,128]{2,1,0:T(8,128)} %bitcast.20), calls=%async_computation.2 | async-start | bytes 3145728 | tf_op jit(solution)/shard_map/all_to_all | solution.py:339
  96.5 1.4 fusion.1
  97.9 1.5 copy.20
  99.4 3.4 %collective-permute-start.2 = (f32[6,256]{1,0:T(8,128)S(1)}, f32[6,256]{1,0:T(8,128)S(1)}, u32[]{:S(2)}, u32[]{:S(2)}) collective-permute-start(f32[6,256]{1,0:T(8,128)S(1)} %bitcast.23), channel_id=1, source_target_pairs={{0,1},{1,2},{2,3},{4,5},{5,6},{6,7},{8,9},{9,10},{10,11},{12,13},{... | collective-permute-start | bytes 18440 | tf_op jit(solution)/shard_map/ppermute | solution.py:333
  102.9 1.5 copy.21
  104.3 1.3 collective-permute-start.3
  105.7 1.9 %collective-permute-start = (f32[6,256]{1,0:T(8,128)S(1)}, f32[6,256]{1,0:T(8,128)S(1)}, u32[]{:S(2)}, u32[]{:S(2)}) collective-permute-start(f32[6,256]{1,0:T(8,128)S(1)} %bitcast.25), channel_id=1, source_target_pairs={{0,4},{4,8},{8,12},{12,16},{16,20},{20,24},{24,28},{28,32},{32,36}... | collective-permute-start | bytes 18440 | tf_op jit(solution)/shard_map/ppermute | solution.py:331
  107.6 5.8 %collective-permute-start.1 = (f32[6,256]{1,0:T(8,128)S(1)}, f32[6,256]{1,0:T(8,128)S(1)}, u32[]{:S(2)}, u32[]{:S(2)}) collective-permute-start(f32[6,256]{1,0:T(8,128)S(1)} %bitcast.26), channel_id=1, source_target_pairs={{4,0},{8,4},{12,8},{16,12},{20,16},{24,20},{28,24},{32,28},{36,32}... | collective-permute-start | bytes 18440 | tf_op jit(solution)/shard_map/ppermute | solution.py:332
  113.3 0.0 collective-permute-done.2.hl
  113.4 0.0 collective-permute-done.3.hr
  113.4 2.2 %collective-permute-done.ha = f32[6,256]{1,0:T(8,128)S(1)} collective-permute-done((f32[6,256]{1,0:T(8,128)S(1)}, f32[6,256]{1,0:T(8,128)S(1)}, u32[]{:S(2)}, u32[]{:S(2)}) %collective-permute-start) | collective-permute-done | bytes 6176 | tf_op jit(solution)/shard_map/ppermute | solution.py:331
  115.6 0.0 collective-permute-done.1.hb
  115.6 1.1 copy-done.4
  116.7 1.0 slave_sweep.1
  117.8 0.9 copy-done.7
  118.7 3.6 %collective-permute-start.10 = (f32[3,256]{1,0:T(4,128)S(1)}, f32[3,256]{1,0:T(4,128)S(1)}, u32[]{:S(2)}, u32[]{:S(2)}) collective-permute-start(f32[3,256]{1,0:T(4,128)S(1)} %get-tuple-element.31), channel_id=1, source_target_pairs={{0,1},{1,2},{2,3},{4,5},{5,6},{6,7},{8,9},{9,10},{10,11},{12,13},{... | collective-permute-start | bytes 9224 | tf_op jit(solution)/shard_map/ppermute | solution.py:333
  122.3 1.3 collective-permute-start.11
  123.6 1.9 %collective-permute-start.8 = (f32[3,256]{1,0:T(4,128)S(1)}, f32[3,256]{1,0:T(4,128)S(1)}, u32[]{:S(2)}, u32[]{:S(2)}) collective-permute-start(f32[3,256]{1,0:T(4,128)S(1)} %get-tuple-element.29), channel_id=1, source_target_pairs={{0,4},{4,8},{8,12},{12,16},{16,20},{20,24},{24,28},{28,32},{32,36}... | collective-permute-start | bytes 9224 | tf_op jit(solution)/shard_map/ppermute | solution.py:331
  125.6 5.8 %collective-permute-start.9 = (f32[3,256]{1,0:T(4,128)S(1)}, f32[3,256]{1,0:T(4,128)S(1)}, u32[]{:S(2)}, u32[]{:S(2)}) collective-permute-start(f32[3,256]{1,0:T(4,128)S(1)} %get-tuple-element.30), channel_id=1, source_target_pairs={{4,0},{8,4},{12,8},{16,12},{20,16},{24,20},{28,24},{32,28},{36,32}... | collective-permute-start | bytes 9224 | tf_op jit(solution)/shard_map/ppermute | solution.py:332
  131.3 0.0 all-to-all-done.2
  131.4 2.8 %master_sweep.1 = (f32[3,256,256]{2,1,0:T(8,128)S(1)}, f32[3,256,256]{2,1,0:T(8,128)S(1)}, f32[3,256]{1,0:T(4,128)S(1)}, f32[3,256]{1,0:T(4,128)S(1)}, f32[3,256]{1,0:T(4,128)S(1)}, /*index=5*/f32[3,256]{1,0:T(4,128)S(1)}) custom-call(s32[128,1,128]{2,1,0:T(1,128)S(1)} %all_to_all.15.asked_ref, f32[3072,128]{1,0:T(8,128)S(1)} %bitcast.18, ...), custom_call_target="tpu_custom_call" | custom-call | tf_op jit(solution)/shard_map/master_sweep/pallas_call | solution.py:292
  134.1 1.9 %collective-permute-start.4 = (f32[3,256]{1,0:T(4,128)S(1)}, f32[3,256]{1,0:T(4,128)S(1)}, u32[]{:S(2)}, u32[]{:S(2)}) collective-permute-start(f32[3,256]{1,0:T(4,128)S(1)} %get-tuple-element.23), channel_id=1, source_target_pairs={{0,4},{4,8},{8,12},{12,16},{16,20},{20,24},{24,28},{28,32},{32,36}... | collective-permute-start | bytes 9224 | tf_op jit(solution)/shard_map/ppermute | solution.py:331
  136.1 0.0 collective-permute-done.10.hl
  136.1 5.8 %collective-permute-start.5 = (f32[3,256]{1,0:T(4,128)S(1)}, f32[3,256]{1,0:T(4,128)S(1)}, u32[]{:S(2)}, u32[]{:S(2)}) collective-permute-start(f32[3,256]{1,0:T(4,128)S(1)} %get-tuple-element.24), channel_id=1, source_target_pairs={{4,0},{8,4},{12,8},{16,12},{20,16},{24,20},{28,24},{32,28},{36,32}... | collective-permute-start | bytes 9224 | tf_op jit(solution)/shard_map/ppermute | solution.py:332
  141.8 0.0 collective-permute-done.11.hr
  141.9 4.6 %collective-permute-start.6 = (f32[3,256]{1,0:T(4,128)S(1)}, f32[3,256]{1,0:T(4,128)S(1)}, u32[]{:S(2)}, u32[]{:S(2)}) collective-permute-start(f32[3,256]{1,0:T(4,128)S(1)} %get-tuple-element.25), channel_id=1, source_target_pairs={{0,1},{1,2},{2,3},{4,5},{5,6},{6,7},{8,9},{9,10},{10,11},{12,13},{... | collective-permute-start | bytes 9224 | tf_op jit(solution)/shard_map/ppermute | solution.py:333
  146.4 0.0 collective-permute-done.8.ha
  146.4 1.3 collective-permute-start.7
  147.7 0.8 copy.17
  148.6 0.0 collective-permute-done.9.hb
  148.6 1.7 %last_sweep.2.rest_0_ = f32[6,256,256]{2,1,0:T(8,128)} custom-call(f32[3,256,256]{2,1,0:T(8,128)S(1)} %copy-done.8, f32[3,256,256]{2,1,0:T(8,128)S(1)} %copy-done.5, f32[256,256]{1,0:T(8,128)S(1)} %copy-done.2, f32[3,256]{1,0:T(4,128)S(1)} %collective-permute-done.8.ha, f32[3,256]{1,0:T(4,128)S(1)} %collective-permute-done.9.hb, ...), custom_call_target="tpu_custom_call" | custom-call | tf_op jit(solution)/shard_map/last_sweep/pallas_call | solution.py:314
  150.3 0.0 collective-permute-done.4.ha
  150.3 1.6 %collective-permute-done.7.hr = f32[3,256]{1,0:T(4,128)S(1)} collective-permute-done((f32[3,256]{1,0:T(4,128)S(1)}, f32[3,256]{1,0:T(4,128)S(1)}, u32[]{:S(2)}, u32[]{:S(2)}) %collective-permute-start.7) | collective-permute-done | bytes 3104 | tf_op jit(solution)/shard_map/ppermute | solution.py:334
  151.9 1.7 %last_sweep.3 = f32[6,256,256]{2,1,0:T(8,128)} custom-call(f32[3,256,256]{2,1,0:T(8,128)S(1)} %get-tuple-element.21.u_ref, f32[3,256,256]{2,1,0:T(8,128)S(1)} %get-tuple-element.22.right_ref, f32[256,256]{1,0:T(8,128)S(1)} %copy-done.2, f32[3,256]{1,0:T(4,128)S(1)} %collective-permute-done.4.ha, ...), custom_call_target="tpu_custom_call", output_to_operand_aliasing={{}: (7, {})} | custom-call | tf_op jit(solution)/shard_map/last_sweep/pallas_call | solution.py:314
  (28 shorter events, 0.1 us)
Async XLA Ops:
  21.1 1.4 copy-start
  27.2 6.3 %copy-start.13 = (f32[128,4,384]{2,1,0:T(4,128)S(1)}, f32[128,4,384]{2,1,0:T(4,128)}, u32[]{:S(2)}) copy-start(f32[128,4,384]{2,1,0:T(4,128)} %param.16) | copy-start | bytes 2359300
  27.2 6.4 %copy-start.14 = (s32[128]{0:T(128)S(1)}, s32[128]{0:T(128)}, u32[]{:S(2)}) copy-start(s32[128]{0:T(128)} %param.15) | copy-start | bytes 1540
  27.2 30.1 %all-to-all-start.1 = ((f32[128,24,128]{2,1,0:T(8,128)}), f32[128,24,128]{2,1,0:T(8,128)}, u32[]{:S(2)}, u32[]{:S(2)}) async-start(f32[128,24,128]{2,1,0:T(8,128)} %serve.1), calls=%async_computation.1 | async-start | bytes 3145728 | tf_op jit(solution)/shard_map/all_to_all | solution.py:339
  33.6 23.7 %copy-start.1 = (f32[6,256,256]{2,1,0:T(8,128)S(1)}, f32[6,256,256]{2,1,0:T(8,128)}, u32[]{:S(2)}) copy-start(f32[6,256,256]{2,1,0:T(8,128)} %u_ref.3) | copy-start | bytes 4718596
  33.6 23.7 %copy-start.11 = (s32[128]{0:T(128)S(1)}, s32[128]{0:T(128)}, u32[]{:S(2)}) copy-start(s32[128]{0:T(128)} %row_ref.1) | copy-start | bytes 1540
  33.6 23.7 %copy-start.12 = (s32[1,128]{1,0:T(1,128)S(1)}, s32[1,128]{1,0:T(1,128)}, u32[]{:S(2)}) copy-start(s32[1,128]{1,0:T(1,128)} %get-tuple-element.19) | copy-start | bytes 1540
  88.8 0.9 copy-start.3
  89.7 1.1 copy-start.6
  90.9 0.8 copy-start.9
  91.7 39.6 %all-to-all-start.2 = ((f32[128,24,128]{2,1,0:T(8,128)}), f32[128,24,128]{2,1,0:T(8,128)S(1)}, u32[]{:S(2)}, u32[]{:S(2)}) async-start(f32[128,24,128]{2,1,0:T(8,128)} %bitcast.20), calls=%async_computation.2 | async-start | bytes 3145728 | tf_op jit(solution)/shard_map/all_to_all | solution.py:339
  97.9 17.7 %copy-start.2 = (f32[256,256]{1,0:T(8,128)S(1)}, f32[256,256]{1,0:T(8,128)}, u32[]{:S(2)}) copy-start(f32[256,256]{1,0:T(8,128)} %stiff_ref.7) | copy-start | bytes 786436
  99.4 13.9 %collective-permute-start.2 = (f32[6,256]{1,0:T(8,128)S(1)}, f32[6,256]{1,0:T(8,128)S(1)}, u32[]{:S(2)}, u32[]{:S(2)}) collective-permute-start(f32[6,256]{1,0:T(8,128)S(1)} %bitcast.23), channel_id=1, source_target_pairs={{0,1},{1,2},{2,3},{4,5},{5,6},{6,7},{8,9},{9,10},{10,11},{12,13},{... | collective-permute-start | bytes 18440 | tf_op jit(solution)/shard_map/ppermute | solution.py:333
  104.3 9.0 %collective-permute-start.3 = (f32[6,256]{1,0:T(8,128)S(1)}, f32[6,256]{1,0:T(8,128)S(1)}, u32[]{:S(2)}, u32[]{:S(2)}) collective-permute-start(f32[6,256]{1,0:T(8,128)S(1)} %bitcast.24), channel_id=1, source_target_pairs={{1,0},{2,1},{3,2},{5,4},{6,5},{7,6},{9,8},{10,9},{11,10},{13,12},{... | collective-permute-start | bytes 18440 | tf_op jit(solution)/shard_map/ppermute | solution.py:334
  105.7 10.0 %collective-permute-start = (f32[6,256]{1,0:T(8,128)S(1)}, f32[6,256]{1,0:T(8,128)S(1)}, u32[]{:S(2)}, u32[]{:S(2)}) collective-permute-start(f32[6,256]{1,0:T(8,128)S(1)} %bitcast.25), channel_id=1, source_target_pairs={{0,4},{4,8},{8,12},{12,16},{16,20},{20,24},{24,28},{28,32},{32,36}... | collective-permute-start | bytes 18440 | tf_op jit(solution)/shard_map/ppermute | solution.py:331
  107.6 8.0 %collective-permute-start.1 = (f32[6,256]{1,0:T(8,128)S(1)}, f32[6,256]{1,0:T(8,128)S(1)}, u32[]{:S(2)}, u32[]{:S(2)}) collective-permute-start(f32[6,256]{1,0:T(8,128)S(1)} %bitcast.26), channel_id=1, source_target_pairs={{4,0},{8,4},{12,8},{16,12},{20,16},{24,20},{28,24},{32,28},{36,32}... | collective-permute-start | bytes 18440 | tf_op jit(solution)/shard_map/ppermute | solution.py:332
  115.6 1.1 copy-start.4
  117.8 0.9 copy-start.7
  118.7 17.4 %collective-permute-start.10 = (f32[3,256]{1,0:T(4,128)S(1)}, f32[3,256]{1,0:T(4,128)S(1)}, u32[]{:S(2)}, u32[]{:S(2)}) collective-permute-start(f32[3,256]{1,0:T(4,128)S(1)} %get-tuple-element.31), channel_id=1, source_target_pairs={{0,1},{1,2},{2,3},{4,5},{5,6},{6,7},{8,9},{9,10},{10,11},{12,13},{... | collective-permute-start | bytes 9224 | tf_op jit(solution)/shard_map/ppermute | solution.py:333
  122.3 19.5 %collective-permute-start.11 = (f32[3,256]{1,0:T(4,128)S(1)}, f32[3,256]{1,0:T(4,128)S(1)}, u32[]{:S(2)}, u32[]{:S(2)}) collective-permute-start(f32[3,256]{1,0:T(4,128)S(1)} %get-tuple-element.32), channel_id=1, source_target_pairs={{1,0},{2,1},{3,2},{5,4},{6,5},{7,6},{9,8},{10,9},{11,10},{13,12},{... | collective-permute-start | bytes 9224 | tf_op jit(solution)/shard_map/ppermute | solution.py:334
  123.6 22.8 %collective-permute-start.8 = (f32[3,256]{1,0:T(4,128)S(1)}, f32[3,256]{1,0:T(4,128)S(1)}, u32[]{:S(2)}, u32[]{:S(2)}) collective-permute-start(f32[3,256]{1,0:T(4,128)S(1)} %get-tuple-element.29), channel_id=1, source_target_pairs={{0,4},{4,8},{8,12},{12,16},{16,20},{20,24},{24,28},{28,32},{32,36}... | collective-permute-start | bytes 9224 | tf_op jit(solution)/shard_map/ppermute | solution.py:331
  125.6 23.0 %collective-permute-start.9 = (f32[3,256]{1,0:T(4,128)S(1)}, f32[3,256]{1,0:T(4,128)S(1)}, u32[]{:S(2)}, u32[]{:S(2)}) collective-permute-start(f32[3,256]{1,0:T(4,128)S(1)} %get-tuple-element.30), channel_id=1, source_target_pairs={{4,0},{8,4},{12,8},{16,12},{20,16},{24,20},{28,24},{32,28},{36,32}... | collective-permute-start | bytes 9224 | tf_op jit(solution)/shard_map/ppermute | solution.py:332
  131.3 16.4 %copy-start.10 = (f32[128,3,256]{2,1,0:T(4,128)S(1)}, f32[128,3,256]{2,1,0:T(4,128)}, u32[]{:S(2)}) copy-start(f32[128,3,256]{2,1,0:T(4,128)} %copy-done.9) | copy-start | bytes 1179652
  131.3 17.2 %copy-start.5 = (f32[3,256,256]{2,1,0:T(8,128)S(1)}, f32[3,256,256]{2,1,0:T(8,128)}, u32[]{:S(2)}) copy-start(f32[3,256,256]{2,1,0:T(8,128)} %copy-done.3) | copy-start | bytes 2359300
  131.3 17.2 %copy-start.8 = (f32[3,256,256]{2,1,0:T(8,128)S(1)}, f32[3,256,256]{2,1,0:T(8,128)}, u32[]{:S(2)}) copy-start(f32[3,256,256]{2,1,0:T(8,128)} %copy-done.7) | copy-start | bytes 2359300
  134.1 16.1 %collective-permute-start.4 = (f32[3,256]{1,0:T(4,128)S(1)}, f32[3,256]{1,0:T(4,128)S(1)}, u32[]{:S(2)}, u32[]{:S(2)}) collective-permute-start(f32[3,256]{1,0:T(4,128)S(1)} %get-tuple-element.23), channel_id=1, source_target_pairs={{0,4},{4,8},{8,12},{12,16},{16,20},{20,24},{24,28},{28,32},{32,36}... | collective-permute-start | bytes 9224 | tf_op jit(solution)/shard_map/ppermute | solution.py:331
  136.1 14.2 %collective-permute-start.5 = (f32[3,256]{1,0:T(4,128)S(1)}, f32[3,256]{1,0:T(4,128)S(1)}, u32[]{:S(2)}, u32[]{:S(2)}) collective-permute-start(f32[3,256]{1,0:T(4,128)S(1)} %get-tuple-element.24), channel_id=1, source_target_pairs={{4,0},{8,4},{12,8},{16,12},{20,16},{24,20},{28,24},{32,28},{36,32}... | collective-permute-start | bytes 9224 | tf_op jit(solution)/shard_map/ppermute | solution.py:332
  141.9 8.4 %collective-permute-start.6 = (f32[3,256]{1,0:T(4,128)S(1)}, f32[3,256]{1,0:T(4,128)S(1)}, u32[]{:S(2)}, u32[]{:S(2)}) collective-permute-start(f32[3,256]{1,0:T(4,128)S(1)} %get-tuple-element.25), channel_id=1, source_target_pairs={{0,1},{1,2},{2,3},{4,5},{5,6},{6,7},{8,9},{9,10},{10,11},{12,13},{... | collective-permute-start | bytes 9224 | tf_op jit(solution)/shard_map/ppermute | solution.py:333
  146.4 5.5 %collective-permute-start.7 = (f32[3,256]{1,0:T(4,128)S(1)}, f32[3,256]{1,0:T(4,128)S(1)}, u32[]{:S(2)}, u32[]{:S(2)}) collective-permute-start(f32[3,256]{1,0:T(4,128)S(1)} %get-tuple-element.26), channel_id=1, source_target_pairs={{1,0},{2,1},{3,2},{5,4},{6,5},{7,6},{9,8},{10,9},{11,10},{13,12},{... | collective-permute-start | bytes 9224 | tf_op jit(solution)/shard_map/ppermute | solution.py:334

commit v2 on v1

v2 whole, which is shorter than its diff:
```python
import functools

import jax
import jax.numpy as jnp
from jax import lax
from jax.experimental import pallas as pl
from jax.experimental.pallas import tpu as pltpu
from jax.sharding import PartitionSpec as P

MODES = 16
QPTS = 16
CAP = 4
PENALTY = 0.5
RELAX = 0.8
DEVICES = 128
PAIRS = 128
NODES = 256
ROWS = 256
PARTS = 6
SLOT_ROWS = DEVICES * CAP * PARTS
PAIR_BLOCK = 8

f32 = jnp.float32
bf16 = jnp.bfloat16
AXES = ("slab", "face")


def vmem():
    return pl.BlockSpec(memory_space=pltpu.VMEM)


def smem():
    return pl.BlockSpec(memory_space=pltpu.SMEM)


def params():
    return pltpu.CompilerParams(vmem_limit_bytes=48 << 20)


def slots_kernel(dev_ref, row_ref, request_ref, slot_ref):
    dev = dev_ref[...]
    row = row_ref[...]
    spread = jnp.broadcast_to(dev, (PAIRS, PAIRS))
    across = jnp.transpose(spread)
    first = lax.broadcasted_iota(jnp.int32, (PAIRS, PAIRS), 0)
    second = lax.broadcasted_iota(jnp.int32, (PAIRS, PAIRS), 1)
    same = jnp.where((spread == across) & (first < second), 1.0, 0.0)
    rank = jnp.sum(same, axis=0, keepdims=True).astype(jnp.int32)
    slot_ref[...] = dev * CAP + rank
    hits = spread == first
    result = jnp.zeros((DEVICES, 128), jnp.int32)
    for k in range(CAP):
        chosen = jnp.where(hits & (rank == k), row.astype(f32), 0.0)
        found = jnp.sum(chosen, axis=1, keepdims=True).astype(jnp.int32)
        result = jnp.where(second == k, found, result)
    request_ref[...] = result.reshape(DEVICES, 1, 128)


def slots(dev, row):
    return pl.pallas_call(
        slots_kernel,
        out_shape=[
            jax.ShapeDtypeStruct((DEVICES, 1, 128), jnp.int32),
            jax.ShapeDtypeStruct((1, PAIRS), jnp.int32),
        ],
        in_specs=[vmem(), vmem()],
        out_specs=[vmem(), vmem()],
        name="slots",
    )(dev, row)


def serve_kernel(asked_ref, field_ref, out_ref):
    def one(s, carry):
        for k in range(CAP):
            r = asked_ref[s * 128 + k]
            for c in range(3):
                line = field_ref[c, pl.ds(r, 1), :]
                out_ref[s, pl.ds(k * PARTS + c, 1), :] = line[:, 0:128]
                out_ref[s, pl.ds(k * PARTS + 3 + c, 1), :] = line[:, 128:256]
        return carry

    lax.fori_loop(0, DEVICES, one, 0, unroll=8)


def serve(asked, field):
    return pl.pallas_call(
        serve_kernel,
        grid=(1,),
        out_shape=pltpu.HBM((DEVICES, CAP * PARTS, 128), f32),
        in_specs=[smem(), pl.BlockSpec((3, ROWS, NODES), lambda i: (1, 0, 0))],
        out_specs=pl.BlockSpec((DEVICES, CAP * PARTS, 128), lambda i: (0, 0, 0)),
        compiler_params=params(),
        name="serve",
    )(asked, field)


def tables_kernel(seg_ref, coords_ref, weights_ref, out_ref, modes, slave_tab, master_tab):
    step = pl.program_id(0)
    points = weights_ref.shape[1]
    row = lax.broadcasted_iota(jnp.int32, (PAIR_BLOCK, points), 0)
    point = lax.broadcasted_iota(jnp.int32, (PAIR_BLOCK, points), 1)
    used = jnp.zeros((PAIR_BLOCK, points), jnp.int32)
    for p in range(PAIR_BLOCK):
        used = jnp.where(row == p, seg_ref[step * PAIR_BLOCK + p] * QPTS, used)
    weights = jnp.where(point < used, weights_ref[...], 0.0)
    for k in range(4):
        x = coords_ref[:, k, :]
        now = weights if k == 0 else jnp.ones_like(x)
        later = now * x
        twice = x + x
        for n in range(MODES):
            modes[k, :, n, :] = now
            now, later = later, twice * later - now

    def build(p):
        for table, along, across in ((master_tab, 2, 3), (slave_tab, 0, 1)):
            inner = modes[across, p]
            for a in range(MODES):
                outer = modes[along, p, a : a + 1, :]
                table[p, a * MODES : (a + 1) * MODES, :] = (inner * outer).astype(bf16)

    def emit(p):
        turned = lax.dot_general(
            master_tab[p], slave_tab[p], (((1,), (1,)), ((), ())), preferred_element_type=f32
        )
        high = turned.astype(bf16)
        out_ref[p, :, 0:NODES] = high
        out_ref[p, :, NODES : 2 * NODES] = (turned - high.astype(f32)).astype(bf16)

    build(0)
    for p in range(PAIR_BLOCK):
        if p + 1 < PAIR_BLOCK:
            build(p + 1)
        emit(p)


def couple_tables(seg_count, coords, weights):
    points = weights.shape[1]
    return pl.pallas_call(
        tables_kernel,
        grid_spec=pltpu.PrefetchScalarGridSpec(
            num_scalar_prefetch=1,
            grid=(PAIRS // PAIR_BLOCK,),
            in_specs=[
                pl.BlockSpec((PAIR_BLOCK, 4, points), lambda i, *_: (i, 0, 0)),
                pl.BlockSpec((PAIR_BLOCK, points), lambda i, *_: (i, 0)),
            ],
            out_specs=pl.BlockSpec((PAIR_BLOCK, NODES, 2 * NODES), lambda i, *_: (i, 0, 0)),
            scratch_shapes=[
                pltpu.VMEM((4, PAIR_BLOCK, MODES, points), f32),
                pltpu.VMEM((PAIR_BLOCK, NODES, points), bf16),
                pltpu.VMEM((PAIR_BLOCK, NODES, points), bf16),
            ],
        ),
        out_shape=jax.ShapeDtypeStruct((PAIRS, NODES, 2 * NODES), bf16),
        compiler_params=pltpu.CompilerParams(vmem_limit_bytes=32 << 20),
        cost_estimate=pl.CostEstimate(
            flops=2 * PAIRS * NODES * NODES * points, bytes_accessed=64 << 20, transcendentals=0
        ),
        name="couple_tables",
    )(seg_count, coords, weights)


def two_pieces(u):
    high = u.astype(bf16)
    low = u - high.astype(f32)
    return jnp.concatenate([high.astype(f32), low], axis=0).astype(bf16)


def times(pieces, table):
    both = lax.dot_general(pieces, table, (((1,), (0,)), ((), ())), preferred_element_type=f32)
    return both[0:8] + both[8:16]


COUPLE_BLOCK = 16
LAG = 2


def couple_kernel(
    slot_ref, row_ref, turned_ref, field_ref, load_ref, arrived_ref, gap_ref, outgoing_ref, right_ref
):
    step = pl.program_id(0)

    @pl.when(step == 0)
    def _():
        outgoing_ref[...] = jnp.zeros_like(outgoing_ref)
        right_ref[...] = load_ref[...]

    rest = jnp.zeros((5, NODES), f32)
    held = {}

    def pull(p):
        pair = step * COUPLE_BLOCK + p
        both = arrived_ref[pl.ds(slot_ref[pair] * PARTS, PARTS), :]
        u = jnp.concatenate([both[0:3], both[3:6]], axis=1)
        u = two_pieces(jnp.concatenate([u, rest], axis=0))
        pulled = times(u, turned_ref[p, :, 0:NODES])
        pulled = pulled + times(u, turned_ref[p, :, NODES : 2 * NODES])
        r = row_ref[pair]
        lines = [field_ref[c, pl.ds(r, 1), :] for c in range(3)]
        gap = jnp.concatenate(lines + [rest], axis=0) - pulled
        half = PENALTY * gap
        for c in range(3):
            gap_ref[c, p : p + 1, :] = gap[c : c + 1]
            right_ref[c, pl.ds(r, 1), :] = right_ref[c, pl.ds(r, 1), :] - half[c : c + 1]
        pieces = two_pieces(half)
        held[p] = jnp.concatenate([pieces, pieces], axis=1)

    def push(p):
        pair = step * COUPLE_BLOCK + p
        both = lax.dot_general(
            turned_ref[p], held[p], (((1,), (1,)), ((), ())), preferred_element_type=f32
        )
        both = jnp.transpose(both)
        back = both[0:8] + both[8:16]
        outgoing_ref[pl.ds(slot_ref[pair] * PARTS, PARTS), :] = jnp.concatenate(
            [back[0:3, 0:128], back[0:3, 128:256]], axis=0
        )

    for p in range(COUPLE_BLOCK + LAG):
        if p < COUPLE_BLOCK:
            pull(p)
        if p >= LAG:
            push(p - LAG)


def couple(slot, slave_row, turned, field, load, arrived):
    whole = lambda i, *_: (0, 0, 0)
    return pl.pallas_call(
        couple_kernel,
        grid_spec=pltpu.PrefetchScalarGridSpec(
            num_scalar_prefetch=2,
            grid=(PAIRS // COUPLE_BLOCK,),
            in_specs=[
                pl.BlockSpec((COUPLE_BLOCK, NODES, 2 * NODES), lambda i, *_: (i, 0, 0)),
                pl.BlockSpec((3, ROWS, NODES), whole),
                pl.BlockSpec((3, ROWS, NODES), whole),
                pl.BlockSpec((SLOT_ROWS, 128), lambda i, *_: (0, 0)),
            ],
            out_specs=[
                pl.BlockSpec((3, COUPLE_BLOCK, NODES), lambda i, *_: (0, i, 0)),
                pl.BlockSpec((SLOT_ROWS, 128), lambda i, *_: (0, 0)),
                pl.BlockSpec((3, ROWS, NODES), whole),
            ],
        ),
        out_shape=[
            pltpu.HBM((3, PAIRS, NODES), f32),
            pltpu.HBM((SLOT_ROWS, 128), f32),
            jax.ShapeDtypeStruct((3, ROWS, NODES), f32),
        ],
        compiler_params=pltpu.CompilerParams(vmem_limit_bytes=40 << 20),
        name="couple",
    )(slot, slave_row, turned, field, load, arrived)


def as_column(line):
    tall = jnp.transpose(jnp.broadcast_to(line, (128, ROWS)))
    return jnp.concatenate([tall, tall], axis=1)


def swept(u, right, stiffness, above, below, left, right_side):
    row = lax.broadcasted_iota(jnp.int32, (ROWS, NODES), 0)
    col = lax.broadcasted_iota(jnp.int32, (ROWS, NODES), 1)
    up = jnp.where(row == 0, above, pltpu.roll(u, 1, 0))
    down = jnp.where(row == ROWS - 1, below, pltpu.roll(u, ROWS - 1, 0))
    west = jnp.where(col == 0, as_column(left), pltpu.roll(u, 1, 1))
    east = jnp.where(col == NODES - 1, as_column(right_side), pltpu.roll(u, NODES - 1, 1))
    diagonal = 4.0 + stiffness
    residual = right - (diagonal * u - (down + up + east + west))
    return u + RELAX * residual / diagonal


def put_edges(c, u, edges):
    top, bottom, left, right = edges
    top[c : c + 1, :] = u[0:1]
    bottom[c : c + 1, :] = u[ROWS - 1 : ROWS]
    left[c : c + 1, :] = jnp.transpose(u[:, 0:128])[0:1]
    right[c : c + 1, :] = jnp.transpose(u[:, 128:256])[127:128]


def slave_sweep_kernel(u_ref, right_ref, stiff_ref, ha, hb, hl, hr, out_ref, *edges):
    for c in range(3):
        u = swept(
            u_ref[c], right_ref[c], stiff_ref[...],
            ha[c : c + 1, :], hb[c : c + 1, :], hl[c : c + 1, :], hr[c : c + 1, :],
        )
        out_ref[c] = u
        put_edges(c, u, edges)


def edges_kernel(u_ref, *edges):
    for c in range(6):
        put_edges(c, u_ref[c], edges)


def first_edges(displacement):
    return pl.pallas_call(
        edges_kernel,
        out_shape=[jax.ShapeDtypeStruct((6, 256), f32)] * 4,
        in_specs=[vmem()],
        out_specs=[vmem()] * 4,
        compiler_params=params(),
        name="first_edges",
    )(displacement)


EDGES = [jax.ShapeDtypeStruct((3, 256), f32)] * 4
FIELD = jax.ShapeDtypeStruct((3, ROWS, NODES), f32)


def slave_sweep(displacement, right, stiffness, halos):
    return pl.pallas_call(
        slave_sweep_kernel,
        grid=(1,),
        out_shape=[FIELD] + EDGES,
        in_specs=[pl.BlockSpec((3, ROWS, NODES), lambda i: (0, 0, 0))] + [vmem()] * 6,
        out_specs=[vmem()] * 5,
        compiler_params=params(),
        name="slave_sweep",
    )(displacement, right, stiffness, *halos)


def master_sweep_kernel(
    asked_ref, incoming_ref, u_ref, load_ref, stiff_ref, ha, hb, hl, hr, ea, eb, el, er,
    out_ref, right_ref, *edges
):
    asked = jnp.transpose(asked_ref[...].reshape(DEVICES, 128))
    row = lax.broadcasted_iota(jnp.int32, (ROWS, DEVICES), 0)
    hits = jnp.concatenate(
        [jnp.where(row == asked[k : k + 1], 1.0, 0.0) for k in range(CAP)], axis=1
    ).astype(bf16)

    def force(part):
        lines = jnp.concatenate(
            [
                incoming_ref[pl.ds(k * PARTS + part, DEVICES, stride=CAP * PARTS), :]
                for k in range(CAP)
            ],
            axis=0,
        )
        high = lines.astype(bf16)
        low = (lines - high.astype(f32)).astype(bf16)
        dims = (((1,), (0,)), ((), ()))
        return lax.dot_general(hits, high, dims, preferred_element_type=f32) + lax.dot_general(
            hits, low, dims, preferred_element_type=f32
        )

    for edge, slave_edge in zip(edges, (ea, eb, el, er)):
        edge[0:3, :] = slave_edge[...]
    for c in range(3):
        right = load_ref[c] + jnp.concatenate([force(c), force(3 + c)], axis=1)
        right_ref[c] = right
        d = 3 + c
        u = swept(
            u_ref[c], right, stiff_ref[...],
            ha[d : d + 1, :], hb[d : d + 1, :], hl[d : d + 1, :], hr[d : d + 1, :],
        )
        out_ref[c] = u
        put_edges(d, u, edges)


def master_sweep(asked, incoming, displacement, load, stiffness, halos, slave_edges):
    second = pl.BlockSpec((3, ROWS, NODES), lambda i: (1, 0, 0))
    return pl.pallas_call(
        master_sweep_kernel,
        grid=(1,),
        out_shape=[FIELD, FIELD] + [jax.ShapeDtypeStruct((6, 256), f32)] * 4,
        in_specs=[vmem(), vmem(), second, second] + [vmem()] * 9,
        out_specs=[vmem()] * 6,
        compiler_params=params(),
        name="master_sweep",
    )(asked, incoming, displacement, load, stiffness, *halos, *slave_edges)


def last_sweep_kernel(us_ref, rs_ref, um_ref, rm_ref, stiff_ref, ha, hb, hl, hr, out_ref):
    for c in range(6):
        u_ref, right_ref = (us_ref, rs_ref) if c < 3 else (um_ref, rm_ref)
        out_ref[c] = swept(
            u_ref[c % 3], right_ref[c % 3], stiff_ref[...],
            ha[c : c + 1, :], hb[c : c + 1, :], hl[c : c + 1, :], hr[c : c + 1, :],
        )


def last_sweep(slave_u, slave_right, master_u, master_right, stiffness, halos):
    return pl.pallas_call(
        last_sweep_kernel,
        out_shape=jax.ShapeDtypeStruct((6, ROWS, NODES), f32),
        in_specs=[vmem()] * 9,
        out_specs=vmem(),
        compiler_params=params(),
        name="last_sweep",
    )(slave_u, slave_right, master_u, master_right, stiffness, *halos)


def exchange(top, bottom, left, right):
    slabs, faces = lax.axis_size("slab"), lax.axis_size("face")
    onward = lambda n: [(i, i + 1) for i in range(n - 1)]
    back = lambda n: [(i + 1, i) for i in range(n - 1)]
    return (
        lax.ppermute(bottom, "slab", onward(slabs)),
        lax.ppermute(top, "slab", back(slabs)),
        lax.ppermute(right, "face", onward(faces)),
        lax.ppermute(left, "face", back(faces)),
    )


def all_to_all(x):
    return lax.all_to_all(x, AXES, split_axis=0, concat_axis=0, tiled=True)


def body(
    displacement,
    load,
    stiffness,
    slave_row,
    master_dev,
    master_row,
    seg_count,
    quad_coords,
    quad_weights,
):
    request, slot = slots(master_dev.reshape(1, PAIRS), master_row.reshape(1, PAIRS))
    slot = slot.reshape(PAIRS)
    asked = all_to_all(request)
    first_halos = exchange(*first_edges(displacement))
    turned = couple_tables(seg_count, quad_coords, quad_weights)
    served = serve(asked.reshape(DEVICES * 128), displacement)
    arrived = all_to_all(served).reshape(SLOT_ROWS, 128)
    gap, outgoing, slave_right = couple(slot, slave_row, turned, displacement, load, arrived)
    incoming = all_to_all(outgoing.reshape(DEVICES, CAP * PARTS, 128)).reshape(SLOT_ROWS, 128)
    slave_u, *slave_edges = slave_sweep(displacement, slave_right, stiffness, first_halos)
    master_u, master_right, *edges = master_sweep(
        asked, incoming, displacement, load, stiffness, first_halos, slave_edges
    )
    relaxed = last_sweep(
        slave_u, slave_right, master_u, master_right, stiffness, exchange(*edges)
    )
    return relaxed, gap.transpose(1, 0, 2)


def solution(mesh):
    pairs = P(AXES)
    field = P(None, "slab", "face")
    return jax.shard_map(
        body,
        mesh=mesh,
        in_specs=(
            field,
            field,
            P("slab", "face"),
            pairs,
            P(AXES, None),
            pairs,
            pairs,
            P(AXES, None, None),
            P(AXES, None),
        ),
        out_specs=(field, P(AXES, None, None)),
        check_vma=False,
    )
```

time: 154 us -> 134 us (0.87)
  waiting for transfers between devices: 26.4 us -> 13.7 us
  starting transfers between devices: 49.7 us -> 38.6 us
  Pallas kernels: 45 us -> 55 us
  local copies, waits for them, and re-layouts: 11.5 us -> 5.82 us
    all_to_all x2, waiting for transfers between devices: 22.5 us -> 3.21 us  [all_to_all(): return lax.all_to_all(x, AXES, split_axis=0, concat_axis=0, tiled=True)]
    pallas_call x4 -> x5, Pallas kernels: 39.6 us -> 49.6 us  [the longest x1 22.5 us: couple_tables(): pl.pallas_call(tables_kernel, grid_spec=pltpu.PrefetchScalarGridSpec(num_...]
    ppermute x3 -> x2, starting transfers between devices: 17.3 us -> 11.3 us  [exchange(): lax.ppermute(top, 'slab', back(slabs))]
    ppermute x3 -> x2, starting transfers between devices: 11.6 us -> 5.97 us  [exchange(): lax.ppermute(right, 'face', onward(faces))]
    unnamed x36 -> x28, local copies, waits for them, and re-layouts: 10.2 us -> 5.82 us
    ppermute x3 -> x2, waiting for transfers between devices: 2.24 us -> 6.24 us  [exchange(): lax.ppermute(bottom, 'slab', onward(slabs))]
    all_to_all x2, starting transfers between devices: 11.2 us -> 14.7 us  [all_to_all(): return lax.all_to_all(x, AXES, split_axis=0, concat_axis=0, tiled=True)]
    ppermute x3 -> x2, waiting for transfers between devices: 1.64 us -> 4.2 us  [exchange(): lax.ppermute(left, 'face', back(faces))]
  transfers between devices with their start and end apart: 14 -> 10, of which waited for: 3 -> 4; matrix products, arithmetic and copies ran while one was open for 4% -> 0% of each run, Pallas kernels for 4% -> 18%
where the time goes in v2:
time: 134 us; the launch traced here: 133 us
  Pallas kernels  55 us (41%)
  starting transfers between devices  38.6 us (29%)
  blocking collectives  18.9 us (14%)
  waiting for transfers between devices  13.7 us (10%)
  local copies, waits for them, and re-layouts  5.82 us (4%)
    pallas_call x1, Pallas kernels, couple_tables(): pl.pallas_call(tables_kernel, grid_spec=pltpu.PrefetchScalarGridSpec(num_...  22.5 us
    pallas_call x1, Pallas kernels, couple(): pl.pallas_call(couple_kernel, grid_spec=pltpu.PrefetchScalarGridSpec(num_...  19.7 us
    all_to_all x1, blocking collectives, all_to_all(): return lax.all_to_all(x, AXES, split_axis=0, concat_axis=0, tiled=True)  18.9 us
    all_to_all x2, starting transfers between devices, all_to_all(): return lax.all_to_all(x, AXES, split_axis=0, concat_axis=0, tiled=True)  14.7 us
    ppermute x2, starting transfers between devices, exchange(): lax.ppermute(top, 'slab', back(slabs))  11.3 us
    ppermute x2, waiting for transfers between devices, exchange(): lax.ppermute(bottom, 'slab', onward(slabs))  6.24 us
    ppermute x2, starting transfers between devices, exchange(): lax.ppermute(right, 'face', onward(faces))  5.97 us
    unnamed x28, local copies, waits for them, and re-layouts  5.82 us
  transfers between devices with their start and end apart: 10, of which 4 were waited for; matrix products, arithmetic and copies ran while one was open for 0% of the time, Pallas kernels for 18%

profile of v2, /device:TPU:32, one launch (start us, length us, event | category | flops | bytes accessed | tf_op | source)
XLA Modules:
  0.0 132.8 jit_solution(10954030605911518110)
XLA Ops:
  0.6 1.6 %slots.1 = (s32[128,1,128]{2,1,0:T(1,128)}, s32[1,128]{1,0:T(1,128)}) custom-call(s32[1,128]{1,0:T(1,128)} %bitcast.14, s32[1,128]{1,0:T(1,128)} %bitcast.15), custom_call_target="tpu_custom_call" | custom-call | tf_op jit(solution)/shard_map/slots/pallas_call | solution.py:60
  2.2 18.9 %all_to_all.15.asked_ref = s32[128,1,128]{2,1,0:T(1,128)S(1)} all-to-all(s32[128,1,128]{2,1,0:T(1,128)} %get-tuple-element.23), channel_id=1, replica_groups=mesh['slab'=32,'face'=4] {'slab','face'}, dimensions={0} | all-to-all | bytes 131072 | tf_op jit(solution)/shard_map/all_to_all | solution.py:408
  21.1 1.4 %copy-done = f32[6,256,256]{2,1,0:T(8,128)S(1)} copy-done((f32[6,256,256]{2,1,0:T(8,128)S(1)}, f32[6,256,256]{2,1,0:T(8,128)}, u32[]{:S(2)}) %copy-start) | copy-done | bytes 1572888
  22.5 4.3 %serve.1 = f32[128,24,128]{2,1,0:T(8,128)} custom-call(s32[16384]{0:T(1024)S(1)} %bitcast.10, f32[6,256,256]{2,1,0:T(8,128)S(1)} %copy-done), custom_call_target="tpu_custom_call" | custom-call | tf_op jit(solution)/shard_map/serve/pallas_call | solution.py:86
  26.8 5.3 %all-to-all-start.1 = ((f32[128,24,128]{2,1,0:T(8,128)}), f32[128,24,128]{2,1,0:T(8,128)S(1)}, u32[]{:S(2)}, u32[]{:S(2)}) async-start(f32[128,24,128]{2,1,0:T(8,128)} %serve.1), calls=%async_computation.1 | async-start | bytes 3145728 | tf_op jit(solution)/shard_map/all_to_all | solution.py:408
  32.1 0.0 copy-done.10
  32.1 0.0 copy-done.11
  32.2 0.0 copy-start.9
  32.2 1.1 copy-done.9
  33.3 22.5 %couple_tables.1.turned_ref = bf16[128,256,512]{2,1,0:T(8,128)(2,1)} custom-call(s32[128]{0:T(128)S(1)} %copy-done.11, f32[128,4,384]{2,1,0:T(4,128)S(1)} %copy-done.9, f32[128,384]{1,0:T(8,128)S(1)} %copy-done.10), custom_call_target="tpu_custom_call" | custom-call | flops 6442450944 | bytes 67108864 | tf_op jit(solution)/shard_map/couple_tables/pallas_call | solution.py:139
  55.8 0.4 all-to-all-done.1
  56.2 0.0 copy-done.1
  56.2 0.0 copy-done.12
  56.2 0.0 copy-done.13
  56.2 0.0 copy-start.2
  56.2 1.4 %copy-done.2 = f32[6,256,256]{2,1,0:T(8,128)S(1)} copy-done((f32[6,256,256]{2,1,0:T(8,128)S(1)}, f32[6,256,256]{2,1,0:T(8,128)}, u32[]{:S(2)}) %copy-start.2) | copy-done | bytes 1572888
  57.6 19.7 %couple.1 = (f32[3,128,256]{2,1,0:T(8,128)}, f32[3072,128]{1,0:T(8,128)}, f32[3,256,256]{2,1,0:T(8,128)S(1)}) custom-call(s32[128]{0:T(128)S(1)} %bitcast.11, s32[128]{0:T(128)S(1)} %copy-done.12, bf16[128,256,512]{2,1,0:T(8,128)(2,1)} %couple_tables.1.turned_ref, f32[6,256,256]{2,1,0:T(8,128)S(1)} %copy-done.1, f32[6,256,256]{2,1,0:T(8,128)S(1)} %copy-done.2, ...), custom_call_target="tpu_custom_call" | custom-call | tf_op jit(solution)/shard_map/couple/pallas_call | solution.py:229
  77.3 0.9 copy-done.3
  78.2 9.4 %all-to-all-start.2 = ((f32[128,24,128]{2,1,0:T(8,128)}), f32[128,24,128]{2,1,0:T(8,128)S(1)}, u32[]{:S(2)}, u32[]{:S(2)}) async-start(f32[128,24,128]{2,1,0:T(8,128)} %bitcast.12), calls=%async_computation.2 | async-start | bytes 3145728 | tf_op jit(solution)/shard_map/all_to_all | solution.py:408
  87.6 0.0 copy-start.4
  87.6 0.0 copy-start.6
  87.6 0.5 first_edges.1
  88.1 2.1 %collective-permute-start = (f32[6,256]{1,0:T(8,128)S(1)}, f32[6,256]{1,0:T(8,128)S(1)}, u32[]{:S(2)}, u32[]{:S(2)}) collective-permute-start(f32[6,256]{1,0:T(8,128)S(1)} %get-tuple-element.25), channel_id=1, source_target_pairs={{0,4},{4,8},{8,12},{12,16},{16,20},{20,24},{24,28},{28,32},{32,36}... | collective-permute-start | bytes 18440 | tf_op jit(solution)/shard_map/ppermute | solution.py:400
  90.1 5.6 %collective-permute-start.1 = (f32[6,256]{1,0:T(8,128)S(1)}, f32[6,256]{1,0:T(8,128)S(1)}, u32[]{:S(2)}, u32[]{:S(2)}) collective-permute-start(f32[6,256]{1,0:T(8,128)S(1)} %get-tuple-element.26), channel_id=1, source_target_pairs={{4,0},{8,4},{12,8},{16,12},{20,16},{24,20},{28,24},{32,28},{36,32}... | collective-permute-start | bytes 18440 | tf_op jit(solution)/shard_map/ppermute | solution.py:401
  95.8 3.4 %collective-permute-start.2 = (f32[6,256]{1,0:T(8,128)S(1)}, f32[6,256]{1,0:T(8,128)S(1)}, u32[]{:S(2)}, u32[]{:S(2)}) collective-permute-start(f32[6,256]{1,0:T(8,128)S(1)} %get-tuple-element.27), channel_id=1, source_target_pairs={{0,1},{1,2},{2,3},{4,5},{5,6},{6,7},{8,9},{9,10},{10,11},{12,13},{... | collective-permute-start | bytes 18440 | tf_op jit(solution)/shard_map/ppermute | solution.py:402
  99.2 1.3 collective-permute-start.3
  100.5 6.2 %collective-permute-done.ha = f32[6,256]{1,0:T(8,128)S(1)} collective-permute-done((f32[6,256]{1,0:T(8,128)S(1)}, f32[6,256]{1,0:T(8,128)S(1)}, u32[]{:S(2)}, u32[]{:S(2)}) %collective-permute-start) | collective-permute-done | bytes 6176 | tf_op jit(solution)/shard_map/ppermute | solution.py:400
  106.7 0.0 collective-permute-done.1.hb
  106.7 0.0 collective-permute-done.2.hl
  106.7 0.0 collective-permute-done.3.hr
  106.7 0.0 copy-done.4
  106.8 0.0 copy-done.6
  106.8 1.0 slave_sweep.1
  107.8 0.0 copy-start.7
  107.8 0.9 copy-done.7
  108.8 2.8 %all-to-all-done.2 = f32[128,24,128]{2,1,0:T(8,128)S(1)} async-done(((f32[128,24,128]{2,1,0:T(8,128)}), f32[128,24,128]{2,1,0:T(8,128)S(1)}, u32[]{:S(2)}, u32[]{:S(2)}) %all-to-all-start.2) | async-done | bytes 1572896 | tf_op jit(solution)/shard_map/all_to_all | solution.py:408
  111.6 2.8 %master_sweep.1 = (f32[3,256,256]{2,1,0:T(8,128)S(1)}, f32[3,256,256]{2,1,0:T(8,128)S(1)}, f32[6,256]{1,0:T(8,128)S(1)}, f32[6,256]{1,0:T(8,128)S(1)}, f32[6,256]{1,0:T(8,128)S(1)}, /*index=5*/f32[6,256]{1,0:T(8,128)S(1)}) custom-call(s32[128,1,128]{2,1,0:T(1,128)S(1)} %all_to_all.15.asked_ref, f32[3072,128]{1,0:T(8,128)S(1)} %bitcast.9, ...), custom_call_target="tpu_custom_call" | custom-call | tf_op jit(solution)/shard_map/master_sweep/pallas_call | solution.py:364
  114.4 2.0 %collective-permute-start.4 = (f32[6,256]{1,0:T(8,128)S(1)}, f32[6,256]{1,0:T(8,128)S(1)}, u32[]{:S(2)}, u32[]{:S(2)}) collective-permute-start(f32[6,256]{1,0:T(8,128)S(1)} %get-tuple-element.37), channel_id=1, source_target_pairs={{0,4},{4,8},{8,12},{12,16},{16,20},{20,24},{24,28},{28,32},{32,36}... | collective-permute-start | bytes 18440 | tf_op jit(solution)/shard_map/ppermute | solution.py:400
  116.4 5.7 %collective-permute-start.5 = (f32[6,256]{1,0:T(8,128)S(1)}, f32[6,256]{1,0:T(8,128)S(1)}, u32[]{:S(2)}, u32[]{:S(2)}) collective-permute-start(f32[6,256]{1,0:T(8,128)S(1)} %get-tuple-element.38), channel_id=1, source_target_pairs={{4,0},{8,4},{12,8},{16,12},{20,16},{24,20},{28,24},{32,28},{36,32}... | collective-permute-start | bytes 18440 | tf_op jit(solution)/shard_map/ppermute | solution.py:401
  122.1 2.5 %collective-permute-start.6 = (f32[6,256]{1,0:T(8,128)S(1)}, f32[6,256]{1,0:T(8,128)S(1)}, u32[]{:S(2)}, u32[]{:S(2)}) collective-permute-start(f32[6,256]{1,0:T(8,128)S(1)} %get-tuple-element.39), channel_id=1, source_target_pairs={{0,1},{1,2},{2,3},{4,5},{5,6},{6,7},{8,9},{9,10},{10,11},{12,13},{... | collective-permute-start | bytes 18440 | tf_op jit(solution)/shard_map/ppermute | solution.py:402
  124.6 1.3 collective-permute-start.7
  125.9 0.0 collective-permute-done.4.ha
  125.9 0.0 collective-permute-done.5.hb
  125.9 0.0 collective-permute-done.6.hl
  126.0 4.2 %collective-permute-done.7.hr = f32[6,256]{1,0:T(8,128)S(1)} collective-permute-done((f32[6,256]{1,0:T(8,128)S(1)}, f32[6,256]{1,0:T(8,128)S(1)}, u32[]{:S(2)}, u32[]{:S(2)}) %collective-permute-start.7) | collective-permute-done | bytes 6176 | tf_op jit(solution)/shard_map/ppermute | solution.py:403
  130.2 0.0 copy-done.5
  130.2 0.0 copy-done.8
  130.2 2.7 %last_sweep.1 = f32[6,256,256]{2,1,0:T(8,128)} custom-call(f32[3,256,256]{2,1,0:T(8,128)S(1)} %copy-done.8, f32[3,256,256]{2,1,0:T(8,128)S(1)} %copy-done.5, f32[3,256,256]{2,1,0:T(8,128)S(1)} %get-tuple-element.35.um_ref, f32[3,256,256]{2,1,0:T(8,128)S(1)} %get-tuple-element.36.rm_ref, f32[256,256]{1,0:T(8,128)S(1)} %copy-done.6, ...), custom_call_target="tpu_custom_call" | custom-call | tf_op jit(solution)/shard_map/last_sweep/pallas_call | solution.py:385
  (9 shorter events, 0.0 us)
Async XLA Ops:
  21.1 1.4 %copy-start = (f32[6,256,256]{2,1,0:T(8,128)S(1)}, f32[6,256,256]{2,1,0:T(8,128)}, u32[]{:S(2)}) copy-start(f32[6,256,256]{2,1,0:T(8,128)} %u_ref.5) | copy-start | bytes 4718596
  26.8 5.3 %copy-start.10 = (f32[128,384]{1,0:T(8,128)S(1)}, f32[128,384]{1,0:T(8,128)}, u32[]{:S(2)}) copy-start(f32[128,384]{1,0:T(8,128)} %weights_ref.1) | copy-start | bytes 589828
  26.8 5.3 %copy-start.11 = (s32[128]{0:T(128)S(1)}, s32[128]{0:T(128)}, u32[]{:S(2)}) copy-start(s32[128]{0:T(128)} %seg_ref.1) | copy-start | bytes 1540
  26.8 29.4 %all-to-all-start.1 = ((f32[128,24,128]{2,1,0:T(8,128)}), f32[128,24,128]{2,1,0:T(8,128)S(1)}, u32[]{:S(2)}, u32[]{:S(2)}) async-start(f32[128,24,128]{2,1,0:T(8,128)} %serve.1), calls=%async_computation.1 | async-start | bytes 3145728 | tf_op jit(solution)/shard_map/all_to_all | solution.py:408
  32.2 1.1 copy-start.9
  33.3 22.9 %copy-start.1 = (f32[6,256,256]{2,1,0:T(8,128)S(1)}, f32[6,256,256]{2,1,0:T(8,128)}, u32[]{:S(2)}) copy-start(f32[6,256,256]{2,1,0:T(8,128)} %u_ref.5) | copy-start | bytes 4718596
  33.3 22.9 %copy-start.12 = (s32[128]{0:T(128)S(1)}, s32[128]{0:T(128)}, u32[]{:S(2)}) copy-start(s32[128]{0:T(128)} %row_ref.1) | copy-start | bytes 1540
  33.3 22.9 %copy-start.13 = (s32[1,128]{1,0:T(1,128)S(1)}, s32[1,128]{1,0:T(1,128)}, u32[]{:S(2)}) copy-start(s32[1,128]{1,0:T(1,128)} %get-tuple-element.22) | copy-start | bytes 1540
  56.2 1.4 %copy-start.2 = (f32[6,256,256]{2,1,0:T(8,128)S(1)}, f32[6,256,256]{2,1,0:T(8,128)}, u32[]{:S(2)}) copy-start(f32[6,256,256]{2,1,0:T(8,128)} %load_ref.3) | copy-start | bytes 4718596
  77.3 0.9 copy-start.3
  78.2 33.4 %all-to-all-start.2 = ((f32[128,24,128]{2,1,0:T(8,128)}), f32[128,24,128]{2,1,0:T(8,128)S(1)}, u32[]{:S(2)}, u32[]{:S(2)}) async-start(f32[128,24,128]{2,1,0:T(8,128)} %bitcast.12), calls=%async_computation.2 | async-start | bytes 3145728 | tf_op jit(solution)/shard_map/all_to_all | solution.py:408
  87.6 19.2 %copy-start.4 = (f32[3,256,256]{2,1,0:T(8,128)S(1)}, f32[3,256,256]{2,1,0:T(8,128)}, u32[]{:S(2)}) copy-start(f32[3,256,256]{2,1,0:T(8,128)} %copy-done.3) | copy-start | bytes 2359300
  87.6 19.2 %copy-start.6 = (f32[256,256]{1,0:T(8,128)S(1)}, f32[256,256]{1,0:T(8,128)}, u32[]{:S(2)}) copy-start(f32[256,256]{1,0:T(8,128)} %stiff_ref.5) | copy-start | bytes 786436
  88.1 18.7 %collective-permute-start = (f32[6,256]{1,0:T(8,128)S(1)}, f32[6,256]{1,0:T(8,128)S(1)}, u32[]{:S(2)}, u32[]{:S(2)}) collective-permute-start(f32[6,256]{1,0:T(8,128)S(1)} %get-tuple-element.25), channel_id=1, source_target_pairs={{0,4},{4,8},{8,12},{12,16},{16,20},{20,24},{24,28},{28,32},{32,36}... | collective-permute-start | bytes 18440 | tf_op jit(solution)/shard_map/ppermute | solution.py:400
  90.1 16.6 %collective-permute-start.1 = (f32[6,256]{1,0:T(8,128)S(1)}, f32[6,256]{1,0:T(8,128)S(1)}, u32[]{:S(2)}, u32[]{:S(2)}) collective-permute-start(f32[6,256]{1,0:T(8,128)S(1)} %get-tuple-element.26), channel_id=1, source_target_pairs={{4,0},{8,4},{12,8},{16,12},{20,16},{24,20},{28,24},{32,28},{36,32}... | collective-permute-start | bytes 18440 | tf_op jit(solution)/shard_map/ppermute | solution.py:401
  95.8 11.0 %collective-permute-start.2 = (f32[6,256]{1,0:T(8,128)S(1)}, f32[6,256]{1,0:T(8,128)S(1)}, u32[]{:S(2)}, u32[]{:S(2)}) collective-permute-start(f32[6,256]{1,0:T(8,128)S(1)} %get-tuple-element.27), channel_id=1, source_target_pairs={{0,1},{1,2},{2,3},{4,5},{5,6},{6,7},{8,9},{9,10},{10,11},{12,13},{... | collective-permute-start | bytes 18440 | tf_op jit(solution)/shard_map/ppermute | solution.py:402
  99.2 7.5 %collective-permute-start.3 = (f32[6,256]{1,0:T(8,128)S(1)}, f32[6,256]{1,0:T(8,128)S(1)}, u32[]{:S(2)}, u32[]{:S(2)}) collective-permute-start(f32[6,256]{1,0:T(8,128)S(1)} %get-tuple-element.28), channel_id=1, source_target_pairs={{1,0},{2,1},{3,2},{5,4},{6,5},{7,6},{9,8},{10,9},{11,10},{13,12},{... | collective-permute-start | bytes 18440 | tf_op jit(solution)/shard_map/ppermute | solution.py:403
  107.8 1.0 copy-start.7
  111.6 18.6 %copy-start.5 = (f32[3,256,256]{2,1,0:T(8,128)S(1)}, f32[3,256,256]{2,1,0:T(8,128)}, u32[]{:S(2)}) copy-start(f32[3,256,256]{2,1,0:T(8,128)} %copy-done.3) | copy-start | bytes 2359300
  111.6 18.6 %copy-start.8 = (f32[3,256,256]{2,1,0:T(8,128)S(1)}, f32[3,256,256]{2,1,0:T(8,128)}, u32[]{:S(2)}) copy-start(f32[3,256,256]{2,1,0:T(8,128)} %copy-done.7) | copy-start | bytes 2359300
  114.4 11.5 %collective-permute-start.4 = (f32[6,256]{1,0:T(8,128)S(1)}, f32[6,256]{1,0:T(8,128)S(1)}, u32[]{:S(2)}, u32[]{:S(2)}) collective-permute-start(f32[6,256]{1,0:T(8,128)S(1)} %get-tuple-element.37), channel_id=1, source_target_pairs={{0,4},{4,8},{8,12},{12,16},{16,20},{20,24},{24,28},{28,32},{32,36}... | collective-permute-start | bytes 18440 | tf_op jit(solution)/shard_map/ppermute | solution.py:400
  116.4 9.5 %collective-permute-start.5 = (f32[6,256]{1,0:T(8,128)S(1)}, f32[6,256]{1,0:T(8,128)S(1)}, u32[]{:S(2)}, u32[]{:S(2)}) collective-permute-start(f32[6,256]{1,0:T(8,128)S(1)} %get-tuple-element.38), channel_id=1, source_target_pairs={{4,0},{8,4},{12,8},{16,12},{20,16},{24,20},{28,24},{32,28},{36,32}... | collective-permute-start | bytes 18440 | tf_op jit(solution)/shard_map/ppermute | solution.py:401
  122.1 3.9 %collective-permute-start.6 = (f32[6,256]{1,0:T(8,128)S(1)}, f32[6,256]{1,0:T(8,128)S(1)}, u32[]{:S(2)}, u32[]{:S(2)}) collective-permute-start(f32[6,256]{1,0:T(8,128)S(1)} %get-tuple-element.39), channel_id=1, source_target_pairs={{0,1},{1,2},{2,3},{4,5},{5,6},{6,7},{8,9},{9,10},{10,11},{12,13},{... | collective-permute-start | bytes 18440 | tf_op jit(solution)/shard_map/ppermute | solution.py:402
  124.6 5.5 %collective-permute-start.7 = (f32[6,256]{1,0:T(8,128)S(1)}, f32[6,256]{1,0:T(8,128)S(1)}, u32[]{:S(2)}, u32[]{:S(2)}) collective-permute-start(f32[6,256]{1,0:T(8,128)S(1)} %get-tuple-element.40), channel_id=1, source_target_pairs={{1,0},{2,1},{3,2},{5,4},{6,5},{7,6},{9,8},{10,9},{11,10},{13,12},{... | collective-permute-start | bytes 18440 | tf_op jit(solution)/shard_map/ppermute | solution.py:403

commit v3 on v2

--- a/solution.py
+++ b/solution.py
@@ -22,6 +22,8 @@
 
 f32 = jnp.float32
 bf16 = jnp.bfloat16
+f8 = jnp.float8_e5m2
+REST_SCALE = 4096.0
 AXES = ("slab", "face")
 
 
@@ -31,6 +33,10 @@
 
 def smem():
     return pl.BlockSpec(memory_space=pltpu.SMEM)
+
+
+def in_hbm(x):
+    return pltpu.with_memory_space_constraint(x, pltpu.HBM)
 
 
 def params():
@@ -87,14 +93,19 @@
         serve_kernel,
         grid=(1,),
         out_shape=pltpu.HBM((DEVICES, CAP * PARTS, 128), f32),
-        in_specs=[smem(), pl.BlockSpec((3, ROWS, NODES), lambda i: (1, 0, 0))],
+        in_specs=[
+            smem(),
+            pl.BlockSpec((3, ROWS, NODES), lambda i: (1, 0, 0)),
+        ],
         out_specs=pl.BlockSpec((DEVICES, CAP * PARTS, 128), lambda i: (0, 0, 0)),
         compiler_params=params(),
         name="serve",
-    )(asked, field)
-
-
-def tables_kernel(seg_ref, coords_ref, weights_ref, out_ref, modes, slave_tab, master_tab):
+    )(asked, in_hbm(field))
+
+
+def tables_kernel(
+    seg_ref, coords_ref, weights_ref, high_ref, rest_ref, modes, slave_tab, master_tab
+):
     step = pl.program_id(0)
     points = weights_ref.shape[1]
     row = lax.broadcasted_iota(jnp.int32, (PAIR_BLOCK, points), 0)
@@ -124,8 +135,8 @@
             master_tab[p], slave_tab[p], (((1,), (1,)), ((), ())), preferred_element_type=f32
         )
         high = turned.astype(bf16)
-        out_ref[p, :, 0:NODES] = high
-        out_ref[p, :, NODES : 2 * NODES] = (turned - high.astype(f32)).astype(bf16)
+        high_ref[p] = high
+        rest_ref[p] = ((turned - high.astype(f32)) * REST_SCALE).astype(f8)
 
     build(0)
     for p in range(PAIR_BLOCK):
@@ -136,6 +147,7 @@
 
 def couple_tables(seg_count, coords, weights):
     points = weights.shape[1]
+    block = pl.BlockSpec((PAIR_BLOCK, NODES, NODES), lambda i, *_: (i, 0, 0))
     return pl.pallas_call(
         tables_kernel,
         grid_spec=pltpu.PrefetchScalarGridSpec(
@@ -145,20 +157,23 @@
                 pl.BlockSpec((PAIR_BLOCK, 4, points), lambda i, *_: (i, 0, 0)),
                 pl.BlockSpec((PAIR_BLOCK, points), lambda i, *_: (i, 0)),
             ],
-            out_specs=pl.BlockSpec((PAIR_BLOCK, NODES, 2 * NODES), lambda i, *_: (i, 0, 0)),
+            out_specs=[block, block],
             scratch_shapes=[
                 pltpu.VMEM((4, PAIR_BLOCK, MODES, points), f32),
                 pltpu.VMEM((PAIR_BLOCK, NODES, points), bf16),
                 pltpu.VMEM((PAIR_BLOCK, NODES, points), bf16),
             ],
         ),
-        out_shape=jax.ShapeDtypeStruct((PAIRS, NODES, 2 * NODES), bf16),
+        out_shape=[
+            pltpu.HBM((PAIRS, NODES, NODES), bf16),
+            pltpu.HBM((PAIRS, NODES, NODES), f8),
+        ],
         compiler_params=pltpu.CompilerParams(vmem_limit_bytes=32 << 20),
         cost_estimate=pl.CostEstimate(
-            flops=2 * PAIRS * NODES * NODES * points, bytes_accessed=64 << 20, transcendentals=0
+            flops=8 * PAIRS * NODES * NODES * points, bytes_accessed=64 << 20, transcendentals=0
         ),
         name="couple_tables",
-    )(seg_count, coords, weights)
+    )(seg_count, in_hbm(coords), in_hbm(weights))
 
 
 def two_pieces(u):
@@ -167,90 +182,134 @@
     return jnp.concatenate([high.astype(f32), low], axis=0).astype(bf16)
 
 
+def two_small_pieces(u):
+    high = u.astype(f8).astype(f32)
+    return jnp.concatenate([high, u - high, jnp.zeros((16, u.shape[1]), f32)], axis=0).astype(f8)
+
+
 def times(pieces, table):
     both = lax.dot_general(pieces, table, (((1,), (0,)), ((), ())), preferred_element_type=f32)
     return both[0:8] + both[8:16]
 
 
+def times_turned(pieces, table):
+    both = lax.dot_general(table, pieces, (((1,), (1,)), ((), ())), preferred_element_type=f32)
+    both = jnp.transpose(both)
+    return both[0:8] + both[8:16]
+
+
 COUPLE_BLOCK = 16
-LAG = 2
+SLOTS = 4
 
 
 def couple_kernel(
-    slot_ref, row_ref, turned_ref, field_ref, load_ref, arrived_ref, gap_ref, outgoing_ref, right_ref
+    slot_ref, row_ref, high_ref, rest_ref, field_ref, arrived_ref,
+    gap_ref, back_ref, highs, rests, held, held_small, sems,
 ):
-    step = pl.program_id(0)
-
-    @pl.when(step == 0)
-    def _():
-        outgoing_ref[...] = jnp.zeros_like(outgoing_ref)
-        right_ref[...] = load_ref[...]
-
-    rest = jnp.zeros((5, NODES), f32)
-    held = {}
-
-    def pull(p):
-        pair = step * COUPLE_BLOCK + p
+    count = PAIRS // COUPLE_BLOCK
+
+    def copies(block):
+        room = lax.rem(block, SLOTS)
+        here = pl.ds(block * COUPLE_BLOCK, COUPLE_BLOCK)
+        return (
+            pltpu.make_async_copy(high_ref.at[here], highs.at[room], sems.at[0, room]),
+            pltpu.make_async_copy(rest_ref.at[here], rests.at[room], sems.at[1, room]),
+        )
+
+    def start(block):
+        for copy in copies(block):
+            copy.start()
+
+    def wait(block):
+        for copy in copies(block):
+            copy.wait()
+
+    empty = jnp.zeros((5, NODES), f32)
+
+    def pull(block, p):
+        room = lax.rem(block, SLOTS)
+        pair = block * COUPLE_BLOCK + p
         both = arrived_ref[pl.ds(slot_ref[pair] * PARTS, PARTS), :]
         u = jnp.concatenate([both[0:3], both[3:6]], axis=1)
-        u = two_pieces(jnp.concatenate([u, rest], axis=0))
-        pulled = times(u, turned_ref[p, :, 0:NODES])
-        pulled = pulled + times(u, turned_ref[p, :, NODES : 2 * NODES])
+        u = jnp.concatenate([u, empty], axis=0)
+        pulled = times(two_pieces(u), highs[room, p])
+        pulled = pulled + times(two_small_pieces(u), rests[room, p]) * (1.0 / REST_SCALE)
         r = row_ref[pair]
         lines = [field_ref[c, pl.ds(r, 1), :] for c in range(3)]
-        gap = jnp.concatenate(lines + [rest], axis=0) - pulled
+        gap = jnp.concatenate(lines + [empty], axis=0) - pulled
+        for c in range(3):
+            gap_ref[c, pl.ds(pair, 1), :] = gap[c : c + 1]
         half = PENALTY * gap
-        for c in range(3):
-            gap_ref[c, p : p + 1, :] = gap[c : c + 1]
-            right_ref[c, pl.ds(r, 1), :] = right_ref[c, pl.ds(r, 1), :] - half[c : c + 1]
-        pieces = two_pieces(half)
-        held[p] = jnp.concatenate([pieces, pieces], axis=1)
-
-    def push(p):
-        pair = step * COUPLE_BLOCK + p
-        both = lax.dot_general(
-            turned_ref[p], held[p], (((1,), (1,)), ((), ())), preferred_element_type=f32
-        )
-        both = jnp.transpose(both)
-        back = both[0:8] + both[8:16]
-        outgoing_ref[pl.ds(slot_ref[pair] * PARTS, PARTS), :] = jnp.concatenate(
+        held[p] = two_pieces(half)
+        held_small[p] = two_small_pieces(half)
+
+    def push(block, p):
+        room = lax.rem(block, SLOTS)
+        back = times_turned(held[p], highs[room, p])
+        back = back + times_turned(held_small[p], rests[room, p]) * (1.0 / REST_SCALE)
+        back_ref[pl.ds(slot_ref[block * COUPLE_BLOCK + p] * PARTS, PARTS), :] = jnp.concatenate(
             [back[0:3, 0:128], back[0:3, 128:256]], axis=0
         )
 
-    for p in range(COUPLE_BLOCK + LAG):
-        if p < COUPLE_BLOCK:
-            pull(p)
-        if p >= LAG:
-            push(p - LAG)
-
-
-def couple(slot, slave_row, turned, field, load, arrived):
-    whole = lambda i, *_: (0, 0, 0)
+    for ahead in range(SLOTS - 1):
+        start(ahead)
+    back_ref[...] = jnp.zeros_like(back_ref)
+    wait(0)
+    for p in range(COUPLE_BLOCK):
+        pull(0, p)
+
+    def one(block, carry):
+        wait(block)
+
+        @pl.when(block + SLOTS - 2 < count)
+        def _():
+            start(block + SLOTS - 2)
+
+        for p in range(COUPLE_BLOCK):
+            push(block - 1, p)
+            pull(block, p)
+        return carry
+
+    lax.fori_loop(1, count, one, 0)
+    for p in range(COUPLE_BLOCK):
+        push(count - 1, p)
+
+
+def couple(slot, slave_row, turned, field, arrived):
+    whole = lambda *_: (0, 0, 0)
+    flat = pl.BlockSpec((SLOT_ROWS, 128), lambda *_: (0, 0))
+    anywhere = pl.BlockSpec(memory_space=pl.ANY)
     return pl.pallas_call(
         couple_kernel,
         grid_spec=pltpu.PrefetchScalarGridSpec(
             num_scalar_prefetch=2,
-            grid=(PAIRS // COUPLE_BLOCK,),
-            in_specs=[
-                pl.BlockSpec((COUPLE_BLOCK, NODES, 2 * NODES), lambda i, *_: (i, 0, 0)),
-                pl.BlockSpec((3, ROWS, NODES), whole),
-                pl.BlockSpec((3, ROWS, NODES), whole),
-                pl.BlockSpec((SLOT_ROWS, 128), lambda i, *_: (0, 0)),
-            ],
-            out_specs=[
-                pl.BlockSpec((3, COUPLE_BLOCK, NODES), lambda i, *_: (0, i, 0)),
-                pl.BlockSpec((SLOT_ROWS, 128), lambda i, *_: (0, 0)),
-                pl.BlockSpec((3, ROWS, NODES), whole),
+            grid=(1,),
+            in_specs=[anywhere, anywhere, pl.BlockSpec((3, ROWS, NODES), whole), flat],
+            out_specs=[pl.BlockSpec((3, PAIRS, NODES), whole), flat],
+            scratch_shapes=[
+                pltpu.VMEM((SLOTS, COUPLE_BLOCK, NODES, NODES), bf16),
+                pltpu.VMEM((SLOTS, COUPLE_BLOCK, NODES, NODES), f8),
+                pltpu.VMEM((COUPLE_BLOCK, 16, NODES), bf16),
+                pltpu.VMEM((COUPLE_BLOCK, 32, NODES), f8),
+                pltpu.SemaphoreType.DMA((2, SLOTS)),
             ],
         ),
         out_shape=[
             pltpu.HBM((3, PAIRS, NODES), f32),
             pltpu.HBM((SLOT_ROWS, 128), f32),
-            jax.ShapeDtypeStruct((3, ROWS, NODES), f32),
         ],
-        compiler_params=pltpu.CompilerParams(vmem_limit_bytes=40 << 20),
+        compiler_params=params(),
         name="couple",
-    )(slot, slave_row, turned, field, load, arrived)
+    )(slot, slave_row, *turned, in_hbm(field), in_hbm(arrived))
+
+
+def gathered(hits, lines):
+    high = lines.astype(bf16)
+    low = (lines - high.astype(f32)).astype(bf16)
+    dims = (((1,), (0,)), ((), ()))
+    return lax.dot_general(hits, high, dims, preferred_element_type=f32) + lax.dot_general(
+        hits, low, dims, preferred_element_type=f32
+    )
 
 
 def as_column(line):
@@ -278,10 +337,16 @@
     right[c : c + 1, :] = jnp.transpose(u[:, 128:256])[127:128]
 
 
-def slave_sweep_kernel(u_ref, right_ref, stiff_ref, ha, hb, hl, hr, out_ref, *edges):
+def slave_sweep_kernel(
+    row_ref, gap_ref, u_ref, load_ref, stiff_ref, ha, hb, hl, hr, out_ref, right_ref, *edges
+):
+    row = lax.broadcasted_iota(jnp.int32, (ROWS, PAIRS), 0)
+    hits = jnp.where(row == row_ref[...], 1.0, 0.0).astype(bf16)
     for c in range(3):
+        right = load_ref[c] - PENALTY * gathered(hits, gap_ref[c])
+        right_ref[c] = right
         u = swept(
-            u_ref[c], right_ref[c], stiff_ref[...],
+            u_ref[c], right, stiff_ref[...],
             ha[c : c + 1, :], hb[c : c + 1, :], hl[c : c + 1, :], hr[c : c + 1, :],
         )
         out_ref[c] = u
@@ -308,16 +373,17 @@
 FIELD = jax.ShapeDtypeStruct((3, ROWS, NODES), f32)
 
 
-def slave_sweep(displacement, right, stiffness, halos):
+def slave_sweep(slave_row, gap, displacement, load, stiffness, halos):
+    half = pl.BlockSpec((3, ROWS, NODES), lambda i: (0, 0, 0))
     return pl.pallas_call(
         slave_sweep_kernel,
         grid=(1,),
-        out_shape=[FIELD] + EDGES,
-        in_specs=[pl.BlockSpec((3, ROWS, NODES), lambda i: (0, 0, 0))] + [vmem()] * 6,
-        out_specs=[vmem()] * 5,
+        out_shape=[FIELD, FIELD] + EDGES,
+        in_specs=[vmem(), vmem(), half, half] + [vmem()] * 5,
+        out_specs=[vmem()] * 6,
         compiler_params=params(),
         name="slave_sweep",
-    )(displacement, right, stiffness, *halos)
+    )(slave_row, gap, in_hbm(displacement), in_hbm(load), stiffness, *halos)
 
 
 def master_sweep_kernel(
@@ -338,12 +404,7 @@
             ],
             axis=0,
         )
-        high = lines.astype(bf16)
-        low = (lines - high.astype(f32)).astype(bf16)
-        dims = (((1,), (0,)), ((), ()))
-        return lax.dot_general(hits, high, dims, preferred_element_type=f32) + lax.dot_general(
-            hits, low, dims, preferred_element_type=f32
-        )
+        return gathered(hits, lines)
 
     for edge, slave_edge in zip(edges, (ea, eb, el, er)):
         edge[0:3, :] = slave_edge[...]
@@ -369,7 +430,7 @@
         out_specs=[vmem()] * 6,
         compiler_params=params(),
         name="master_sweep",
-    )(asked, incoming, displacement, load, stiffness, *halos, *slave_edges)
+    )(asked, incoming, in_hbm(displacement), in_hbm(load), stiffness, *halos, *slave_edges)
 
 
 def last_sweep_kernel(us_ref, rs_ref, um_ref, rm_ref, stiff_ref, ha, hb, hl, hr, out_ref):
@@ -426,9 +487,11 @@
     turned = couple_tables(seg_count, quad_coords, quad_weights)
     served = serve(asked.reshape(DEVICES * 128), displacement)
     arrived = all_to_all(served).reshape(SLOT_ROWS, 128)
-    gap, outgoing, slave_right = couple(slot, slave_row, turned, displacement, load, arrived)
+    gap, outgoing = couple(slot, slave_row, turned, displacement, arrived)
     incoming = all_to_all(outgoing.reshape(DEVICES, CAP * PARTS, 128)).reshape(SLOT_ROWS, 128)
-    slave_u, *slave_edges = slave_sweep(displacement, slave_right, stiffness, first_halos)
+    slave_u, slave_right, *slave_edges = slave_sweep(
+        slave_row.reshape(1, PAIRS), gap, displacement, load, stiffness, first_halos
+    )
     master_u, master_right, *edges = master_sweep(
         asked, incoming, displacement, load, stiffness, first_halos, slave_edges
     )

time: 134 us -> 128 us (0.955)
  local copies, waits for them, and re-layouts: 5.82 us -> 1.18 us
    unnamed x28 -> x14, local copies, waits for them, and re-layouts: 5.82 us -> 1.18 us
    pallas_call x1, Pallas kernels: 19.7 us -> 16.5 us  [couple(): pl.pallas_call(couple_kernel, grid_spec=pltpu.PrefetchScalarGridSpec(num_...]
    pallas_call x1, Pallas kernels: 1.05 us -> 2.48 us  [slave_sweep(): pl.pallas_call(slave_sweep_kernel, grid=(1,), out_shape=[FIELD, FIELD] +...]
  transfers between devices with their start and end apart: 10 -> 10, of which waited for: 4 -> 4; matrix products, arithmetic and copies ran while one was open for 0% -> 0% of each run, Pallas kernels for 18% -> 21%
where the time goes in v3:
time: 128 us; the launch traced here: 127 us
  Pallas kernels  54.7 us (43%)
  starting transfers between devices  38.7 us (30%)
  blocking collectives  18.9 us (15%)
  waiting for transfers between devices  13.2 us (10%)
    pallas_call x1, Pallas kernels, couple_tables(): pl.pallas_call(tables_kernel, grid_spec=pltpu.PrefetchScalarGridSpec(num_...  23.7 us
    all_to_all x1, blocking collectives, all_to_all(): return lax.all_to_all(x, AXES, split_axis=0, concat_axis=0, tiled=True)  18.9 us
    pallas_call x1, Pallas kernels, couple(): pl.pallas_call(couple_kernel, grid_spec=pltpu.PrefetchScalarGridSpec(num_...  16.5 us
    all_to_all x2, starting transfers between devices, all_to_all(): return lax.all_to_all(x, AXES, split_axis=0, concat_axis=0, tiled=True)  14.8 us
    ppermute x2, starting transfers between devices, exchange(): lax.ppermute(top, 'slab', back(slabs))  11.3 us
    ppermute x2, waiting for transfers between devices, exchange(): lax.ppermute(bottom, 'slab', onward(slabs))  6.23 us
    ppermute x2, starting transfers between devices, exchange(): lax.ppermute(right, 'face', onward(faces))  5.97 us
    pallas_call x1, Pallas kernels, serve(): pl.pallas_call(serve_kernel, grid=(1,), out_shape=pltpu.HBM((DEVICES, CAP...  4.45 us
  transfers between devices with their start and end apart: 10, of which 4 were waited for; matrix products, arithmetic and copies ran while one was open for 0% of the time, Pallas kernels for 21%

profile of v3, /device:TPU:32, one launch (start us, length us, event | category | flops | bytes accessed | tf_op | source)
XLA Modules:
  0.0 127.4 jit_solution(12329923147923940805)
XLA Ops:
  0.6 1.6 %slots.1 = (s32[128,1,128]{2,1,0:T(1,128)}, s32[1,128]{1,0:T(1,128)}) custom-call(s32[1,128]{1,0:T(1,128)} %bitcast.16, s32[1,128]{1,0:T(1,128)} %bitcast.17), custom_call_target="tpu_custom_call" | custom-call | tf_op jit(solution)/shard_map/slots/pallas_call | solution.py:66
  2.2 18.9 %all_to_all.15.asked_ref = s32[128,1,128]{2,1,0:T(1,128)S(1)} all-to-all(s32[128,1,128]{2,1,0:T(1,128)} %get-tuple-element.27), channel_id=1, replica_groups=mesh['slab'=32,'face'=4] {'slab','face'}, dimensions={0} | all-to-all | bytes 131072 | tf_op jit(solution)/shard_map/all_to_all | solution.py:469
  21.1 4.5 %serve.1 = f32[128,24,128]{2,1,0:T(8,128)} custom-call(s32[16384]{0:T(1024)S(1)} %bitcast.10, f32[6,256,256]{2,1,0:T(8,128)} %u_ref.5), custom_call_target="tpu_custom_call" | custom-call | tf_op jit(solution)/shard_map/serve/pallas_call | solution.py:92
  25.6 0.0 copy-start.5
  25.6 5.3 %all-to-all-start.1 = ((f32[128,24,128]{2,1,0:T(8,128)}), f32[128,24,128]{2,1,0:T(8,128)S(1)}, u32[]{:S(2)}, u32[]{:S(2)}) async-start(f32[128,24,128]{2,1,0:T(8,128)} %serve.1), calls=%async_computation.1 | async-start | bytes 3145728 | tf_op jit(solution)/shard_map/all_to_all | solution.py:469
  30.9 0.0 copy-done.5
  30.9 0.0 copy-start.3
  30.9 0.0 copy-start.4
  31.0 23.7 %couple_tables.1 = (bf16[128,256,256]{2,1,0:T(8,128)(2,1)}, f8e5m2[128,256,256]{2,1,0:T(32,128)(4,1)}) custom-call(s32[128]{0:T(128)S(1)} %copy-done.5, f32[128,4,384]{2,1,0:T(4,128)} %coords_ref.1, f32[128,384]{1,0:T(8,128)} %weights_ref.1), custom_call_target="tpu_custom_call" | custom-call | flops 25769803776 | bytes 67108864 | tf_op jit(solution)/shard_map/couple_tables/pallas_call | solution.py:151
  54.6 0.3 all-to-all-done.1
  55.0 0.0 copy-start.6
  55.0 1.1 copy-done.6
  56.1 0.0 copy-done.3
  56.1 0.0 copy-done.4
  56.1 16.5 %couple.1 = (f32[3,128,256]{2,1,0:T(8,128)}, f32[3072,128]{1,0:T(8,128)}) custom-call(s32[128]{0:T(128)S(1)} %bitcast.13, s32[128]{0:T(128)S(1)} %copy-done.3, bf16[128,256,256]{2,1,0:T(8,128)(2,1)} %get-tuple-element.25.high_ref, f8e5m2[128,256,256]{2,1,0:T(32,128)(4,1)} %get-tuple-element.26.rest_ref, f32[6,256,256]{2,1,0:T(8,128)} %u_ref.5, ...), custom_call_target="tpu_custom_call" | custom-call | tf_op jit(solution)/shard_map/couple/pallas_call | solution.py:282
  72.6 0.0 copy-start
  72.6 9.4 %all-to-all-start.2 = ((f32[128,24,128]{2,1,0:T(8,128)}), f32[128,24,128]{2,1,0:T(8,128)S(1)}, u32[]{:S(2)}, u32[]{:S(2)}) async-start(f32[128,24,128]{2,1,0:T(8,128)} %bitcast.15), calls=%async_computation.2 | async-start | bytes 3145728 | tf_op jit(solution)/shard_map/all_to_all | solution.py:469
  82.0 0.0 copy-done
  82.1 0.0 copy-start.1
  82.1 0.0 copy-start.2
  82.1 0.5 first_edges.1
  82.5 2.1 %collective-permute-start = (f32[6,256]{1,0:T(8,128)S(1)}, f32[6,256]{1,0:T(8,128)S(1)}, u32[]{:S(2)}, u32[]{:S(2)}) collective-permute-start(f32[6,256]{1,0:T(8,128)S(1)} %get-tuple-element.29), channel_id=1, source_target_pairs={{0,4},{4,8},{8,12},{12,16},{16,20},{20,24},{24,28},{28,32},{32,36}... | collective-permute-start | bytes 18440 | tf_op jit(solution)/shard_map/ppermute | solution.py:461
  84.6 5.6 %collective-permute-start.1 = (f32[6,256]{1,0:T(8,128)S(1)}, f32[6,256]{1,0:T(8,128)S(1)}, u32[]{:S(2)}, u32[]{:S(2)}) collective-permute-start(f32[6,256]{1,0:T(8,128)S(1)} %get-tuple-element.30), channel_id=1, source_target_pairs={{4,0},{8,4},{12,8},{16,12},{20,16},{24,20},{28,24},{32,28},{36,32}... | collective-permute-start | bytes 18440 | tf_op jit(solution)/shard_map/ppermute | solution.py:462
  90.2 3.4 %collective-permute-start.2 = (f32[6,256]{1,0:T(8,128)S(1)}, f32[6,256]{1,0:T(8,128)S(1)}, u32[]{:S(2)}, u32[]{:S(2)}) collective-permute-start(f32[6,256]{1,0:T(8,128)S(1)} %get-tuple-element.31), channel_id=1, source_target_pairs={{0,1},{1,2},{2,3},{4,5},{5,6},{6,7},{8,9},{9,10},{10,11},{12,13},{... | collective-permute-start | bytes 18440 | tf_op jit(solution)/shard_map/ppermute | solution.py:463
  93.7 1.3 %collective-permute-start.3 = (f32[6,256]{1,0:T(8,128)S(1)}, f32[6,256]{1,0:T(8,128)S(1)}, u32[]{:S(2)}, u32[]{:S(2)}) collective-permute-start(f32[6,256]{1,0:T(8,128)S(1)} %get-tuple-element.32), channel_id=1, source_target_pairs={{1,0},{2,1},{3,2},{5,4},{6,5},{7,6},{9,8},{10,9},{11,10},{13,12},{... | collective-permute-start | bytes 18440 | tf_op jit(solution)/shard_map/ppermute | solution.py:464
  95.0 6.2 %collective-permute-done.ha = f32[6,256]{1,0:T(8,128)S(1)} collective-permute-done((f32[6,256]{1,0:T(8,128)S(1)}, f32[6,256]{1,0:T(8,128)S(1)}, u32[]{:S(2)}, u32[]{:S(2)}) %collective-permute-start) | collective-permute-done | bytes 6176 | tf_op jit(solution)/shard_map/ppermute | solution.py:461
  101.2 0.0 collective-permute-done.1.hb
  101.2 0.0 collective-permute-done.2.hl
  101.2 0.0 collective-permute-done.3.hr
  101.2 0.0 copy-done.1
  101.2 0.0 copy-done.2
  101.2 2.5 %slave_sweep.1 = (f32[3,256,256]{2,1,0:T(8,128)S(1)}, f32[3,256,256]{2,1,0:T(8,128)S(1)}, f32[3,256]{1,0:T(4,128)S(1)}, f32[3,256]{1,0:T(4,128)S(1)}, f32[3,256]{1,0:T(4,128)S(1)}, /*index=5*/f32[3,256]{1,0:T(4,128)S(1)}) custom-call(s32[1,128]{1,0:T(1,128)S(1)} %bitcast.12, f32[3,128,256]{2,1,0:T(8,128)S(1)} %copy-done.2, f32[6,256,256]{2,1,0:T(8,128)} %u_ref.5, ...), custom_call_target="tpu_custom_call" | custom-call | tf_op jit(solution)/shard_map/slave_sweep/pallas_call | solution.py:378
  103.7 2.4 %all-to-all-done.2 = f32[128,24,128]{2,1,0:T(8,128)S(1)} async-done(((f32[128,24,128]{2,1,0:T(8,128)}), f32[128,24,128]{2,1,0:T(8,128)S(1)}, u32[]{:S(2)}, u32[]{:S(2)}) %all-to-all-start.2) | async-done | bytes 1572896 | tf_op jit(solution)/shard_map/all_to_all | solution.py:469
  106.1 2.9 %master_sweep.1 = (f32[3,256,256]{2,1,0:T(8,128)S(1)}, f32[3,256,256]{2,1,0:T(8,128)S(1)}, f32[6,256]{1,0:T(8,128)S(1)}, f32[6,256]{1,0:T(8,128)S(1)}, f32[6,256]{1,0:T(8,128)S(1)}, /*index=5*/f32[6,256]{1,0:T(8,128)S(1)}) custom-call(s32[128,1,128]{2,1,0:T(1,128)S(1)} %all_to_all.15.asked_ref, f32[3072,128]{1,0:T(8,128)S(1)} %bitcast.9, ...), custom_call_target="tpu_custom_call" | custom-call | tf_op jit(solution)/shard_map/master_sweep/pallas_call | solution.py:425
  109.0 2.0 %collective-permute-start.4 = (f32[6,256]{1,0:T(8,128)S(1)}, f32[6,256]{1,0:T(8,128)S(1)}, u32[]{:S(2)}, u32[]{:S(2)}) collective-permute-start(f32[6,256]{1,0:T(8,128)S(1)} %get-tuple-element.42), channel_id=1, source_target_pairs={{0,4},{4,8},{8,12},{12,16},{16,20},{20,24},{24,28},{28,32},{32,36}... | collective-permute-start | bytes 18440 | tf_op jit(solution)/shard_map/ppermute | solution.py:461
  111.0 5.7 %collective-permute-start.5 = (f32[6,256]{1,0:T(8,128)S(1)}, f32[6,256]{1,0:T(8,128)S(1)}, u32[]{:S(2)}, u32[]{:S(2)}) collective-permute-start(f32[6,256]{1,0:T(8,128)S(1)} %get-tuple-element.43), channel_id=1, source_target_pairs={{4,0},{8,4},{12,8},{16,12},{20,16},{24,20},{28,24},{32,28},{36,32}... | collective-permute-start | bytes 18440 | tf_op jit(solution)/shard_map/ppermute | solution.py:462
  116.7 2.5 %collective-permute-start.6 = (f32[6,256]{1,0:T(8,128)S(1)}, f32[6,256]{1,0:T(8,128)S(1)}, u32[]{:S(2)}, u32[]{:S(2)}) collective-permute-start(f32[6,256]{1,0:T(8,128)S(1)} %get-tuple-element.44), channel_id=1, source_target_pairs={{0,1},{1,2},{2,3},{4,5},{5,6},{6,7},{8,9},{9,10},{10,11},{12,13},{... | collective-permute-start | bytes 18440 | tf_op jit(solution)/shard_map/ppermute | solution.py:463
  119.2 1.3 %collective-permute-start.7 = (f32[6,256]{1,0:T(8,128)S(1)}, f32[6,256]{1,0:T(8,128)S(1)}, u32[]{:S(2)}, u32[]{:S(2)}) collective-permute-start(f32[6,256]{1,0:T(8,128)S(1)} %get-tuple-element.45), channel_id=1, source_target_pairs={{1,0},{2,1},{3,2},{5,4},{6,5},{7,6},{9,8},{10,9},{11,10},{13,12},{... | collective-permute-start | bytes 18440 | tf_op jit(solution)/shard_map/ppermute | solution.py:464
  120.5 0.0 collective-permute-done.4.ha
  120.5 0.0 collective-permute-done.5.hb
  120.5 0.0 collective-permute-done.6.hl
  120.6 4.2 %collective-permute-done.7.hr = f32[6,256]{1,0:T(8,128)S(1)} collective-permute-done((f32[6,256]{1,0:T(8,128)S(1)}, f32[6,256]{1,0:T(8,128)S(1)}, u32[]{:S(2)}, u32[]{:S(2)}) %collective-permute-start.7) | collective-permute-done | bytes 6176 | tf_op jit(solution)/shard_map/ppermute | solution.py:464
  124.8 2.7 %last_sweep.1 = f32[6,256,256]{2,1,0:T(8,128)} custom-call(f32[3,256,256]{2,1,0:T(8,128)S(1)} %get-tuple-element.33.us_ref, f32[3,256,256]{2,1,0:T(8,128)S(1)} %get-tuple-element.34.rs_ref, f32[3,256,256]{2,1,0:T(8,128)S(1)} %get-tuple-element.40.um_ref, f32[3,256,256]{2,1,0:T(8,128)S(1)} %get-tuple-element.41.rm_ref, f32[256,256]{1,0:T(8,128)S(1)} %copy-done.1, ...), custom_call_target="tpu_custom_call" | custom-call | tf_op jit(solution)/shard_map/last_sweep/pallas_call | solution.py:446
Async XLA Ops:
  25.6 5.3 %copy-start.5 = (s32[128]{0:T(128)S(1)}, s32[128]{0:T(128)}, u32[]{:S(2)}) copy-start(s32[128]{0:T(128)} %seg_ref.1) | copy-start | bytes 1540
  25.6 29.4 %all-to-all-start.1 = ((f32[128,24,128]{2,1,0:T(8,128)}), f32[128,24,128]{2,1,0:T(8,128)S(1)}, u32[]{:S(2)}, u32[]{:S(2)}) async-start(f32[128,24,128]{2,1,0:T(8,128)} %serve.1), calls=%async_computation.1 | async-start | bytes 3145728 | tf_op jit(solution)/shard_map/all_to_all | solution.py:469
  30.9 25.2 %copy-start.3 = (s32[128]{0:T(128)S(1)}, s32[128]{0:T(128)}, u32[]{:S(2)}) copy-start(s32[128]{0:T(128)} %row_ref.1) | copy-start | bytes 1540
  30.9 25.2 %copy-start.4 = (s32[1,128]{1,0:T(1,128)S(1)}, s32[1,128]{1,0:T(1,128)}, u32[]{:S(2)}) copy-start(s32[1,128]{1,0:T(1,128)} %get-tuple-element.24) | copy-start | bytes 1540
  55.0 1.1 copy-start.6
  72.6 9.5 %copy-start = (f32[6,256,256]{2,1,0:T(8,128)S(1)}, f32[6,256,256]{2,1,0:T(8,128)}, u32[]{:S(2)}) copy-start(f32[6,256,256]{2,1,0:T(8,128)} %u_ref.5) | copy-start | bytes 4718596
  72.6 33.5 %all-to-all-start.2 = ((f32[128,24,128]{2,1,0:T(8,128)}), f32[128,24,128]{2,1,0:T(8,128)S(1)}, u32[]{:S(2)}, u32[]{:S(2)}) async-start(f32[128,24,128]{2,1,0:T(8,128)} %bitcast.15), calls=%async_computation.2 | async-start | bytes 3145728 | tf_op jit(solution)/shard_map/all_to_all | solution.py:469
  82.1 19.2 %copy-start.1 = (f32[256,256]{1,0:T(8,128)S(1)}, f32[256,256]{1,0:T(8,128)}, u32[]{:S(2)}) copy-start(f32[256,256]{1,0:T(8,128)} %stiff_ref.5) | copy-start | bytes 786436
  82.1 19.2 %copy-start.2 = (f32[3,128,256]{2,1,0:T(8,128)S(1)}, f32[3,128,256]{2,1,0:T(8,128)}, u32[]{:S(2)}) copy-start(f32[3,128,256]{2,1,0:T(8,128)} %get-tuple-element.28.gap_ref) | copy-start | bytes 1179652
  82.5 18.7 %collective-permute-start = (f32[6,256]{1,0:T(8,128)S(1)}, f32[6,256]{1,0:T(8,128)S(1)}, u32[]{:S(2)}, u32[]{:S(2)}) collective-permute-start(f32[6,256]{1,0:T(8,128)S(1)} %get-tuple-element.29), channel_id=1, source_target_pairs={{0,4},{4,8},{8,12},{12,16},{16,20},{20,24},{24,28},{28,32},{32,36}... | collective-permute-start | bytes 18440 | tf_op jit(solution)/shard_map/ppermute | solution.py:461
  84.6 16.6 %collective-permute-start.1 = (f32[6,256]{1,0:T(8,128)S(1)}, f32[6,256]{1,0:T(8,128)S(1)}, u32[]{:S(2)}, u32[]{:S(2)}) collective-permute-start(f32[6,256]{1,0:T(8,128)S(1)} %get-tuple-element.30), channel_id=1, source_target_pairs={{4,0},{8,4},{12,8},{16,12},{20,16},{24,20},{28,24},{32,28},{36,32}... | collective-permute-start | bytes 18440 | tf_op jit(solution)/shard_map/ppermute | solution.py:462
  90.2 11.0 %collective-permute-start.2 = (f32[6,256]{1,0:T(8,128)S(1)}, f32[6,256]{1,0:T(8,128)S(1)}, u32[]{:S(2)}, u32[]{:S(2)}) collective-permute-start(f32[6,256]{1,0:T(8,128)S(1)} %get-tuple-element.31), channel_id=1, source_target_pairs={{0,1},{1,2},{2,3},{4,5},{5,6},{6,7},{8,9},{9,10},{10,11},{12,13},{... | collective-permute-start | bytes 18440 | tf_op jit(solution)/shard_map/ppermute | solution.py:463
  93.7 7.5 %collective-permute-start.3 = (f32[6,256]{1,0:T(8,128)S(1)}, f32[6,256]{1,0:T(8,128)S(1)}, u32[]{:S(2)}, u32[]{:S(2)}) collective-permute-start(f32[6,256]{1,0:T(8,128)S(1)} %get-tuple-element.32), channel_id=1, source_target_pairs={{1,0},{2,1},{3,2},{5,4},{6,5},{7,6},{9,8},{10,9},{11,10},{13,12},{... | collective-permute-start | bytes 18440 | tf_op jit(solution)/shard_map/ppermute | solution.py:464
  109.0 11.5 %collective-permute-start.4 = (f32[6,256]{1,0:T(8,128)S(1)}, f32[6,256]{1,0:T(8,128)S(1)}, u32[]{:S(2)}, u32[]{:S(2)}) collective-permute-start(f32[6,256]{1,0:T(8,128)S(1)} %get-tuple-element.42), channel_id=1, source_target_pairs={{0,4},{4,8},{8,12},{12,16},{16,20},{20,24},{24,28},{28,32},{32,36}... | collective-permute-start | bytes 18440 | tf_op jit(solution)/shard_map/ppermute | solution.py:461
  111.0 9.5 %collective-permute-start.5 = (f32[6,256]{1,0:T(8,128)S(1)}, f32[6,256]{1,0:T(8,128)S(1)}, u32[]{:S(2)}, u32[]{:S(2)}) collective-permute-start(f32[6,256]{1,0:T(8,128)S(1)} %get-tuple-element.43), channel_id=1, source_target_pairs={{4,0},{8,4},{12,8},{16,12},{20,16},{24,20},{28,24},{32,28},{36,32}... | collective-permute-start | bytes 18440 | tf_op jit(solution)/shard_map/ppermute | solution.py:462
  116.7 3.9 %collective-permute-start.6 = (f32[6,256]{1,0:T(8,128)S(1)}, f32[6,256]{1,0:T(8,128)S(1)}, u32[]{:S(2)}, u32[]{:S(2)}) collective-permute-start(f32[6,256]{1,0:T(8,128)S(1)} %get-tuple-element.44), channel_id=1, source_target_pairs={{0,1},{1,2},{2,3},{4,5},{5,6},{6,7},{8,9},{9,10},{10,11},{12,13},{... | collective-permute-start | bytes 18440 | tf_op jit(solution)/shard_map/ppermute | solution.py:463
  119.2 5.5 %collective-permute-start.7 = (f32[6,256]{1,0:T(8,128)S(1)}, f32[6,256]{1,0:T(8,128)S(1)}, u32[]{:S(2)}, u32[]{:S(2)}) collective-permute-start(f32[6,256]{1,0:T(8,128)S(1)} %get-tuple-element.45), channel_id=1, source_target_pairs={{1,0},{2,1},{3,2},{5,4},{6,5},{7,6},{9,8},{10,9},{11,10},{13,12},{... | collective-permute-start | bytes 18440 | tf_op jit(solution)/shard_map/ppermute | solution.py:464

commit v4 on v3

--- a/solution.py
+++ b/solution.py
@@ -33,6 +33,10 @@
 
 def smem():
     return pl.BlockSpec(memory_space=pltpu.SMEM)
+
+
+def in_vmem(x):
+    return pltpu.with_memory_space_constraint(x, pltpu.VMEM)
 
 
 def in_hbm(x):
@@ -75,29 +79,40 @@
     )(dev, row)
 
 
+SERVE_STEPS = 2
+
+
 def serve_kernel(asked_ref, field_ref, out_ref):
+    begin = pl.program_id(0) * (DEVICES // SERVE_STEPS)
+
     def one(s, carry):
+        lines = []
         for k in range(CAP):
-            r = asked_ref[s * 128 + k]
-            for c in range(3):
-                line = field_ref[c, pl.ds(r, 1), :]
-                out_ref[s, pl.ds(k * PARTS + c, 1), :] = line[:, 0:128]
-                out_ref[s, pl.ds(k * PARTS + 3 + c, 1), :] = line[:, 128:256]
+            r = asked_ref[(begin + s) * 128 + k]
+            lines.append([field_ref[c, pl.ds(r, 1), :] for c in range(3)])
+        out_ref[s] = jnp.concatenate(
+            [
+                line[:, h * 128 : h * 128 + 128]
+                for k in range(CAP)
+                for h in range(2)
+                for line in lines[k]
+            ],
+            axis=0,
+        )
         return carry
 
-    lax.fori_loop(0, DEVICES, one, 0, unroll=8)
+    lax.fori_loop(0, DEVICES // SERVE_STEPS, one, 0, unroll=8)
 
 
 def serve(asked, field):
     return pl.pallas_call(
         serve_kernel,
-        grid=(1,),
+        grid=(SERVE_STEPS,),
         out_shape=pltpu.HBM((DEVICES, CAP * PARTS, 128), f32),
-        in_specs=[
-            smem(),
-            pl.BlockSpec((3, ROWS, NODES), lambda i: (1, 0, 0)),
-        ],
-        out_specs=pl.BlockSpec((DEVICES, CAP * PARTS, 128), lambda i: (0, 0, 0)),
+        in_specs=[smem(), pl.BlockSpec((3, ROWS, NODES), lambda i: (1, 0, 0))],
+        out_specs=pl.BlockSpec(
+            (DEVICES // SERVE_STEPS, CAP * PARTS, 128), lambda i: (i, 0, 0)
+        ),
         compiler_params=params(),
         name="serve",
     )(asked, in_hbm(field))
@@ -284,7 +299,7 @@
         grid_spec=pltpu.PrefetchScalarGridSpec(
             num_scalar_prefetch=2,
             grid=(1,),
-            in_specs=[anywhere, anywhere, pl.BlockSpec((3, ROWS, NODES), whole), flat],
+            in_specs=[anywhere, anywhere, pl.BlockSpec((3, ROWS, NODES), whole), vmem()],
             out_specs=[pl.BlockSpec((3, PAIRS, NODES), whole), flat],
             scratch_shapes=[
                 pltpu.VMEM((SLOTS, COUPLE_BLOCK, NODES, NODES), bf16),
@@ -300,7 +315,7 @@
         ],
         compiler_params=params(),
         name="couple",
-    )(slot, slave_row, *turned, in_hbm(field), in_hbm(arrived))
+    )(slot, slave_row, *turned, in_hbm(field), in_vmem(arrived))
 
 
 def gathered(hits, lines):
@@ -312,21 +327,38 @@
     )
 
 
-def as_column(line):
-    tall = jnp.transpose(jnp.broadcast_to(line, (128, ROWS)))
-    return jnp.concatenate([tall, tall], axis=1)
-
-
-def swept(u, right, stiffness, above, below, left, right_side):
+def turned_sides(inside_ref, left_ref, right_ref):
+    count = left_ref.shape[0]
+    pad = jnp.zeros((8 - count, ROWS), f32)
+    left, right = left_ref[...] * inside_ref[2], right_ref[...] * inside_ref[3]
+    x = jnp.concatenate([left, pad, right, pad], axis=0)
+    high = x.astype(bf16).astype(f32)
+    rest = x - high
+    middle = rest.astype(bf16).astype(f32)
+    pieces = jnp.concatenate([high, middle, rest - middle, jnp.zeros((80, ROWS), f32)], axis=0)
+    return jnp.transpose(pieces).astype(bf16)
+
+
+def beside(u, above, below, sides, c):
     row = lax.broadcasted_iota(jnp.int32, (ROWS, NODES), 0)
     col = lax.broadcasted_iota(jnp.int32, (ROWS, NODES), 1)
     up = jnp.where(row == 0, above, pltpu.roll(u, 1, 0))
     down = jnp.where(row == ROWS - 1, below, pltpu.roll(u, ROWS - 1, 0))
-    west = jnp.where(col == 0, as_column(left), pltpu.roll(u, 1, 1))
-    east = jnp.where(col == NODES - 1, as_column(right_side), pltpu.roll(u, NODES - 1, 1))
-    diagonal = 4.0 + stiffness
-    residual = right - (diagonal * u - (down + up + east + west))
-    return u + RELAX * residual / diagonal
+    west = jnp.where(col == 0, 0.0, pltpu.roll(u, 1, 1))
+    east = jnp.where(col == NODES - 1, 0.0, pltpu.roll(u, NODES - 1, 1))
+    piece = lax.broadcasted_iota(jnp.int32, (128, NODES), 0) & 15
+    place = lax.broadcasted_iota(jnp.int32, (128, NODES), 1)
+    pick = ((piece == c) & (place == 0)) | ((piece == 8 + c) & (place == NODES - 1))
+    pick = jnp.where(pick, 1.0, 0.0).astype(bf16)
+    rim = lax.dot_general(sides, pick, (((1,), (0,)), ((), ())), preferred_element_type=f32)
+    return (down + up) + (east + west) + rim
+
+
+def swept(u, right, gain, inside_ref, above_ref, below_ref, sides, c):
+    above = above_ref[c : c + 1, :] * inside_ref[0]
+    below = below_ref[c : c + 1, :] * inside_ref[1]
+    around = beside(u, above, below, sides, c)
+    return (1.0 - RELAX) * u + gain * (right + around)
 
 
 def put_edges(c, u, edges):
@@ -337,20 +369,40 @@
     right[c : c + 1, :] = jnp.transpose(u[:, 128:256])[127:128]
 
 
-def slave_sweep_kernel(
-    row_ref, gap_ref, u_ref, load_ref, stiff_ref, ha, hb, hl, hr, out_ref, right_ref, *edges
-):
+def slave_right_kernel(row_ref, gap_ref, load_ref, stiff_ref, right_out, gain_out):
     row = lax.broadcasted_iota(jnp.int32, (ROWS, PAIRS), 0)
     hits = jnp.where(row == row_ref[...], 1.0, 0.0).astype(bf16)
+    gain_out[...] = RELAX / (4.0 + stiff_ref[...])
     for c in range(3):
-        right = load_ref[c] - PENALTY * gathered(hits, gap_ref[c])
-        right_ref[c] = right
-        u = swept(
-            u_ref[c], right, stiff_ref[...],
-            ha[c : c + 1, :], hb[c : c + 1, :], hl[c : c + 1, :], hr[c : c + 1, :],
-        )
-        out_ref[c] = u
+        right_out[c] = load_ref[c] - PENALTY * gathered(hits, gap_ref[c])
+
+
+def slave_right_side(slave_row, gap, load, stiffness):
+    half = pl.BlockSpec((3, ROWS, NODES), lambda i: (0, 0, 0))
+    plane = pl.BlockSpec((ROWS, NODES), lambda i: (0, 0))
+    return pl.pallas_call(
+        slave_right_kernel,
+        grid=(1,),
+        out_shape=[pltpu.HBM(FIELD.shape, f32), pltpu.HBM((ROWS, NODES), f32)],
+        in_specs=[vmem(), pl.BlockSpec((3, PAIRS, NODES), lambda i: (0, 0, 0)), half, plane],
+        out_specs=[half, plane],
+        compiler_params=params(),
+        name="slave_right_side",
+    )(slave_row, in_hbm(gap), in_hbm(load), in_hbm(stiffness))
+
+
+def early_sweep_kernel(
+    inside_ref, u_ref, right_ref, load_ref, gain_ref, ha, hb, hl, hr, late_out, base_out, *edges
+):
+    gain = gain_ref[...]
+    sides = turned_sides(inside_ref, hl, hr)
+    for c in range(3):
+        u = swept(u_ref[c], right_ref[c], gain, inside_ref, ha, hb, sides, c)
+        late_out[c] = u
+        late_out[3 + c] = right_ref[c]
+        late_out[6 + c] = load_ref[c]
         put_edges(c, u, edges)
+        base_out[c] = swept(u_ref[3 + c], load_ref[c], gain, inside_ref, ha, hb, sides, 3 + c)
 
 
 def edges_kernel(u_ref, *edges):
@@ -373,22 +425,28 @@
 FIELD = jax.ShapeDtypeStruct((3, ROWS, NODES), f32)
 
 
-def slave_sweep(slave_row, gap, displacement, load, stiffness, halos):
-    half = pl.BlockSpec((3, ROWS, NODES), lambda i: (0, 0, 0))
-    return pl.pallas_call(
-        slave_sweep_kernel,
+def early_sweep(within, displacement, right, load, gain, halos):
+    part = pl.BlockSpec((3, ROWS, NODES), lambda i: (0, 0, 0))
+    return pl.pallas_call(
+        early_sweep_kernel,
         grid=(1,),
-        out_shape=[FIELD, FIELD] + EDGES,
-        in_specs=[vmem(), vmem(), half, half] + [vmem()] * 5,
-        out_specs=[vmem()] * 6,
-        compiler_params=params(),
-        name="slave_sweep",
-    )(slave_row, gap, in_hbm(displacement), in_hbm(load), stiffness, *halos)
+        out_shape=[pltpu.HBM((9, ROWS, NODES), f32), pltpu.HBM(FIELD.shape, f32)] + EDGES,
+        in_specs=[
+            smem(),
+            vmem(),
+            part,
+            pl.BlockSpec((3, ROWS, NODES), lambda i: (1, 0, 0)),
+            pl.BlockSpec((ROWS, NODES), lambda i: (0, 0)),
+        ]
+        + [vmem()] * 4,
+        out_specs=[pl.BlockSpec((9, ROWS, NODES), lambda i: (0, 0, 0)), part] + [vmem()] * 4,
+        compiler_params=params(),
+        name="early_sweep",
+    )(within, displacement, in_hbm(right), in_hbm(load), in_hbm(gain), *halos)
 
 
 def master_sweep_kernel(
-    asked_ref, incoming_ref, u_ref, load_ref, stiff_ref, ha, hb, hl, hr, ea, eb, el, er,
-    out_ref, right_ref, *edges
+    asked_ref, incoming_ref, base_ref, gain_ref, ea, eb, el, er, u_out, added_out, *edges
 ):
     asked = jnp.transpose(asked_ref[...].reshape(DEVICES, 128))
     row = lax.broadcasted_iota(jnp.int32, (ROWS, DEVICES), 0)
@@ -409,60 +467,78 @@
     for edge, slave_edge in zip(edges, (ea, eb, el, er)):
         edge[0:3, :] = slave_edge[...]
     for c in range(3):
-        right = load_ref[c] + jnp.concatenate([force(c), force(3 + c)], axis=1)
-        right_ref[c] = right
-        d = 3 + c
-        u = swept(
-            u_ref[c], right, stiff_ref[...],
-            ha[d : d + 1, :], hb[d : d + 1, :], hl[d : d + 1, :], hr[d : d + 1, :],
-        )
-        out_ref[c] = u
-        put_edges(d, u, edges)
-
-
-def master_sweep(asked, incoming, displacement, load, stiffness, halos, slave_edges):
-    second = pl.BlockSpec((3, ROWS, NODES), lambda i: (1, 0, 0))
+        added = jnp.concatenate([force(c), force(3 + c)], axis=1)
+        added_out[c] = added
+        u = base_ref[c] + gain_ref[...] * added
+        u_out[c] = u
+        put_edges(3 + c, u, edges)
+
+
+def master_sweep(asked, incoming, base, gain, slave_edges):
     return pl.pallas_call(
         master_sweep_kernel,
         grid=(1,),
         out_shape=[FIELD, FIELD] + [jax.ShapeDtypeStruct((6, 256), f32)] * 4,
-        in_specs=[vmem(), vmem(), second, second] + [vmem()] * 9,
+        in_specs=[
+            vmem(),
+            vmem(),
+            pl.BlockSpec((3, ROWS, NODES), lambda i: (0, 0, 0)),
+            pl.BlockSpec((ROWS, NODES), lambda i: (0, 0)),
+        ]
+        + [vmem()] * 4,
         out_specs=[vmem()] * 6,
         compiler_params=params(),
         name="master_sweep",
-    )(asked, incoming, in_hbm(displacement), in_hbm(load), stiffness, *halos, *slave_edges)
-
-
-def last_sweep_kernel(us_ref, rs_ref, um_ref, rm_ref, stiff_ref, ha, hb, hl, hr, out_ref):
+    )(asked, in_vmem(incoming), in_hbm(base), in_hbm(gain), *slave_edges)
+
+
+def last_sweep_kernel(
+    inside_ref, late_ref, um_ref, added_ref, gain_ref, ha, hb, hl, hr, out_ref, done, sems
+):
+    copies = []
+    gain = gain_ref[...]
+    sides = turned_sides(inside_ref, hl, hr)
     for c in range(6):
-        u_ref, right_ref = (us_ref, rs_ref) if c < 3 else (um_ref, rm_ref)
-        out_ref[c] = swept(
-            u_ref[c % 3], right_ref[c % 3], stiff_ref[...],
-            ha[c : c + 1, :], hb[c : c + 1, :], hl[c : c + 1, :], hr[c : c + 1, :],
-        )
-
-
-def last_sweep(slave_u, slave_right, master_u, master_right, stiffness, halos):
+        if c < 3:
+            u, right = late_ref[c], late_ref[3 + c]
+        else:
+            u, right = um_ref[c - 3], late_ref[3 + c] + added_ref[c - 3]
+        done[c] = swept(u, right, gain, inside_ref, ha, hb, sides, c)
+        copies.append(pltpu.make_async_copy(done.at[c], out_ref.at[c], sems.at[c]))
+        copies[-1].start()
+    for copy in copies:
+        copy.wait()
+
+
+def last_sweep(within, late, master_u, added, gain, halos):
     return pl.pallas_call(
         last_sweep_kernel,
         out_shape=jax.ShapeDtypeStruct((6, ROWS, NODES), f32),
-        in_specs=[vmem()] * 9,
-        out_specs=vmem(),
+        in_specs=[smem()] + [vmem()] * 8,
+        out_specs=pl.BlockSpec(memory_space=pl.ANY),
+        scratch_shapes=[pltpu.VMEM((6, ROWS, NODES), f32), pltpu.SemaphoreType.DMA((6,))],
         compiler_params=params(),
         name="last_sweep",
-    )(slave_u, slave_right, master_u, master_right, stiffness, *halos)
+    )(within, late, master_u, added, gain, *halos)
 
 
 def exchange(top, bottom, left, right):
     slabs, faces = lax.axis_size("slab"), lax.axis_size("face")
-    onward = lambda n: [(i, i + 1) for i in range(n - 1)]
-    back = lambda n: [(i + 1, i) for i in range(n - 1)]
+    onward = lambda n: [(i, (i + 1) % n) for i in range(n)]
+    back = lambda n: [((i + 1) % n, i) for i in range(n)]
     return (
         lax.ppermute(bottom, "slab", onward(slabs)),
         lax.ppermute(top, "slab", back(slabs)),
         lax.ppermute(right, "face", onward(faces)),
         lax.ppermute(left, "face", back(faces)),
     )
+
+
+def inside():
+    slab, face = lax.axis_index("slab"), lax.axis_index("face")
+    return jnp.stack(
+        [slab > 0, slab < lax.axis_size("slab") - 1, face > 0, face < lax.axis_size("face") - 1]
+    ).astype(f32)
 
 
 def all_to_all(x):
@@ -489,15 +565,13 @@
     arrived = all_to_all(served).reshape(SLOT_ROWS, 128)
     gap, outgoing = couple(slot, slave_row, turned, displacement, arrived)
     incoming = all_to_all(outgoing.reshape(DEVICES, CAP * PARTS, 128)).reshape(SLOT_ROWS, 128)
-    slave_u, slave_right, *slave_edges = slave_sweep(
-        slave_row.reshape(1, PAIRS), gap, displacement, load, stiffness, first_halos
+    slave_right, gain = slave_right_side(slave_row.reshape(1, PAIRS), gap, load, stiffness)
+    within = inside()
+    late, base, *slave_edges = early_sweep(
+        within, displacement, slave_right, load, gain, first_halos
     )
-    master_u, master_right, *edges = master_sweep(
-        asked, incoming, displacement, load, stiffness, first_halos, slave_edges
-    )
-    relaxed = last_sweep(
-        slave_u, slave_right, master_u, master_right, stiffness, exchange(*edges)
-    )
+    master_u, added, *edges = master_sweep(asked, incoming, base, gain, slave_edges)
+    relaxed = last_sweep(within, late, master_u, added, gain, exchange(*edges))
     return relaxed, gap.transpose(1, 0, 2)
 
 

time: 128 us -> 123 us (0.961)
  the two profiles are of different devices: /device:TPU:32 before, /device:TPU:24 now
where the time goes in v4:
time: 123 us; the launch traced here: 122 us
  Pallas kernels  58.1 us (47%)
  starting transfers between devices  30.4 us (25%)
  blocking collectives  18.3 us (15%)
  waiting for transfers between devices  14.7 us (12%)
    pallas_call x1, Pallas kernels, couple_tables(): pl.pallas_call(tables_kernel, grid_spec=pltpu.PrefetchScalarGridSpec(num_...  23.7 us
    all_to_all x1, blocking collectives, all_to_all(): return lax.all_to_all(x, AXES, split_axis=0, concat_axis=0, tiled=True)  18.3 us
    pallas_call x1, Pallas kernels, couple(): pl.pallas_call(couple_kernel, grid_spec=pltpu.PrefetchScalarGridSpec(num_...  15.9 us
    all_to_all x2, starting transfers between devices, all_to_all(): return lax.all_to_all(x, AXES, split_axis=0, concat_axis=0, tiled=True)  15.7 us
    ppermute x2, waiting for transfers between devices, exchange(): lax.ppermute(bottom, 'slab', onward(slabs))  11.6 us
    ppermute x2, starting transfers between devices, exchange(): lax.ppermute(top, 'slab', back(slabs))  10.4 us
    pallas_call x1, Pallas kernels, early_sweep(): pl.pallas_call(early_sweep_kernel, grid=(1,), out_shape=[pltpu.HBM((9, RO...  4.93 us
    pallas_call x1, Pallas kernels, serve(): pl.pallas_call(serve_kernel, grid=(SERVE_STEPS,), out_shape=pltpu.HBM((DE...  3.76 us
  transfers between devices with their start and end apart: 10, of which 3 were waited for; matrix products, arithmetic and copies ran while one was open for 0% of the time, Pallas kernels for 26%

profile of v4, /device:TPU:24, one launch (start us, length us, event | category | flops | bytes accessed | tf_op | source)
XLA Modules:
  0.0 122.4 jit_solution(14493243942547889780)
XLA Ops:
  0.6 1.6 %slots.1 = (s32[128,1,128]{2,1,0:T(1,128)}, s32[1,128]{1,0:T(1,128)}) custom-call(s32[1,128]{1,0:T(1,128)} %bitcast.20, s32[1,128]{1,0:T(1,128)} %bitcast.21), custom_call_target="tpu_custom_call" | custom-call | tf_op jit(solution)/shard_map/slots/pallas_call | solution.py:70
  2.2 18.3 %all_to_all.15.asked_ref = s32[128,1,128]{2,1,0:T(1,128)S(1)} all-to-all(s32[128,1,128]{2,1,0:T(1,128)} %get-tuple-element.29), channel_id=1, replica_groups=mesh['slab'=32,'face'=4] {'slab','face'}, dimensions={0} | all-to-all | bytes 131072 | tf_op jit(solution)/shard_map/all_to_all | solution.py:545
  20.6 3.8 %serve.1 = f32[128,24,128]{2,1,0:T(8,128)} custom-call(s32[16384]{0:T(1024)S(1)} %bitcast.15, f32[6,256,256]{2,1,0:T(8,128)} %u_ref.3), custom_call_target="tpu_custom_call" | custom-call | tf_op jit(solution)/shard_map/serve/pallas_call | solution.py:108
  24.3 0.0 copy-start.5
  24.3 5.9 %all-to-all-start.1 = ((f32[128,24,128]{2,1,0:T(8,128)}), f32[128,24,128]{2,1,0:T(8,128)S(1)}, u32[]{:S(2)}, u32[]{:S(2)}) async-start(f32[128,24,128]{2,1,0:T(8,128)} %serve.1), calls=%async_computation.1 | async-start | bytes 3145728 | tf_op jit(solution)/shard_map/all_to_all | solution.py:545
  30.3 0.0 copy-done.5
  30.3 0.0 copy-start.3
  30.3 0.0 copy-start.4
  30.3 23.7 %couple_tables.1 = (bf16[128,256,256]{2,1,0:T(8,128)(2,1)}, f8e5m2[128,256,256]{2,1,0:T(32,128)(4,1)}) custom-call(s32[128]{0:T(128)S(1)} %copy-done.5, f32[128,4,384]{2,1,0:T(4,128)} %coords_ref.1, f32[128,384]{1,0:T(8,128)} %weights_ref.1), custom_call_target="tpu_custom_call" | custom-call | flops 25769803776 | bytes 67108864 | tf_op jit(solution)/shard_map/couple_tables/pallas_call | solution.py:166
  54.0 0.0 all-to-all-done.1
  54.0 0.0 copy-done.3
  54.0 0.0 copy-done.4
  54.0 15.9 %couple.1 = (f32[3,128,256]{2,1,0:T(8,128)}, f32[3072,128]{1,0:T(8,128)}) custom-call(s32[128]{0:T(128)S(1)} %bitcast.17, s32[128]{0:T(128)S(1)} %copy-done.3, bf16[128,256,256]{2,1,0:T(8,128)(2,1)} %get-tuple-element.27.high_ref, f8e5m2[128,256,256]{2,1,0:T(32,128)(4,1)} %get-tuple-element.28.rest_ref, f32[6,256,256]{2,1,0:T(8,128)} %u_ref.3, ...), custom_call_target="tpu_custom_call" | custom-call | tf_op jit(solution)/shard_map/couple/pallas_call | solution.py:297
  69.9 0.0 copy-start
  69.9 9.8 %all-to-all-start.2 = ((f32[128,24,128]{2,1,0:T(8,128)}), f32[128,24,128]{2,1,0:T(8,128)S(1)}, u32[]{:S(2)}, u32[]{:S(2)}) async-start(f32[128,24,128]{2,1,0:T(8,128)} %bitcast.18), calls=%async_computation.2 | async-start | bytes 3145728 | tf_op jit(solution)/shard_map/all_to_all | solution.py:545
  79.7 0.0 copy-done
  79.7 0.5 first_edges.1
  80.2 0.2 collective-permute-start
  80.4 5.3 %collective-permute-start.1 = (f32[6,256]{1,0:T(8,128)S(1)}, f32[6,256]{1,0:T(8,128)S(1)}, u32[]{:S(2)}, u32[]{:S(2)}) collective-permute-start(f32[6,256]{1,0:T(8,128)S(1)} %get-tuple-element.34), channel_id=1, source_target_pairs={{4,0},{8,4},{12,8},{16,12},{20,16},{24,20},{28,24},{32,28},{36,32}... | collective-permute-start | bytes 18440 | tf_op jit(solution)/shard_map/ppermute | solution.py:531
  85.7 0.6 collective-permute-start.2
  86.3 1.4 %collective-permute-start.3 = (f32[6,256]{1,0:T(8,128)S(1)}, f32[6,256]{1,0:T(8,128)S(1)}, u32[]{:S(2)}, u32[]{:S(2)}) collective-permute-start(f32[6,256]{1,0:T(8,128)S(1)} %get-tuple-element.36), channel_id=1, source_target_pairs={{1,0},{2,1},{3,2},{0,3},{5,4},{6,5},{7,6},{4,7},{9,8},{10,9},{11,1... | collective-permute-start | bytes 18440 | tf_op jit(solution)/shard_map/ppermute | solution.py:533
  87.7 0.1 add_convert_fusion.inside_ref
  87.8 2.7 %slave_right_side.1 = (f32[3,256,256]{2,1,0:T(8,128)}, f32[256,256]{1,0:T(8,128)}) custom-call(s32[1,128]{1,0:T(1,128)S(1)} %bitcast.16, f32[3,128,256]{2,1,0:T(8,128)} %get-tuple-element.30.gap_ref, f32[6,256,256]{2,1,0:T(8,128)} %load_ref.3, f32[256,256]{1,0:T(8,128)} %stiff_ref.1), custom_call_target="tpu_custom_call" | custom-call | tf_op jit(solution)/shard_map/slave_right_side/pallas_call | solution.py:383
  90.5 11.6 %collective-permute-done.ha = f32[6,256]{1,0:T(8,128)S(1)} collective-permute-done((f32[6,256]{1,0:T(8,128)S(1)}, f32[6,256]{1,0:T(8,128)S(1)}, u32[]{:S(2)}, u32[]{:S(2)}) %collective-permute-start) | collective-permute-done | bytes 6176 | tf_op jit(solution)/shard_map/ppermute | solution.py:530
  102.1 0.0 collective-permute-done.1.hb
  102.1 0.0 collective-permute-done.2.hl
  102.1 0.0 collective-permute-done.3.hr
  102.1 4.9 %early_sweep.1 = (f32[9,256,256]{2,1,0:T(8,128)}, f32[3,256,256]{2,1,0:T(8,128)}, f32[3,256]{1,0:T(4,128)S(1)}, f32[3,256]{1,0:T(4,128)S(1)}, f32[3,256]{1,0:T(4,128)S(1)}, /*index=5*/f32[3,256]{1,0:T(4,128)S(1)}) custom-call(f32[4]{0:T(128)S(1)} %add_convert_fusion.inside_ref, f32[6,256,256]{2,1,0:T(8,128)S(1)} %copy-done, ...), custom_call_target="tpu_custom_call" | custom-call | tf_op jit(solution)/shard_map/early_sweep/pallas_call | solution.py:430
  107.0 0.0 copy-start.2
  107.0 0.0 all-to-all-done.2
  107.0 0.0 copy-start.1
  107.0 2.5 %master_sweep.1 = (f32[3,256,256]{2,1,0:T(8,128)S(1)}, f32[3,256,256]{2,1,0:T(8,128)S(1)}, f32[6,256]{1,0:T(8,128)S(1)}, f32[6,256]{1,0:T(8,128)S(1)}, f32[6,256]{1,0:T(8,128)S(1)}, /*index=5*/f32[6,256]{1,0:T(8,128)S(1)}) custom-call(s32[128,1,128]{2,1,0:T(1,128)S(1)} %all_to_all.15.asked_ref, f32[3072,128]{1,0:T(8,128)S(1)} %bitcast.14, ...), custom_call_target="tpu_custom_call" | custom-call | tf_op jit(solution)/shard_map/master_sweep/pallas_call | solution.py:478
  109.5 0.1 collective-permute-start.4
  109.6 5.1 %collective-permute-start.5 = (f32[6,256]{1,0:T(8,128)S(1)}, f32[6,256]{1,0:T(8,128)S(1)}, u32[]{:S(2)}, u32[]{:S(2)}) collective-permute-start(f32[6,256]{1,0:T(8,128)S(1)} %get-tuple-element.47), channel_id=1, source_target_pairs={{4,0},{8,4},{12,8},{16,12},{20,16},{24,20},{28,24},{32,28},{36,32}... | collective-permute-start | bytes 18440 | tf_op jit(solution)/shard_map/ppermute | solution.py:531
  114.7 0.2 collective-permute-start.6
  114.9 1.8 %collective-permute-start.7 = (f32[6,256]{1,0:T(8,128)S(1)}, f32[6,256]{1,0:T(8,128)S(1)}, u32[]{:S(2)}, u32[]{:S(2)}) collective-permute-start(f32[6,256]{1,0:T(8,128)S(1)} %get-tuple-element.49), channel_id=1, source_target_pairs={{1,0},{2,1},{3,2},{0,3},{5,4},{6,5},{7,6},{4,7},{9,8},{10,9},{11,1... | collective-permute-start | bytes 18440 | tf_op jit(solution)/shard_map/ppermute | solution.py:533
  116.7 0.0 collective-permute-done.4.ha
  116.7 0.0 collective-permute-done.5.hb
  116.7 1.6 %collective-permute-done.6.hl = f32[6,256]{1,0:T(8,128)S(1)} collective-permute-done((f32[6,256]{1,0:T(8,128)S(1)}, f32[6,256]{1,0:T(8,128)S(1)}, u32[]{:S(2)}, u32[]{:S(2)}) %collective-permute-start.6) | collective-permute-done | bytes 6176 | tf_op jit(solution)/shard_map/ppermute | solution.py:532
  118.3 1.4 %collective-permute-done.7.hr = f32[6,256]{1,0:T(8,128)S(1)} collective-permute-done((f32[6,256]{1,0:T(8,128)S(1)}, f32[6,256]{1,0:T(8,128)S(1)}, u32[]{:S(2)}, u32[]{:S(2)}) %collective-permute-start.7) | collective-permute-done | bytes 6176 | tf_op jit(solution)/shard_map/ppermute | solution.py:533
  119.8 0.0 copy-done.2
  119.8 0.0 copy-done.1
  119.8 2.6 %last_sweep.1 = f32[6,256,256]{2,1,0:T(8,128)} custom-call(f32[4]{0:T(128)S(1)} %add_convert_fusion.inside_ref, f32[9,256,256]{2,1,0:T(8,128)S(1)} %copy-done.1, f32[3,256,256]{2,1,0:T(8,128)S(1)} %get-tuple-element.44.um_ref, f32[3,256,256]{2,1,0:T(8,128)S(1)} %get-tuple-element.45.added_ref, f32[256,256]{1,0:T(8,128)S(1)} %copy-done.2, ...), custom_call_target="tpu_custom_call" | custom-call | tf_op jit(solution)/shard_map/last_sweep/pallas_call | solution.py:514
Async XLA Ops:
  24.3 6.0 %copy-start.5 = (s32[128]{0:T(128)S(1)}, s32[128]{0:T(128)}, u32[]{:S(2)}) copy-start(s32[128]{0:T(128)} %seg_ref.1) | copy-start | bytes 1540
  24.3 29.7 %all-to-all-start.1 = ((f32[128,24,128]{2,1,0:T(8,128)}), f32[128,24,128]{2,1,0:T(8,128)S(1)}, u32[]{:S(2)}, u32[]{:S(2)}) async-start(f32[128,24,128]{2,1,0:T(8,128)} %serve.1), calls=%async_computation.1 | async-start | bytes 3145728 | tf_op jit(solution)/shard_map/all_to_all | solution.py:545
  30.3 23.7 %copy-start.3 = (s32[128]{0:T(128)S(1)}, s32[128]{0:T(128)}, u32[]{:S(2)}) copy-start(s32[128]{0:T(128)} %row_ref.1) | copy-start | bytes 1540
  30.3 23.7 %copy-start.4 = (s32[1,128]{1,0:T(1,128)S(1)}, s32[1,128]{1,0:T(1,128)}, u32[]{:S(2)}) copy-start(s32[1,128]{1,0:T(1,128)} %get-tuple-element.26) | copy-start | bytes 1540
  69.9 9.8 %copy-start = (f32[6,256,256]{2,1,0:T(8,128)S(1)}, f32[6,256,256]{2,1,0:T(8,128)}, u32[]{:S(2)}) copy-start(f32[6,256,256]{2,1,0:T(8,128)} %u_ref.3) | copy-start | bytes 4718596
  69.9 37.1 %all-to-all-start.2 = ((f32[128,24,128]{2,1,0:T(8,128)}), f32[128,24,128]{2,1,0:T(8,128)S(1)}, u32[]{:S(2)}, u32[]{:S(2)}) async-start(f32[128,24,128]{2,1,0:T(8,128)} %bitcast.18), calls=%async_computation.2 | async-start | bytes 3145728 | tf_op jit(solution)/shard_map/all_to_all | solution.py:545
  80.2 21.9 %collective-permute-start = (f32[6,256]{1,0:T(8,128)S(1)}, f32[6,256]{1,0:T(8,128)S(1)}, u32[]{:S(2)}, u32[]{:S(2)}) collective-permute-start(f32[6,256]{1,0:T(8,128)S(1)} %get-tuple-element.33), channel_id=1, source_target_pairs={{0,4},{4,8},{8,12},{12,16},{16,20},{20,24},{24,28},{28,32},{32,36}... | collective-permute-start | bytes 18440 | tf_op jit(solution)/shard_map/ppermute | solution.py:530
  80.4 21.7 %collective-permute-start.1 = (f32[6,256]{1,0:T(8,128)S(1)}, f32[6,256]{1,0:T(8,128)S(1)}, u32[]{:S(2)}, u32[]{:S(2)}) collective-permute-start(f32[6,256]{1,0:T(8,128)S(1)} %get-tuple-element.34), channel_id=1, source_target_pairs={{4,0},{8,4},{12,8},{16,12},{20,16},{24,20},{28,24},{32,28},{36,32}... | collective-permute-start | bytes 18440 | tf_op jit(solution)/shard_map/ppermute | solution.py:531
  85.7 16.4 %collective-permute-start.2 = (f32[6,256]{1,0:T(8,128)S(1)}, f32[6,256]{1,0:T(8,128)S(1)}, u32[]{:S(2)}, u32[]{:S(2)}) collective-permute-start(f32[6,256]{1,0:T(8,128)S(1)} %get-tuple-element.35), channel_id=1, source_target_pairs={{0,1},{1,2},{2,3},{3,0},{4,5},{5,6},{6,7},{7,4},{8,9},{9,10},{10,1... | collective-permute-start | bytes 18440 | tf_op jit(solution)/shard_map/ppermute | solution.py:532
  86.3 15.8 %collective-permute-start.3 = (f32[6,256]{1,0:T(8,128)S(1)}, f32[6,256]{1,0:T(8,128)S(1)}, u32[]{:S(2)}, u32[]{:S(2)}) collective-permute-start(f32[6,256]{1,0:T(8,128)S(1)} %get-tuple-element.36), channel_id=1, source_target_pairs={{1,0},{2,1},{3,2},{0,3},{5,4},{6,5},{7,6},{4,7},{9,8},{10,9},{11,1... | collective-permute-start | bytes 18440 | tf_op jit(solution)/shard_map/ppermute | solution.py:533
  107.0 12.7 %copy-start.2 = (f32[256,256]{1,0:T(8,128)S(1)}, f32[256,256]{1,0:T(8,128)}, u32[]{:S(2)}) copy-start(f32[256,256]{1,0:T(8,128)} %get-tuple-element.32.gain_ref) | copy-start | bytes 786436
  107.0 12.7 %copy-start.1 = (f32[9,256,256]{2,1,0:T(8,128)S(1)}, f32[9,256,256]{2,1,0:T(8,128)}, u32[]{:S(2)}) copy-start(f32[9,256,256]{2,1,0:T(8,128)} %get-tuple-element.37.late_ref) | copy-start | bytes 7077892
  109.5 7.2 %collective-permute-start.4 = (f32[6,256]{1,0:T(8,128)S(1)}, f32[6,256]{1,0:T(8,128)S(1)}, u32[]{:S(2)}, u32[]{:S(2)}) collective-permute-start(f32[6,256]{1,0:T(8,128)S(1)} %get-tuple-element.46), channel_id=1, source_target_pairs={{0,4},{4,8},{8,12},{12,16},{16,20},{20,24},{24,28},{28,32},{32,36}... | collective-permute-start | bytes 18440 | tf_op jit(solution)/shard_map/ppermute | solution.py:530
  109.6 7.1 %collective-permute-start.5 = (f32[6,256]{1,0:T(8,128)S(1)}, f32[6,256]{1,0:T(8,128)S(1)}, u32[]{:S(2)}, u32[]{:S(2)}) collective-permute-start(f32[6,256]{1,0:T(8,128)S(1)} %get-tuple-element.47), channel_id=1, source_target_pairs={{4,0},{8,4},{12,8},{16,12},{20,16},{24,20},{28,24},{32,28},{36,32}... | collective-permute-start | bytes 18440 | tf_op jit(solution)/shard_map/ppermute | solution.py:531
  114.7 3.7 %collective-permute-start.6 = (f32[6,256]{1,0:T(8,128)S(1)}, f32[6,256]{1,0:T(8,128)S(1)}, u32[]{:S(2)}, u32[]{:S(2)}) collective-permute-start(f32[6,256]{1,0:T(8,128)S(1)} %get-tuple-element.48), channel_id=1, source_target_pairs={{0,1},{1,2},{2,3},{3,0},{4,5},{5,6},{6,7},{7,4},{8,9},{9,10},{10,1... | collective-permute-start | bytes 18440 | tf_op jit(solution)/shard_map/ppermute | solution.py:532
  114.9 4.9 %collective-permute-start.7 = (f32[6,256]{1,0:T(8,128)S(1)}, f32[6,256]{1,0:T(8,128)S(1)}, u32[]{:S(2)}, u32[]{:S(2)}) collective-permute-start(f32[6,256]{1,0:T(8,128)S(1)} %get-tuple-element.49), channel_id=1, source_target_pairs={{1,0},{2,1},{3,2},{0,3},{5,4},{6,5},{7,6},{4,7},{9,8},{10,9},{11,1... | collective-permute-start | bytes 18440 | tf_op jit(solution)/shard_map/ppermute | solution.py:533

commit v5 on v4

--- a/solution.py
+++ b/solution.py
@@ -327,10 +327,16 @@
     )
 
 
-def turned_sides(inside_ref, left_ref, right_ref):
+def inside():
+    slab, face = lax.axis_index("slab"), lax.axis_index("face")
+    there = [slab > 0, slab < lax.axis_size("slab") - 1, face > 0, face < lax.axis_size("face") - 1]
+    return [jnp.where(neighbour, 1.0, 0.0) for neighbour in there]
+
+
+def turned_sides(within, left_ref, right_ref):
     count = left_ref.shape[0]
     pad = jnp.zeros((8 - count, ROWS), f32)
-    left, right = left_ref[...] * inside_ref[2], right_ref[...] * inside_ref[3]
+    left, right = left_ref[...] * within[2], right_ref[...] * within[3]
     x = jnp.concatenate([left, pad, right, pad], axis=0)
     high = x.astype(bf16).astype(f32)
     rest = x - high
@@ -339,25 +345,29 @@
     return jnp.transpose(pieces).astype(bf16)
 
 
-def beside(u, above, below, sides, c):
+def inner(u):
     row = lax.broadcasted_iota(jnp.int32, (ROWS, NODES), 0)
     col = lax.broadcasted_iota(jnp.int32, (ROWS, NODES), 1)
-    up = jnp.where(row == 0, above, pltpu.roll(u, 1, 0))
-    down = jnp.where(row == ROWS - 1, below, pltpu.roll(u, ROWS - 1, 0))
+    up = jnp.where(row == 0, 0.0, pltpu.roll(u, 1, 0))
+    down = jnp.where(row == ROWS - 1, 0.0, pltpu.roll(u, ROWS - 1, 0))
     west = jnp.where(col == 0, 0.0, pltpu.roll(u, 1, 1))
     east = jnp.where(col == NODES - 1, 0.0, pltpu.roll(u, NODES - 1, 1))
+    return (down + up) + (east + west)
+
+
+def rim(within, above_ref, below_ref, sides, c):
+    row = lax.broadcasted_iota(jnp.int32, (ROWS, NODES), 0)
     piece = lax.broadcasted_iota(jnp.int32, (128, NODES), 0) & 15
     place = lax.broadcasted_iota(jnp.int32, (128, NODES), 1)
     pick = ((piece == c) & (place == 0)) | ((piece == 8 + c) & (place == NODES - 1))
     pick = jnp.where(pick, 1.0, 0.0).astype(bf16)
-    rim = lax.dot_general(sides, pick, (((1,), (0,)), ((), ())), preferred_element_type=f32)
-    return (down + up) + (east + west) + rim
-
-
-def swept(u, right, gain, inside_ref, above_ref, below_ref, sides, c):
-    above = above_ref[c : c + 1, :] * inside_ref[0]
-    below = below_ref[c : c + 1, :] * inside_ref[1]
-    around = beside(u, above, below, sides, c)
+    beside = lax.dot_general(sides, pick, (((1,), (0,)), ((), ())), preferred_element_type=f32)
+    above = above_ref[c : c + 1, :] * within[0]
+    below = below_ref[c : c + 1, :] * within[1]
+    return beside + jnp.where(row == 0, above, jnp.where(row == ROWS - 1, below, 0.0))
+
+
+def swept(u, right, gain, around):
     return (1.0 - RELAX) * u + gain * (right + around)
 
 
@@ -369,40 +379,34 @@
     right[c : c + 1, :] = jnp.transpose(u[:, 128:256])[127:128]
 
 
-def slave_right_kernel(row_ref, gap_ref, load_ref, stiff_ref, right_out, gain_out):
+def early_sweep_kernel(row_ref, gap_ref, u_ref, load_ref, stiff_ref, right_out, first_out, gain_out):
     row = lax.broadcasted_iota(jnp.int32, (ROWS, PAIRS), 0)
     hits = jnp.where(row == row_ref[...], 1.0, 0.0).astype(bf16)
-    gain_out[...] = RELAX / (4.0 + stiff_ref[...])
-    for c in range(3):
-        right_out[c] = load_ref[c] - PENALTY * gathered(hits, gap_ref[c])
-
-
-def slave_right_side(slave_row, gap, load, stiffness):
-    half = pl.BlockSpec((3, ROWS, NODES), lambda i: (0, 0, 0))
+    gain = RELAX / (4.0 + stiff_ref[...])
+    gain_out[...] = gain
+    for c in range(6):
+        right = load_ref[c]
+        if c < 3:
+            right = right - PENALTY * gathered(hits, gap_ref[c])
+        right_out[c] = right
+        first_out[c] = swept(u_ref[c], right, gain, inner(u_ref[c]))
+
+
+def early_sweep(slave_row, gap, displacement, load, stiffness):
+    whole = pl.BlockSpec((6, ROWS, NODES), lambda i: (0, 0, 0))
     plane = pl.BlockSpec((ROWS, NODES), lambda i: (0, 0))
-    return pl.pallas_call(
-        slave_right_kernel,
+    field = pltpu.HBM((6, ROWS, NODES), f32)
+    return pl.pallas_call(
+        early_sweep_kernel,
         grid=(1,),
-        out_shape=[pltpu.HBM(FIELD.shape, f32), pltpu.HBM((ROWS, NODES), f32)],
-        in_specs=[vmem(), pl.BlockSpec((3, PAIRS, NODES), lambda i: (0, 0, 0)), half, plane],
-        out_specs=[half, plane],
+        out_shape=[field, field, pltpu.HBM((ROWS, NODES), f32)],
+        in_specs=[
+            vmem(), pl.BlockSpec((3, PAIRS, NODES), lambda i: (0, 0, 0)), whole, whole, plane
+        ],
+        out_specs=[whole, whole, plane],
         compiler_params=params(),
-        name="slave_right_side",
-    )(slave_row, in_hbm(gap), in_hbm(load), in_hbm(stiffness))
-
-
-def early_sweep_kernel(
-    inside_ref, u_ref, right_ref, load_ref, gain_ref, ha, hb, hl, hr, late_out, base_out, *edges
-):
-    gain = gain_ref[...]
-    sides = turned_sides(inside_ref, hl, hr)
-    for c in range(3):
-        u = swept(u_ref[c], right_ref[c], gain, inside_ref, ha, hb, sides, c)
-        late_out[c] = u
-        late_out[3 + c] = right_ref[c]
-        late_out[6 + c] = load_ref[c]
-        put_edges(c, u, edges)
-        base_out[c] = swept(u_ref[3 + c], load_ref[c], gain, inside_ref, ha, hb, sides, 3 + c)
+        name="early_sweep",
+    )(slave_row, in_hbm(gap), in_hbm(displacement), in_hbm(load), in_hbm(stiffness))
 
 
 def edges_kernel(u_ref, *edges):
@@ -421,33 +425,18 @@
     )(displacement)
 
 
-EDGES = [jax.ShapeDtypeStruct((3, 256), f32)] * 4
-FIELD = jax.ShapeDtypeStruct((3, ROWS, NODES), f32)
-
-
-def early_sweep(within, displacement, right, load, gain, halos):
-    part = pl.BlockSpec((3, ROWS, NODES), lambda i: (0, 0, 0))
-    return pl.pallas_call(
-        early_sweep_kernel,
-        grid=(1,),
-        out_shape=[pltpu.HBM((9, ROWS, NODES), f32), pltpu.HBM(FIELD.shape, f32)] + EDGES,
-        in_specs=[
-            smem(),
-            vmem(),
-            part,
-            pl.BlockSpec((3, ROWS, NODES), lambda i: (1, 0, 0)),
-            pl.BlockSpec((ROWS, NODES), lambda i: (0, 0)),
-        ]
-        + [vmem()] * 4,
-        out_specs=[pl.BlockSpec((9, ROWS, NODES), lambda i: (0, 0, 0)), part] + [vmem()] * 4,
-        compiler_params=params(),
-        name="early_sweep",
-    )(within, displacement, in_hbm(right), in_hbm(load), in_hbm(gain), *halos)
-
-
 def master_sweep_kernel(
-    asked_ref, incoming_ref, base_ref, gain_ref, ea, eb, el, er, u_out, added_out, *edges
+    asked_ref, incoming_ref, first_ref, gain_ref, ha, hb, hl, hr,
+    u_out, added_out, *refs
 ):
+    edges, first, gain_here, sems = refs[:4], *refs[4:]
+    within = inside()
+    arrivals = [
+        pltpu.make_async_copy(first_ref.at[c], first.at[c], sems.at[c]) for c in range(6)
+    ]
+    arrivals.append(pltpu.make_async_copy(gain_ref, gain_here, sems.at[6]))
+    for k in (6, 3, 4, 5, 0, 1, 2):
+        arrivals[k].start()
     asked = jnp.transpose(asked_ref[...].reshape(DEVICES, 128))
     row = lax.broadcasted_iota(jnp.int32, (ROWS, DEVICES), 0)
     hits = jnp.concatenate(
@@ -464,62 +453,71 @@
         )
         return gathered(hits, lines)
 
-    for edge, slave_edge in zip(edges, (ea, eb, el, er)):
-        edge[0:3, :] = slave_edge[...]
-    for c in range(3):
-        added = jnp.concatenate([force(c), force(3 + c)], axis=1)
-        added_out[c] = added
-        u = base_ref[c] + gain_ref[...] * added
+    sides = turned_sides(within, hl, hr)
+    for c in (3, 4, 5, 0, 1, 2):
+        more = rim(within, ha, hb, sides, c)
+        if c >= 3:
+            added = jnp.concatenate([force(c - 3), force(c)], axis=1)
+            added_out[c - 3] = added
+            more = more + added
+        if c == 3:
+            arrivals[6].wait()
+        arrivals[c].wait()
+        u = first[c] + gain_here[...] * more
         u_out[c] = u
-        put_edges(3 + c, u, edges)
-
-
-def master_sweep(asked, incoming, base, gain, slave_edges):
+        put_edges(c, u, edges)
+
+
+def master_sweep(asked, incoming, first, gain, halos):
+    lines = jax.ShapeDtypeStruct((6, 256), f32)
     return pl.pallas_call(
         master_sweep_kernel,
-        grid=(1,),
-        out_shape=[FIELD, FIELD] + [jax.ShapeDtypeStruct((6, 256), f32)] * 4,
+        out_shape=[jax.ShapeDtypeStruct((n, ROWS, NODES), f32) for n in (6, 3)] + [lines] * 4,
         in_specs=[
             vmem(),
             vmem(),
-            pl.BlockSpec((3, ROWS, NODES), lambda i: (0, 0, 0)),
-            pl.BlockSpec((ROWS, NODES), lambda i: (0, 0)),
+            pl.BlockSpec(memory_space=pl.ANY),
+            pl.BlockSpec(memory_space=pl.ANY),
         ]
         + [vmem()] * 4,
         out_specs=[vmem()] * 6,
+        scratch_shapes=[
+            pltpu.VMEM((6, ROWS, NODES), f32),
+            pltpu.VMEM((ROWS, NODES), f32),
+            pltpu.SemaphoreType.DMA((7,)),
+        ],
         compiler_params=params(),
         name="master_sweep",
-    )(asked, in_vmem(incoming), in_hbm(base), in_hbm(gain), *slave_edges)
+    )(asked, in_vmem(incoming), in_hbm(first), in_hbm(gain), *halos)
 
 
 def last_sweep_kernel(
-    inside_ref, late_ref, um_ref, added_ref, gain_ref, ha, hb, hl, hr, out_ref, done, sems
+    u_ref, right_ref, added_ref, gain_ref, ha, hb, hl, hr, out_ref, done, sems
 ):
     copies = []
+    within = inside()
     gain = gain_ref[...]
-    sides = turned_sides(inside_ref, hl, hr)
+    sides = turned_sides(within, hl, hr)
     for c in range(6):
-        if c < 3:
-            u, right = late_ref[c], late_ref[3 + c]
-        else:
-            u, right = um_ref[c - 3], late_ref[3 + c] + added_ref[c - 3]
-        done[c] = swept(u, right, gain, inside_ref, ha, hb, sides, c)
+        right = right_ref[c] if c < 3 else right_ref[c] + added_ref[c - 3]
+        around = inner(u_ref[c]) + rim(within, ha, hb, sides, c)
+        done[c] = swept(u_ref[c], right, gain, around)
         copies.append(pltpu.make_async_copy(done.at[c], out_ref.at[c], sems.at[c]))
         copies[-1].start()
     for copy in copies:
         copy.wait()
 
 
-def last_sweep(within, late, master_u, added, gain, halos):
+def last_sweep(u, right, added, gain, halos):
     return pl.pallas_call(
         last_sweep_kernel,
         out_shape=jax.ShapeDtypeStruct((6, ROWS, NODES), f32),
-        in_specs=[smem()] + [vmem()] * 8,
+        in_specs=[vmem()] * 8,
         out_specs=pl.BlockSpec(memory_space=pl.ANY),
         scratch_shapes=[pltpu.VMEM((6, ROWS, NODES), f32), pltpu.SemaphoreType.DMA((6,))],
         compiler_params=params(),
         name="last_sweep",
-    )(within, late, master_u, added, gain, *halos)
+    )(u, right, added, gain, *halos)
 
 
 def exchange(top, bottom, left, right):
@@ -532,13 +530,6 @@
         lax.ppermute(right, "face", onward(faces)),
         lax.ppermute(left, "face", back(faces)),
     )
-
-
-def inside():
-    slab, face = lax.axis_index("slab"), lax.axis_index("face")
-    return jnp.stack(
-        [slab > 0, slab < lax.axis_size("slab") - 1, face > 0, face < lax.axis_size("face") - 1]
-    ).astype(f32)
 
 
 def all_to_all(x):
@@ -565,13 +556,11 @@
     arrived = all_to_all(served).reshape(SLOT_ROWS, 128)
     gap, outgoing = couple(slot, slave_row, turned, displacement, arrived)
     incoming = all_to_all(outgoing.reshape(DEVICES, CAP * PARTS, 128)).reshape(SLOT_ROWS, 128)
-    slave_right, gain = slave_right_side(slave_row.reshape(1, PAIRS), gap, load, stiffness)
-    within = inside()
-    late, base, *slave_edges = early_sweep(
-        within, displacement, slave_right, load, gain, first_halos
+    right, first, gain = early_sweep(
+        slave_row.reshape(1, PAIRS), gap, displacement, load, stiffness
     )
-    master_u, added, *edges = master_sweep(asked, incoming, base, gain, slave_edges)
-    relaxed = last_sweep(within, late, master_u, added, gain, exchange(*edges))
+    u, added, *edges = master_sweep(asked, incoming, first, gain, first_halos)
+    relaxed = last_sweep(u, right, added, gain, exchange(*edges))
     return relaxed, gap.transpose(1, 0, 2)
 
 

time: 123 us -> 121 us (0.984)
  Pallas kernels: 58.1 us -> 55.4 us
    ppermute x2, waiting for transfers between devices: 11.6 us -> 9.39 us  [exchange(): lax.ppermute(bottom, 'slab', onward(slabs))]
    pallas_call x3 -> x2, Pallas kernels: 10.1 us -> 7.95 us  [the longest x1 4.97 us: early_sweep(): pl.pallas_call(early_sweep_kernel, grid=(1,), out_shape=[field, field, pl...]
    ppermute x2, starting transfers between devices: 3.22 us -> 1.57 us  [exchange(): lax.ppermute(left, 'face', back(faces))]
    ppermute x2, waiting for transfers between devices: 1.44 us -> 3.09 us  [exchange(): lax.ppermute(left, 'face', back(faces))]
    ppermute x2, starting transfers between devices: 0.83 us -> 2.48 us  [exchange(): lax.ppermute(right, 'face', onward(faces))]
  transfers between devices with their start and end apart: 10 -> 10, of which waited for: 3 -> 4; matrix products, arithmetic and copies ran while one was open for 0% -> 0% of each run, Pallas kernels for 26% -> 24%
where the time goes in v5:
time: 121 us; the launch traced here: 120 us
  Pallas kernels  55.4 us (46%)
  starting transfers between devices  30.6 us (25%)
  blocking collectives  18.3 us (15%)
  waiting for transfers between devices  15.1 us (12%)
    pallas_call x1, Pallas kernels, couple_tables(): pl.pallas_call(tables_kernel, grid_spec=pltpu.PrefetchScalarGridSpec(num_...  23.7 us
    all_to_all x1, blocking collectives, all_to_all(): return lax.all_to_all(x, AXES, split_axis=0, concat_axis=0, tiled=True)  18.3 us
    pallas_call x1, Pallas kernels, couple(): pl.pallas_call(couple_kernel, grid_spec=pltpu.PrefetchScalarGridSpec(num_...  15.9 us
    all_to_all x2, starting transfers between devices, all_to_all(): return lax.all_to_all(x, AXES, split_axis=0, concat_axis=0, tiled=True)  15.7 us
    ppermute x2, starting transfers between devices, exchange(): lax.ppermute(top, 'slab', back(slabs))  10.4 us
    ppermute x2, waiting for transfers between devices, exchange(): lax.ppermute(bottom, 'slab', onward(slabs))  9.39 us
    pallas_call x1, Pallas kernels, early_sweep(): pl.pallas_call(early_sweep_kernel, grid=(1,), out_shape=[field, field, pl...  4.97 us
    pallas_call x1, Pallas kernels, serve(): pl.pallas_call(serve_kernel, grid=(SERVE_STEPS,), out_shape=pltpu.HBM((DE...  3.76 us
  transfers between devices with their start and end apart: 10, of which 4 were waited for; matrix products, arithmetic and copies ran while one was open for 0% of the time, Pallas kernels for 24%

profile of v5, /device:TPU:24, one launch (start us, length us, event | category | flops | bytes accessed | tf_op | source)
XLA Modules:
  0.0 120.4 jit_solution(12409583502349354565)
XLA Ops:
  0.6 1.6 %slots.1 = (s32[128,1,128]{2,1,0:T(1,128)}, s32[1,128]{1,0:T(1,128)}) custom-call(s32[1,128]{1,0:T(1,128)} %bitcast.16, s32[1,128]{1,0:T(1,128)} %bitcast.17), custom_call_target="tpu_custom_call" | custom-call | tf_op jit(solution)/shard_map/slots/pallas_call | solution.py:70
  2.2 18.3 %all_to_all.15.asked_ref = s32[128,1,128]{2,1,0:T(1,128)S(1)} all-to-all(s32[128,1,128]{2,1,0:T(1,128)} %get-tuple-element.21), channel_id=1, replica_groups=mesh['slab'=32,'face'=4] {'slab','face'}, dimensions={0} | all-to-all | bytes 131072 | tf_op jit(solution)/shard_map/all_to_all | solution.py:536
  20.6 3.8 %serve.1 = f32[128,24,128]{2,1,0:T(8,128)} custom-call(s32[16384]{0:T(1024)S(1)} %bitcast.11, f32[6,256,256]{2,1,0:T(8,128)} %u_ref.3), custom_call_target="tpu_custom_call" | custom-call | tf_op jit(solution)/shard_map/serve/pallas_call | solution.py:108
  24.3 0.0 copy-start.5
  24.3 5.9 %all-to-all-start.1 = ((f32[128,24,128]{2,1,0:T(8,128)}), f32[128,24,128]{2,1,0:T(8,128)S(1)}, u32[]{:S(2)}, u32[]{:S(2)}) async-start(f32[128,24,128]{2,1,0:T(8,128)} %serve.1), calls=%async_computation.1 | async-start | bytes 3145728 | tf_op jit(solution)/shard_map/all_to_all | solution.py:536
  30.3 0.0 copy-done.5
  30.3 0.0 copy-start.3
  30.3 0.0 copy-start.4
  30.3 23.7 %couple_tables.1 = (bf16[128,256,256]{2,1,0:T(8,128)(2,1)}, f8e5m2[128,256,256]{2,1,0:T(32,128)(4,1)}) custom-call(s32[128]{0:T(128)S(1)} %copy-done.5, f32[128,4,384]{2,1,0:T(4,128)} %coords_ref.1, f32[128,384]{1,0:T(8,128)} %weights_ref.1), custom_call_target="tpu_custom_call" | custom-call | flops 25769803776 | bytes 67108864 | tf_op jit(solution)/shard_map/couple_tables/pallas_call | solution.py:166
  54.0 0.0 all-to-all-done.1
  54.0 0.0 copy-done.3
  54.0 0.0 copy-done.4
  54.0 15.9 %couple.1 = (f32[3,128,256]{2,1,0:T(8,128)}, f32[3072,128]{1,0:T(8,128)}) custom-call(s32[128]{0:T(128)S(1)} %bitcast.13, s32[128]{0:T(128)S(1)} %copy-done.3, bf16[128,256,256]{2,1,0:T(8,128)(2,1)} %get-tuple-element.23.high_ref, f8e5m2[128,256,256]{2,1,0:T(32,128)(4,1)} %get-tuple-element.24.rest_ref, f32[6,256,256]{2,1,0:T(8,128)} %u_ref.3, ...), custom_call_target="tpu_custom_call" | custom-call | tf_op jit(solution)/shard_map/couple/pallas_call | solution.py:297
  69.9 0.0 copy-start
  69.9 9.8 %all-to-all-start.2 = ((f32[128,24,128]{2,1,0:T(8,128)}), f32[128,24,128]{2,1,0:T(8,128)S(1)}, u32[]{:S(2)}, u32[]{:S(2)}) async-start(f32[128,24,128]{2,1,0:T(8,128)} %bitcast.14), calls=%async_computation.2 | async-start | bytes 3145728 | tf_op jit(solution)/shard_map/all_to_all | solution.py:536
  79.7 0.0 copy-done
  79.7 0.5 first_edges.1
  80.2 0.2 collective-permute-start
  80.4 5.3 %collective-permute-start.1 = (f32[6,256]{1,0:T(8,128)S(1)}, f32[6,256]{1,0:T(8,128)S(1)}, u32[]{:S(2)}, u32[]{:S(2)}) collective-permute-start(f32[6,256]{1,0:T(8,128)S(1)} %get-tuple-element.30), channel_id=1, source_target_pairs={{4,0},{8,4},{12,8},{16,12},{20,16},{24,20},{28,24},{32,28},{36,32}... | collective-permute-start | bytes 18440 | tf_op jit(solution)/shard_map/ppermute | solution.py:529
  85.7 0.6 collective-permute-start.2
  86.3 1.4 %collective-permute-start.3 = (f32[6,256]{1,0:T(8,128)S(1)}, f32[6,256]{1,0:T(8,128)S(1)}, u32[]{:S(2)}, u32[]{:S(2)}) collective-permute-start(f32[6,256]{1,0:T(8,128)S(1)} %get-tuple-element.32), channel_id=1, source_target_pairs={{1,0},{2,1},{3,2},{0,3},{5,4},{6,5},{7,6},{4,7},{9,8},{10,9},{11,1... | collective-permute-start | bytes 18440 | tf_op jit(solution)/shard_map/ppermute | solution.py:531
  87.7 5.0 %early_sweep.1 = (f32[6,256,256]{2,1,0:T(8,128)}, f32[6,256,256]{2,1,0:T(8,128)}, f32[256,256]{1,0:T(8,128)}) custom-call(s32[1,128]{1,0:T(1,128)S(1)} %bitcast.12, f32[3,128,256]{2,1,0:T(8,128)} %get-tuple-element.26.gap_ref, f32[6,256,256]{2,1,0:T(8,128)} %u_ref.3, f32[6,256,256]{2,1,0:T(8,128)} %load_ref.1, f32[256,256]{1,0:T(8,128)} %stiff_ref.1), custom_call_target="tpu_custom_call" | custom-call | tf_op jit(solution)/shard_map/early_sweep/pallas_call | solution.py:399
  92.7 9.4 %collective-permute-done.ha = f32[6,256]{1,0:T(8,128)S(1)} collective-permute-done((f32[6,256]{1,0:T(8,128)S(1)}, f32[6,256]{1,0:T(8,128)S(1)}, u32[]{:S(2)}, u32[]{:S(2)}) %collective-permute-start) | collective-permute-done | bytes 6176 | tf_op jit(solution)/shard_map/ppermute | solution.py:528
  102.1 0.0 collective-permute-done.1.hb
  102.1 0.0 collective-permute-done.2.hl
  102.1 0.0 collective-permute-done.3.hr
  102.1 1.0 all-to-all-done.2
  103.1 0.0 copy-start.1
  103.1 0.0 copy-start.2
  103.1 3.0 %master_sweep.1 = (f32[6,256,256]{2,1,0:T(8,128)S(1)}, f32[3,256,256]{2,1,0:T(8,128)S(1)}, f32[6,256]{1,0:T(8,128)S(1)}, f32[6,256]{1,0:T(8,128)S(1)}, f32[6,256]{1,0:T(8,128)S(1)}, /*index=5*/f32[6,256]{1,0:T(8,128)S(1)}) custom-call(s32[128,1,128]{2,1,0:T(1,128)S(1)} %all_to_all.15.asked_ref, f32[3072,128]{1,0:T(8,128)S(1)} %bitcast.9, ...), custom_call_target="tpu_custom_call" | custom-call | tf_op jit(solution)/shard_map/master_sweep/pallas_call | solution.py:473
  106.1 0.3 collective-permute-start.4
  106.4 5.1 %collective-permute-start.5 = (f32[6,256]{1,0:T(8,128)S(1)}, f32[6,256]{1,0:T(8,128)S(1)}, u32[]{:S(2)}, u32[]{:S(2)}) collective-permute-start(f32[6,256]{1,0:T(8,128)S(1)} %get-tuple-element.37), channel_id=1, source_target_pairs={{4,0},{8,4},{12,8},{16,12},{20,16},{24,20},{28,24},{32,28},{36,32}... | collective-permute-start | bytes 18440 | tf_op jit(solution)/shard_map/ppermute | solution.py:529
  111.4 1.9 %collective-permute-start.6 = (f32[6,256]{1,0:T(8,128)S(1)}, f32[6,256]{1,0:T(8,128)S(1)}, u32[]{:S(2)}, u32[]{:S(2)}) collective-permute-start(f32[6,256]{1,0:T(8,128)S(1)} %get-tuple-element.38), channel_id=1, source_target_pairs={{0,1},{1,2},{2,3},{3,0},{4,5},{5,6},{6,7},{7,4},{8,9},{9,10},{10,1... | collective-permute-start | bytes 18440 | tf_op jit(solution)/shard_map/ppermute | solution.py:530
  113.3 0.1 collective-permute-start.7
  113.5 0.0 collective-permute-done.4.ha
  113.5 0.0 collective-permute-done.5.hb
  113.5 1.6 %collective-permute-done.6.hl = f32[6,256]{1,0:T(8,128)S(1)} collective-permute-done((f32[6,256]{1,0:T(8,128)S(1)}, f32[6,256]{1,0:T(8,128)S(1)}, u32[]{:S(2)}, u32[]{:S(2)}) %collective-permute-start.6) | collective-permute-done | bytes 6176 | tf_op jit(solution)/shard_map/ppermute | solution.py:530
  115.1 3.1 %collective-permute-done.7.hr = f32[6,256]{1,0:T(8,128)S(1)} collective-permute-done((f32[6,256]{1,0:T(8,128)S(1)}, f32[6,256]{1,0:T(8,128)S(1)}, u32[]{:S(2)}, u32[]{:S(2)}) %collective-permute-start.7) | collective-permute-done | bytes 6176 | tf_op jit(solution)/shard_map/ppermute | solution.py:531
  118.2 0.0 copy-done.1
  118.2 0.0 copy-done.2
  118.2 2.0 %last_sweep.1 = f32[6,256,256]{2,1,0:T(8,128)} custom-call(f32[6,256,256]{2,1,0:T(8,128)S(1)} %get-tuple-element.33.u_ref, f32[6,256,256]{2,1,0:T(8,128)S(1)} %copy-done.1, f32[3,256,256]{2,1,0:T(8,128)S(1)} %get-tuple-element.35.added_ref, f32[256,256]{1,0:T(8,128)S(1)} %copy-done.2, f32[6,256]{1,0:T(8,128)S(1)} %collective-permute-done.4.ha, ...), custom_call_target="tpu_custom_call" | custom-call | tf_op jit(solution)/shard_map/last_sweep/pallas_call | solution.py:512
Async XLA Ops:
  24.3 6.0 %copy-start.5 = (s32[128]{0:T(128)S(1)}, s32[128]{0:T(128)}, u32[]{:S(2)}) copy-start(s32[128]{0:T(128)} %seg_ref.1) | copy-start | bytes 1540
  24.3 29.7 %all-to-all-start.1 = ((f32[128,24,128]{2,1,0:T(8,128)}), f32[128,24,128]{2,1,0:T(8,128)S(1)}, u32[]{:S(2)}, u32[]{:S(2)}) async-start(f32[128,24,128]{2,1,0:T(8,128)} %serve.1), calls=%async_computation.1 | async-start | bytes 3145728 | tf_op jit(solution)/shard_map/all_to_all | solution.py:536
  30.3 23.7 %copy-start.3 = (s32[128]{0:T(128)S(1)}, s32[128]{0:T(128)}, u32[]{:S(2)}) copy-start(s32[128]{0:T(128)} %row_ref.1) | copy-start | bytes 1540
  30.3 23.7 %copy-start.4 = (s32[1,128]{1,0:T(1,128)S(1)}, s32[1,128]{1,0:T(1,128)}, u32[]{:S(2)}) copy-start(s32[1,128]{1,0:T(1,128)} %get-tuple-element.22) | copy-start | bytes 1540
  69.9 9.8 %copy-start = (f32[6,256,256]{2,1,0:T(8,128)S(1)}, f32[6,256,256]{2,1,0:T(8,128)}, u32[]{:S(2)}) copy-start(f32[6,256,256]{2,1,0:T(8,128)} %u_ref.3) | copy-start | bytes 4718596
  69.9 33.2 %all-to-all-start.2 = ((f32[128,24,128]{2,1,0:T(8,128)}), f32[128,24,128]{2,1,0:T(8,128)S(1)}, u32[]{:S(2)}, u32[]{:S(2)}) async-start(f32[128,24,128]{2,1,0:T(8,128)} %bitcast.14), calls=%async_computation.2 | async-start | bytes 3145728 | tf_op jit(solution)/shard_map/all_to_all | solution.py:536
  80.2 21.9 %collective-permute-start = (f32[6,256]{1,0:T(8,128)S(1)}, f32[6,256]{1,0:T(8,128)S(1)}, u32[]{:S(2)}, u32[]{:S(2)}) collective-permute-start(f32[6,256]{1,0:T(8,128)S(1)} %get-tuple-element.29), channel_id=1, source_target_pairs={{0,4},{4,8},{8,12},{12,16},{16,20},{20,24},{24,28},{28,32},{32,36}... | collective-permute-start | bytes 18440 | tf_op jit(solution)/shard_map/ppermute | solution.py:528
  80.4 21.7 %collective-permute-start.1 = (f32[6,256]{1,0:T(8,128)S(1)}, f32[6,256]{1,0:T(8,128)S(1)}, u32[]{:S(2)}, u32[]{:S(2)}) collective-permute-start(f32[6,256]{1,0:T(8,128)S(1)} %get-tuple-element.30), channel_id=1, source_target_pairs={{4,0},{8,4},{12,8},{16,12},{20,16},{24,20},{28,24},{32,28},{36,32}... | collective-permute-start | bytes 18440 | tf_op jit(solution)/shard_map/ppermute | solution.py:529
  85.7 16.4 %collective-permute-start.2 = (f32[6,256]{1,0:T(8,128)S(1)}, f32[6,256]{1,0:T(8,128)S(1)}, u32[]{:S(2)}, u32[]{:S(2)}) collective-permute-start(f32[6,256]{1,0:T(8,128)S(1)} %get-tuple-element.31), channel_id=1, source_target_pairs={{0,1},{1,2},{2,3},{3,0},{4,5},{5,6},{6,7},{7,4},{8,9},{9,10},{10,1... | collective-permute-start | bytes 18440 | tf_op jit(solution)/shard_map/ppermute | solution.py:530
  86.3 15.8 %collective-permute-start.3 = (f32[6,256]{1,0:T(8,128)S(1)}, f32[6,256]{1,0:T(8,128)S(1)}, u32[]{:S(2)}, u32[]{:S(2)}) collective-permute-start(f32[6,256]{1,0:T(8,128)S(1)} %get-tuple-element.32), channel_id=1, source_target_pairs={{1,0},{2,1},{3,2},{0,3},{5,4},{6,5},{7,6},{4,7},{9,8},{10,9},{11,1... | collective-permute-start | bytes 18440 | tf_op jit(solution)/shard_map/ppermute | solution.py:531
  103.1 15.1 %copy-start.1 = (f32[6,256,256]{2,1,0:T(8,128)S(1)}, f32[6,256,256]{2,1,0:T(8,128)}, u32[]{:S(2)}) copy-start(f32[6,256,256]{2,1,0:T(8,128)} %get-tuple-element.34.right_ref) | copy-start | bytes 4718596
  103.1 15.1 %copy-start.2 = (f32[256,256]{1,0:T(8,128)S(1)}, f32[256,256]{1,0:T(8,128)}, u32[]{:S(2)}) copy-start(f32[256,256]{1,0:T(8,128)} %get-tuple-element.28.gain_ref) | copy-start | bytes 786436
  106.1 7.3 %collective-permute-start.4 = (f32[6,256]{1,0:T(8,128)S(1)}, f32[6,256]{1,0:T(8,128)S(1)}, u32[]{:S(2)}, u32[]{:S(2)}) collective-permute-start(f32[6,256]{1,0:T(8,128)S(1)} %get-tuple-element.36), channel_id=1, source_target_pairs={{0,4},{4,8},{8,12},{12,16},{16,20},{20,24},{24,28},{28,32},{32,36}... | collective-permute-start | bytes 18440 | tf_op jit(solution)/shard_map/ppermute | solution.py:528
  106.4 7.1 %collective-permute-start.5 = (f32[6,256]{1,0:T(8,128)S(1)}, f32[6,256]{1,0:T(8,128)S(1)}, u32[]{:S(2)}, u32[]{:S(2)}) collective-permute-start(f32[6,256]{1,0:T(8,128)S(1)} %get-tuple-element.37), channel_id=1, source_target_pairs={{4,0},{8,4},{12,8},{16,12},{20,16},{24,20},{28,24},{32,28},{36,32}... | collective-permute-start | bytes 18440 | tf_op jit(solution)/shard_map/ppermute | solution.py:529
  111.4 3.7 %collective-permute-start.6 = (f32[6,256]{1,0:T(8,128)S(1)}, f32[6,256]{1,0:T(8,128)S(1)}, u32[]{:S(2)}, u32[]{:S(2)}) collective-permute-start(f32[6,256]{1,0:T(8,128)S(1)} %get-tuple-element.38), channel_id=1, source_target_pairs={{0,1},{1,2},{2,3},{3,0},{4,5},{5,6},{6,7},{7,4},{8,9},{9,10},{10,1... | collective-permute-start | bytes 18440 | tf_op jit(solution)/shard_map/ppermute | solution.py:530
  113.3 4.9 %collective-permute-start.7 = (f32[6,256]{1,0:T(8,128)S(1)}, f32[6,256]{1,0:T(8,128)S(1)}, u32[]{:S(2)}, u32[]{:S(2)}) collective-permute-start(f32[6,256]{1,0:T(8,128)S(1)} %get-tuple-element.39), channel_id=1, source_target_pairs={{1,0},{2,1},{3,2},{0,3},{5,4},{6,5},{7,6},{4,7},{9,8},{10,9},{11,1... | collective-permute-start | bytes 18440 | tf_op jit(solution)/shard_map/ppermute | solution.py:531

commit v6 on v5

--- a/solution.py
+++ b/solution.py
@@ -219,7 +219,7 @@
 
 def couple_kernel(
     slot_ref, row_ref, high_ref, rest_ref, field_ref, arrived_ref,
-    gap_ref, back_ref, highs, rests, held, held_small, sems,
+    gap_ref, back_ref, highs, rests, held, held_small, field_here, sems, field_sem,
 ):
     count = PAIRS // COUPLE_BLOCK
 
@@ -250,7 +250,7 @@
         pulled = times(two_pieces(u), highs[room, p])
         pulled = pulled + times(two_small_pieces(u), rests[room, p]) * (1.0 / REST_SCALE)
         r = row_ref[pair]
-        lines = [field_ref[c, pl.ds(r, 1), :] for c in range(3)]
+        lines = [field_here[c, pl.ds(r, 1), :] for c in range(3)]
         gap = jnp.concatenate(lines + [empty], axis=0) - pulled
         for c in range(3):
             gap_ref[c, pl.ds(pair, 1), :] = gap[c : c + 1]
@@ -266,10 +266,14 @@
             [back[0:3, 0:128], back[0:3, 128:256]], axis=0
         )
 
-    for ahead in range(SLOTS - 1):
-        start(ahead)
+    start(0)
+    field = pltpu.make_async_copy(field_ref.at[0:3], field_here, field_sem)
+    field.start()
+    start(1)
     back_ref[...] = jnp.zeros_like(back_ref)
     wait(0)
+    start(2)
+    field.wait()
     for p in range(COUPLE_BLOCK):
         pull(0, p)
 
@@ -299,14 +303,16 @@
         grid_spec=pltpu.PrefetchScalarGridSpec(
             num_scalar_prefetch=2,
             grid=(1,),
-            in_specs=[anywhere, anywhere, pl.BlockSpec((3, ROWS, NODES), whole), vmem()],
+            in_specs=[anywhere, anywhere, anywhere, vmem()],
             out_specs=[pl.BlockSpec((3, PAIRS, NODES), whole), flat],
             scratch_shapes=[
                 pltpu.VMEM((SLOTS, COUPLE_BLOCK, NODES, NODES), bf16),
                 pltpu.VMEM((SLOTS, COUPLE_BLOCK, NODES, NODES), f8),
                 pltpu.VMEM((COUPLE_BLOCK, 16, NODES), bf16),
                 pltpu.VMEM((COUPLE_BLOCK, 32, NODES), f8),
+                pltpu.VMEM((3, ROWS, NODES), f32),
                 pltpu.SemaphoreType.DMA((2, SLOTS)),
+                pltpu.SemaphoreType.DMA,
             ],
         ),
         out_shape=[

time: 121 us -> 120 us (level)
  no operation moved by 1% of the time
where the time goes in v6:
time: 120 us
  Pallas kernels  54.7 us (46%)
  starting transfers between devices  30.6 us (26%)
  blocking collectives  18.3 us (15%)
  waiting for transfers between devices  15.1 us (13%)
    pallas_call x1, Pallas kernels, couple_tables(): pl.pallas_call(tables_kernel, grid_spec=pltpu.PrefetchScalarGridSpec(num_...  23.7 us
    all_to_all x1, blocking collectives, all_to_all(): return lax.all_to_all(x, AXES, split_axis=0, concat_axis=0, tiled=True)  18.3 us
    all_to_all x2, starting transfers between devices, all_to_all(): return lax.all_to_all(x, AXES, split_axis=0, concat_axis=0, tiled=True)  15.7 us
    pallas_call x1, Pallas kernels, couple(): pl.pallas_call(couple_kernel, grid_spec=pltpu.PrefetchScalarGridSpec(num_...  15.2 us
    ppermute x2, starting transfers between devices, exchange(): lax.ppermute(top, 'slab', back(slabs))  10.4 us
    ppermute x2, waiting for transfers between devices, exchange(): lax.ppermute(bottom, 'slab', onward(slabs))  9.39 us
    pallas_call x1, Pallas kernels, early_sweep(): pl.pallas_call(early_sweep_kernel, grid=(1,), out_shape=[field, field, pl...  4.97 us
    pallas_call x1, Pallas kernels, serve(): pl.pallas_call(serve_kernel, grid=(SERVE_STEPS,), out_shape=pltpu.HBM((DE...  3.76 us
  transfers between devices with their start and end apart: 10, of which 4 were waited for; matrix products, arithmetic and copies ran while one was open for 0% of the time, Pallas kernels for 24%

profile of v6, /device:TPU:24, one launch (start us, length us, event | category | flops | bytes accessed | tf_op | source)
XLA Modules:
  0.0 119.7 jit_solution(9043228719921474069)
XLA Ops:
  0.6 1.6 %slots.1 = (s32[128,1,128]{2,1,0:T(1,128)}, s32[1,128]{1,0:T(1,128)}) custom-call(s32[1,128]{1,0:T(1,128)} %bitcast.16, s32[1,128]{1,0:T(1,128)} %bitcast.17), custom_call_target="tpu_custom_call" | custom-call | tf_op jit(solution)/shard_map/slots/pallas_call | solution.py:70
  2.2 18.3 %all_to_all.15.asked_ref = s32[128,1,128]{2,1,0:T(1,128)S(1)} all-to-all(s32[128,1,128]{2,1,0:T(1,128)} %get-tuple-element.21), channel_id=1, replica_groups=mesh['slab'=32,'face'=4] {'slab','face'}, dimensions={0} | all-to-all | bytes 131072 | tf_op jit(solution)/shard_map/all_to_all | solution.py:542
  20.6 3.8 %serve.1 = f32[128,24,128]{2,1,0:T(8,128)} custom-call(s32[16384]{0:T(1024)S(1)} %bitcast.11, f32[6,256,256]{2,1,0:T(8,128)} %u_ref.3), custom_call_target="tpu_custom_call" | custom-call | tf_op jit(solution)/shard_map/serve/pallas_call | solution.py:108
  24.3 0.0 copy-start.5
  24.3 5.9 %all-to-all-start.1 = ((f32[128,24,128]{2,1,0:T(8,128)}), f32[128,24,128]{2,1,0:T(8,128)S(1)}, u32[]{:S(2)}, u32[]{:S(2)}) async-start(f32[128,24,128]{2,1,0:T(8,128)} %serve.1), calls=%async_computation.1 | async-start | bytes 3145728 | tf_op jit(solution)/shard_map/all_to_all | solution.py:542
  30.3 0.0 copy-done.5
  30.3 0.0 copy-start.3
  30.3 0.0 copy-start.4
  30.3 23.7 %couple_tables.1 = (bf16[128,256,256]{2,1,0:T(8,128)(2,1)}, f8e5m2[128,256,256]{2,1,0:T(32,128)(4,1)}) custom-call(s32[128]{0:T(128)S(1)} %copy-done.5, f32[128,4,384]{2,1,0:T(4,128)} %coords_ref.1, f32[128,384]{1,0:T(8,128)} %weights_ref.1), custom_call_target="tpu_custom_call" | custom-call | flops 25769803776 | bytes 67108864 | tf_op jit(solution)/shard_map/couple_tables/pallas_call | solution.py:166
  54.0 0.0 all-to-all-done.1
  54.0 0.0 copy-done.3
  54.0 0.0 copy-done.4
  54.0 15.2 %couple.1 = (f32[3,128,256]{2,1,0:T(8,128)}, f32[3072,128]{1,0:T(8,128)}) custom-call(s32[128]{0:T(128)S(1)} %bitcast.13, s32[128]{0:T(128)S(1)} %copy-done.3, bf16[128,256,256]{2,1,0:T(8,128)(2,1)} %get-tuple-element.23.high_ref, f8e5m2[128,256,256]{2,1,0:T(32,128)(4,1)} %get-tuple-element.24.rest_ref, f32[6,256,256]{2,1,0:T(8,128)} %u_ref.3, ...), custom_call_target="tpu_custom_call" | custom-call | tf_op jit(solution)/shard_map/couple/pallas_call | solution.py:301
  69.2 0.0 copy-start
  69.2 9.8 %all-to-all-start.2 = ((f32[128,24,128]{2,1,0:T(8,128)}), f32[128,24,128]{2,1,0:T(8,128)S(1)}, u32[]{:S(2)}, u32[]{:S(2)}) async-start(f32[128,24,128]{2,1,0:T(8,128)} %bitcast.14), calls=%async_computation.2 | async-start | bytes 3145728 | tf_op jit(solution)/shard_map/all_to_all | solution.py:542
  79.0 0.0 copy-done
  79.0 0.5 first_edges.1
  79.5 0.2 collective-permute-start
  79.7 5.3 %collective-permute-start.1 = (f32[6,256]{1,0:T(8,128)S(1)}, f32[6,256]{1,0:T(8,128)S(1)}, u32[]{:S(2)}, u32[]{:S(2)}) collective-permute-start(f32[6,256]{1,0:T(8,128)S(1)} %get-tuple-element.30), channel_id=1, source_target_pairs={{4,0},{8,4},{12,8},{16,12},{20,16},{24,20},{28,24},{32,28},{36,32}... | collective-permute-start | bytes 18440 | tf_op jit(solution)/shard_map/ppermute | solution.py:535
  85.0 0.6 collective-permute-start.2
  85.6 1.4 %collective-permute-start.3 = (f32[6,256]{1,0:T(8,128)S(1)}, f32[6,256]{1,0:T(8,128)S(1)}, u32[]{:S(2)}, u32[]{:S(2)}) collective-permute-start(f32[6,256]{1,0:T(8,128)S(1)} %get-tuple-element.32), channel_id=1, source_target_pairs={{1,0},{2,1},{3,2},{0,3},{5,4},{6,5},{7,6},{4,7},{9,8},{10,9},{11,1... | collective-permute-start | bytes 18440 | tf_op jit(solution)/shard_map/ppermute | solution.py:537
  87.1 5.0 %early_sweep.1 = (f32[6,256,256]{2,1,0:T(8,128)}, f32[6,256,256]{2,1,0:T(8,128)}, f32[256,256]{1,0:T(8,128)}) custom-call(s32[1,128]{1,0:T(1,128)S(1)} %bitcast.12, f32[3,128,256]{2,1,0:T(8,128)} %get-tuple-element.26.gap_ref, f32[6,256,256]{2,1,0:T(8,128)} %u_ref.3, f32[6,256,256]{2,1,0:T(8,128)} %load_ref.1, f32[256,256]{1,0:T(8,128)} %stiff_ref.1), custom_call_target="tpu_custom_call" | custom-call | tf_op jit(solution)/shard_map/early_sweep/pallas_call | solution.py:405
  92.0 9.4 %collective-permute-done.ha = f32[6,256]{1,0:T(8,128)S(1)} collective-permute-done((f32[6,256]{1,0:T(8,128)S(1)}, f32[6,256]{1,0:T(8,128)S(1)}, u32[]{:S(2)}, u32[]{:S(2)}) %collective-permute-start) | collective-permute-done | bytes 6176 | tf_op jit(solution)/shard_map/ppermute | solution.py:534
  101.4 0.0 collective-permute-done.1.hb
  101.4 0.0 collective-permute-done.2.hl
  101.4 0.0 collective-permute-done.3.hr
  101.4 1.0 all-to-all-done.2
  102.5 0.0 copy-start.1
  102.5 0.0 copy-start.2
  102.5 3.0 %master_sweep.1 = (f32[6,256,256]{2,1,0:T(8,128)S(1)}, f32[3,256,256]{2,1,0:T(8,128)S(1)}, f32[6,256]{1,0:T(8,128)S(1)}, f32[6,256]{1,0:T(8,128)S(1)}, f32[6,256]{1,0:T(8,128)S(1)}, /*index=5*/f32[6,256]{1,0:T(8,128)S(1)}) custom-call(s32[128,1,128]{2,1,0:T(1,128)S(1)} %all_to_all.15.asked_ref, f32[3072,128]{1,0:T(8,128)S(1)} %bitcast.9, ...), custom_call_target="tpu_custom_call" | custom-call | tf_op jit(solution)/shard_map/master_sweep/pallas_call | solution.py:479
  105.5 0.3 collective-permute-start.4
  105.7 5.1 %collective-permute-start.5 = (f32[6,256]{1,0:T(8,128)S(1)}, f32[6,256]{1,0:T(8,128)S(1)}, u32[]{:S(2)}, u32[]{:S(2)}) collective-permute-start(f32[6,256]{1,0:T(8,128)S(1)} %get-tuple-element.37), channel_id=1, source_target_pairs={{4,0},{8,4},{12,8},{16,12},{20,16},{24,20},{28,24},{32,28},{36,32}... | collective-permute-start | bytes 18440 | tf_op jit(solution)/shard_map/ppermute | solution.py:535
  110.8 1.9 %collective-permute-start.6 = (f32[6,256]{1,0:T(8,128)S(1)}, f32[6,256]{1,0:T(8,128)S(1)}, u32[]{:S(2)}, u32[]{:S(2)}) collective-permute-start(f32[6,256]{1,0:T(8,128)S(1)} %get-tuple-element.38), channel_id=1, source_target_pairs={{0,1},{1,2},{2,3},{3,0},{4,5},{5,6},{6,7},{7,4},{8,9},{9,10},{10,1... | collective-permute-start | bytes 18440 | tf_op jit(solution)/shard_map/ppermute | solution.py:536
  112.7 0.1 collective-permute-start.7
  112.8 0.0 collective-permute-done.4.ha
  112.8 0.0 collective-permute-done.5.hb
  112.8 1.6 %collective-permute-done.6.hl = f32[6,256]{1,0:T(8,128)S(1)} collective-permute-done((f32[6,256]{1,0:T(8,128)S(1)}, f32[6,256]{1,0:T(8,128)S(1)}, u32[]{:S(2)}, u32[]{:S(2)}) %collective-permute-start.6) | collective-permute-done | bytes 6176 | tf_op jit(solution)/shard_map/ppermute | solution.py:536
  114.4 3.1 %collective-permute-done.7.hr = f32[6,256]{1,0:T(8,128)S(1)} collective-permute-done((f32[6,256]{1,0:T(8,128)S(1)}, f32[6,256]{1,0:T(8,128)S(1)}, u32[]{:S(2)}, u32[]{:S(2)}) %collective-permute-start.7) | collective-permute-done | bytes 6176 | tf_op jit(solution)/shard_map/ppermute | solution.py:537
  117.5 0.0 copy-done.1
  117.5 0.0 copy-done.2
  117.5 2.0 %last_sweep.1 = f32[6,256,256]{2,1,0:T(8,128)} custom-call(f32[6,256,256]{2,1,0:T(8,128)S(1)} %get-tuple-element.33.u_ref, f32[6,256,256]{2,1,0:T(8,128)S(1)} %copy-done.1, f32[3,256,256]{2,1,0:T(8,128)S(1)} %get-tuple-element.35.added_ref, f32[256,256]{1,0:T(8,128)S(1)} %copy-done.2, f32[6,256]{1,0:T(8,128)S(1)} %collective-permute-done.4.ha, ...), custom_call_target="tpu_custom_call" | custom-call | tf_op jit(solution)/shard_map/last_sweep/pallas_call | solution.py:518
Async XLA Ops:
  24.3 6.0 %copy-start.5 = (s32[128]{0:T(128)S(1)}, s32[128]{0:T(128)}, u32[]{:S(2)}) copy-start(s32[128]{0:T(128)} %seg_ref.1) | copy-start | bytes 1540
  24.3 29.7 %all-to-all-start.1 = ((f32[128,24,128]{2,1,0:T(8,128)}), f32[128,24,128]{2,1,0:T(8,128)S(1)}, u32[]{:S(2)}, u32[]{:S(2)}) async-start(f32[128,24,128]{2,1,0:T(8,128)} %serve.1), calls=%async_computation.1 | async-start | bytes 3145728 | tf_op jit(solution)/shard_map/all_to_all | solution.py:542
  30.3 23.7 %copy-start.3 = (s32[128]{0:T(128)S(1)}, s32[128]{0:T(128)}, u32[]{:S(2)}) copy-start(s32[128]{0:T(128)} %row_ref.1) | copy-start | bytes 1540
  30.3 23.7 %copy-start.4 = (s32[1,128]{1,0:T(1,128)S(1)}, s32[1,128]{1,0:T(1,128)}, u32[]{:S(2)}) copy-start(s32[1,128]{1,0:T(1,128)} %get-tuple-element.22) | copy-start | bytes 1540
  69.2 9.8 %copy-start = (f32[6,256,256]{2,1,0:T(8,128)S(1)}, f32[6,256,256]{2,1,0:T(8,128)}, u32[]{:S(2)}) copy-start(f32[6,256,256]{2,1,0:T(8,128)} %u_ref.3) | copy-start | bytes 4718596
  69.2 33.2 %all-to-all-start.2 = ((f32[128,24,128]{2,1,0:T(8,128)}), f32[128,24,128]{2,1,0:T(8,128)S(1)}, u32[]{:S(2)}, u32[]{:S(2)}) async-start(f32[128,24,128]{2,1,0:T(8,128)} %bitcast.14), calls=%async_computation.2 | async-start | bytes 3145728 | tf_op jit(solution)/shard_map/all_to_all | solution.py:542
  79.5 21.9 %collective-permute-start = (f32[6,256]{1,0:T(8,128)S(1)}, f32[6,256]{1,0:T(8,128)S(1)}, u32[]{:S(2)}, u32[]{:S(2)}) collective-permute-start(f32[6,256]{1,0:T(8,128)S(1)} %get-tuple-element.29), channel_id=1, source_target_pairs={{0,4},{4,8},{8,12},{12,16},{16,20},{20,24},{24,28},{28,32},{32,36}... | collective-permute-start | bytes 18440 | tf_op jit(solution)/shard_map/ppermute | solution.py:534
  79.7 21.7 %collective-permute-start.1 = (f32[6,256]{1,0:T(8,128)S(1)}, f32[6,256]{1,0:T(8,128)S(1)}, u32[]{:S(2)}, u32[]{:S(2)}) collective-permute-start(f32[6,256]{1,0:T(8,128)S(1)} %get-tuple-element.30), channel_id=1, source_target_pairs={{4,0},{8,4},{12,8},{16,12},{20,16},{24,20},{28,24},{32,28},{36,32}... | collective-permute-start | bytes 18440 | tf_op jit(solution)/shard_map/ppermute | solution.py:535
  85.0 16.4 %collective-permute-start.2 = (f32[6,256]{1,0:T(8,128)S(1)}, f32[6,256]{1,0:T(8,128)S(1)}, u32[]{:S(2)}, u32[]{:S(2)}) collective-permute-start(f32[6,256]{1,0:T(8,128)S(1)} %get-tuple-element.31), channel_id=1, source_target_pairs={{0,1},{1,2},{2,3},{3,0},{4,5},{5,6},{6,7},{7,4},{8,9},{9,10},{10,1... | collective-permute-start | bytes 18440 | tf_op jit(solution)/shard_map/ppermute | solution.py:536
  85.6 15.8 %collective-permute-start.3 = (f32[6,256]{1,0:T(8,128)S(1)}, f32[6,256]{1,0:T(8,128)S(1)}, u32[]{:S(2)}, u32[]{:S(2)}) collective-permute-start(f32[6,256]{1,0:T(8,128)S(1)} %get-tuple-element.32), channel_id=1, source_target_pairs={{1,0},{2,1},{3,2},{0,3},{5,4},{6,5},{7,6},{4,7},{9,8},{10,9},{11,1... | collective-permute-start | bytes 18440 | tf_op jit(solution)/shard_map/ppermute | solution.py:537
  102.5 15.1 %copy-start.1 = (f32[6,256,256]{2,1,0:T(8,128)S(1)}, f32[6,256,256]{2,1,0:T(8,128)}, u32[]{:S(2)}) copy-start(f32[6,256,256]{2,1,0:T(8,128)} %get-tuple-element.34.right_ref) | copy-start | bytes 4718596
  102.5 15.1 %copy-start.2 = (f32[256,256]{1,0:T(8,128)S(1)}, f32[256,256]{1,0:T(8,128)}, u32[]{:S(2)}) copy-start(f32[256,256]{1,0:T(8,128)} %get-tuple-element.28.gain_ref) | copy-start | bytes 786436
  105.5 7.3 %collective-permute-start.4 = (f32[6,256]{1,0:T(8,128)S(1)}, f32[6,256]{1,0:T(8,128)S(1)}, u32[]{:S(2)}, u32[]{:S(2)}) collective-permute-start(f32[6,256]{1,0:T(8,128)S(1)} %get-tuple-element.36), channel_id=1, source_target_pairs={{0,4},{4,8},{8,12},{12,16},{16,20},{20,24},{24,28},{28,32},{32,36}... | collective-permute-start | bytes 18440 | tf_op jit(solution)/shard_map/ppermute | solution.py:534
  105.7 7.1 %collective-permute-start.5 = (f32[6,256]{1,0:T(8,128)S(1)}, f32[6,256]{1,0:T(8,128)S(1)}, u32[]{:S(2)}, u32[]{:S(2)}) collective-permute-start(f32[6,256]{1,0:T(8,128)S(1)} %get-tuple-element.37), channel_id=1, source_target_pairs={{4,0},{8,4},{12,8},{16,12},{20,16},{24,20},{28,24},{32,28},{36,32}... | collective-permute-start | bytes 18440 | tf_op jit(solution)/shard_map/ppermute | solution.py:535
  110.8 3.7 %collective-permute-start.6 = (f32[6,256]{1,0:T(8,128)S(1)}, f32[6,256]{1,0:T(8,128)S(1)}, u32[]{:S(2)}, u32[]{:S(2)}) collective-permute-start(f32[6,256]{1,0:T(8,128)S(1)} %get-tuple-element.38), channel_id=1, source_target_pairs={{0,1},{1,2},{2,3},{3,0},{4,5},{5,6},{6,7},{7,4},{8,9},{9,10},{10,1... | collective-permute-start | bytes 18440 | tf_op jit(solution)/shard_map/ppermute | solution.py:536
  112.7 4.9 %collective-permute-start.7 = (f32[6,256]{1,0:T(8,128)S(1)}, f32[6,256]{1,0:T(8,128)S(1)}, u32[]{:S(2)}, u32[]{:S(2)}) collective-permute-start(f32[6,256]{1,0:T(8,128)S(1)} %get-tuple-element.39), channel_id=1, source_target_pairs={{1,0},{2,1},{3,2},{0,3},{5,4},{6,5},{7,6},{4,7},{9,8},{10,9},{11,1... | collective-permute-start | bytes 18440 | tf_op jit(solution)/shard_map/ppermute | solution.py:537

commit v7 on v6

--- a/solution.py
+++ b/solution.py
@@ -219,7 +219,7 @@
 
 def couple_kernel(
     slot_ref, row_ref, high_ref, rest_ref, field_ref, arrived_ref,
-    gap_ref, back_ref, highs, rests, held, held_small, field_here, sems, field_sem,
+    gap_ref, back_ref, highs, rests, held, held_small, field_here, gap_here, sems, field_sem, gap_sem,
 ):
     count = PAIRS // COUPLE_BLOCK
 
@@ -253,7 +253,7 @@
         lines = [field_here[c, pl.ds(r, 1), :] for c in range(3)]
         gap = jnp.concatenate(lines + [empty], axis=0) - pulled
         for c in range(3):
-            gap_ref[c, pl.ds(pair, 1), :] = gap[c : c + 1]
+            gap_here[c, pl.ds(pair, 1), :] = gap[c : c + 1]
         half = PENALTY * gap
         held[p] = two_pieces(half)
         held_small[p] = two_small_pieces(half)
@@ -290,12 +290,14 @@
         return carry
 
     lax.fori_loop(1, count, one, 0)
+    gaps = pltpu.make_async_copy(gap_here, gap_ref, gap_sem)
+    gaps.start()
     for p in range(COUPLE_BLOCK):
         push(count - 1, p)
+    gaps.wait()
 
 
 def couple(slot, slave_row, turned, field, arrived):
-    whole = lambda *_: (0, 0, 0)
     flat = pl.BlockSpec((SLOT_ROWS, 128), lambda *_: (0, 0))
     anywhere = pl.BlockSpec(memory_space=pl.ANY)
     return pl.pallas_call(
@@ -304,14 +306,16 @@
             num_scalar_prefetch=2,
             grid=(1,),
             in_specs=[anywhere, anywhere, anywhere, vmem()],
-            out_specs=[pl.BlockSpec((3, PAIRS, NODES), whole), flat],
+            out_specs=[anywhere, flat],
             scratch_shapes=[
                 pltpu.VMEM((SLOTS, COUPLE_BLOCK, NODES, NODES), bf16),
                 pltpu.VMEM((SLOTS, COUPLE_BLOCK, NODES, NODES), f8),
                 pltpu.VMEM((COUPLE_BLOCK, 16, NODES), bf16),
                 pltpu.VMEM((COUPLE_BLOCK, 32, NODES), f8),
                 pltpu.VMEM((3, ROWS, NODES), f32),
+                pltpu.VMEM((3, PAIRS, NODES), f32),
                 pltpu.SemaphoreType.DMA((2, SLOTS)),
+                pltpu.SemaphoreType.DMA,
                 pltpu.SemaphoreType.DMA,
             ],
         ),
@@ -449,21 +453,20 @@
         [jnp.where(row == asked[k : k + 1], 1.0, 0.0) for k in range(CAP)], axis=1
     ).astype(bf16)
 
-    def force(part):
-        lines = jnp.concatenate(
+    def lines(part):
+        return jnp.concatenate(
             [
                 incoming_ref[pl.ds(k * PARTS + part, DEVICES, stride=CAP * PARTS), :]
                 for k in range(CAP)
             ],
             axis=0,
         )
-        return gathered(hits, lines)
 
     sides = turned_sides(within, hl, hr)
     for c in (3, 4, 5, 0, 1, 2):
         more = rim(within, ha, hb, sides, c)
         if c >= 3:
-            added = jnp.concatenate([force(c - 3), force(c)], axis=1)
+            added = gathered(hits, jnp.concatenate([lines(c - 3), lines(c)], axis=1))
             added_out[c - 3] = added
             more = more + added
         if c == 3:

time: 120 us -> 120 us (level)
  no operation moved by 1% of the time
where the time goes in v7:
time: 120 us
  Pallas kernels  54.8 us (46%)
  starting transfers between devices  30.4 us (25%)
  blocking collectives  18.3 us (15%)
  waiting for transfers between devices  15.1 us (13%)
    pallas_call x1, Pallas kernels, couple_tables(): pl.pallas_call(tables_kernel, grid_spec=pltpu.PrefetchScalarGridSpec(num_...  23.7 us
    all_to_all x1, blocking collectives, all_to_all(): return lax.all_to_all(x, AXES, split_axis=0, concat_axis=0, tiled=True)  18.3 us
    all_to_all x2, starting transfers between devices, all_to_all(): return lax.all_to_all(x, AXES, split_axis=0, concat_axis=0, tiled=True)  15.7 us
    pallas_call x1, Pallas kernels, couple(): pl.pallas_call(couple_kernel, grid_spec=pltpu.PrefetchScalarGridSpec(num_...  15.2 us
    ppermute x2, starting transfers between devices, exchange(): lax.ppermute(top, 'slab', back(slabs))  10.4 us
    ppermute x2, waiting for transfers between devices, exchange(): lax.ppermute(bottom, 'slab', onward(slabs))  9.39 us
    pallas_call x1, Pallas kernels, early_sweep(): pl.pallas_call(early_sweep_kernel, grid=(1,), out_shape=[field, field, pl...  4.97 us
    pallas_call x1, Pallas kernels, serve(): pl.pallas_call(serve_kernel, grid=(SERVE_STEPS,), out_shape=pltpu.HBM((DE...  3.76 us
  transfers between devices with their start and end apart: 10, of which 4 were waited for; matrix products, arithmetic and copies ran while one was open for 0% of the time, Pallas kernels for 24%

profile of v7, /device:TPU:24, one launch (start us, length us, event | category | flops | bytes accessed | tf_op | source)
XLA Modules:
  0.0 119.5 jit_solution(17890856590319469849)
XLA Ops:
  0.6 1.6 %slots.1 = (s32[128,1,128]{2,1,0:T(1,128)}, s32[1,128]{1,0:T(1,128)}) custom-call(s32[1,128]{1,0:T(1,128)} %bitcast.16, s32[1,128]{1,0:T(1,128)} %bitcast.17), custom_call_target="tpu_custom_call" | custom-call | tf_op jit(solution)/shard_map/slots/pallas_call | solution.py:70
  2.2 18.3 %all_to_all.15.asked_ref = s32[128,1,128]{2,1,0:T(1,128)S(1)} all-to-all(s32[128,1,128]{2,1,0:T(1,128)} %get-tuple-element.21), channel_id=1, replica_groups=mesh['slab'=32,'face'=4] {'slab','face'}, dimensions={0} | all-to-all | bytes 131072 | tf_op jit(solution)/shard_map/all_to_all | solution.py:545
  20.6 3.8 %serve.1 = f32[128,24,128]{2,1,0:T(8,128)} custom-call(s32[16384]{0:T(1024)S(1)} %bitcast.11, f32[6,256,256]{2,1,0:T(8,128)} %u_ref.3), custom_call_target="tpu_custom_call" | custom-call | tf_op jit(solution)/shard_map/serve/pallas_call | solution.py:108
  24.3 0.0 copy-start.5
  24.3 5.9 %all-to-all-start.1 = ((f32[128,24,128]{2,1,0:T(8,128)}), f32[128,24,128]{2,1,0:T(8,128)S(1)}, u32[]{:S(2)}, u32[]{:S(2)}) async-start(f32[128,24,128]{2,1,0:T(8,128)} %serve.1), calls=%async_computation.1 | async-start | bytes 3145728 | tf_op jit(solution)/shard_map/all_to_all | solution.py:545
  30.3 0.0 copy-done.5
  30.3 0.0 copy-start.3
  30.3 0.0 copy-start.4
  30.3 23.7 %couple_tables.1 = (bf16[128,256,256]{2,1,0:T(8,128)(2,1)}, f8e5m2[128,256,256]{2,1,0:T(32,128)(4,1)}) custom-call(s32[128]{0:T(128)S(1)} %copy-done.5, f32[128,4,384]{2,1,0:T(4,128)} %coords_ref.1, f32[128,384]{1,0:T(8,128)} %weights_ref.1), custom_call_target="tpu_custom_call" | custom-call | flops 25769803776 | bytes 67108864 | tf_op jit(solution)/shard_map/couple_tables/pallas_call | solution.py:166
  54.0 0.0 all-to-all-done.1
  54.0 0.0 copy-done.3
  54.0 0.0 copy-done.4
  54.0 15.2 %couple.1 = (f32[3,128,256]{2,1,0:T(8,128)}, f32[3072,128]{1,0:T(8,128)}) custom-call(s32[128]{0:T(128)S(1)} %bitcast.13, s32[128]{0:T(128)S(1)} %copy-done.3, bf16[128,256,256]{2,1,0:T(8,128)(2,1)} %get-tuple-element.23.high_ref, f8e5m2[128,256,256]{2,1,0:T(32,128)(4,1)} %get-tuple-element.24.rest_ref, f32[6,256,256]{2,1,0:T(8,128)} %u_ref.3, ...), custom_call_target="tpu_custom_call" | custom-call | tf_op jit(solution)/shard_map/couple/pallas_call | solution.py:303
  69.2 0.0 copy-start
  69.3 9.8 %all-to-all-start.2 = ((f32[128,24,128]{2,1,0:T(8,128)}), f32[128,24,128]{2,1,0:T(8,128)S(1)}, u32[]{:S(2)}, u32[]{:S(2)}) async-start(f32[128,24,128]{2,1,0:T(8,128)} %bitcast.14), calls=%async_computation.2 | async-start | bytes 3145728 | tf_op jit(solution)/shard_map/all_to_all | solution.py:545
  79.0 0.0 copy-done
  79.0 0.5 first_edges.1
  79.5 0.2 collective-permute-start
  79.7 5.3 %collective-permute-start.1 = (f32[6,256]{1,0:T(8,128)S(1)}, f32[6,256]{1,0:T(8,128)S(1)}, u32[]{:S(2)}, u32[]{:S(2)}) collective-permute-start(f32[6,256]{1,0:T(8,128)S(1)} %get-tuple-element.30), channel_id=1, source_target_pairs={{4,0},{8,4},{12,8},{16,12},{20,16},{24,20},{28,24},{32,28},{36,32}... | collective-permute-start | bytes 18440 | tf_op jit(solution)/shard_map/ppermute | solution.py:538
  85.0 0.6 collective-permute-start.2
  85.7 1.4 %collective-permute-start.3 = (f32[6,256]{1,0:T(8,128)S(1)}, f32[6,256]{1,0:T(8,128)S(1)}, u32[]{:S(2)}, u32[]{:S(2)}) collective-permute-start(f32[6,256]{1,0:T(8,128)S(1)} %get-tuple-element.32), channel_id=1, source_target_pairs={{1,0},{2,1},{3,2},{0,3},{5,4},{6,5},{7,6},{4,7},{9,8},{10,9},{11,1... | collective-permute-start | bytes 18440 | tf_op jit(solution)/shard_map/ppermute | solution.py:540
  87.1 5.0 %early_sweep.1 = (f32[6,256,256]{2,1,0:T(8,128)}, f32[6,256,256]{2,1,0:T(8,128)}, f32[256,256]{1,0:T(8,128)}) custom-call(s32[1,128]{1,0:T(1,128)S(1)} %bitcast.12, f32[3,128,256]{2,1,0:T(8,128)} %get-tuple-element.26.gap_ref, f32[6,256,256]{2,1,0:T(8,128)} %u_ref.3, f32[6,256,256]{2,1,0:T(8,128)} %load_ref.1, f32[256,256]{1,0:T(8,128)} %stiff_ref.1), custom_call_target="tpu_custom_call" | custom-call | tf_op jit(solution)/shard_map/early_sweep/pallas_call | solution.py:409
  92.0 9.4 %collective-permute-done.ha = f32[6,256]{1,0:T(8,128)S(1)} collective-permute-done((f32[6,256]{1,0:T(8,128)S(1)}, f32[6,256]{1,0:T(8,128)S(1)}, u32[]{:S(2)}, u32[]{:S(2)}) %collective-permute-start) | collective-permute-done | bytes 6176 | tf_op jit(solution)/shard_map/ppermute | solution.py:537
  101.4 0.0 collective-permute-done.1.hb
  101.4 0.0 collective-permute-done.2.hl
  101.4 0.0 collective-permute-done.3.hr
  101.4 1.0 all-to-all-done.2
  102.5 0.0 copy-start.1
  102.5 0.0 copy-start.2
  102.5 3.1 %master_sweep.1 = (f32[6,256,256]{2,1,0:T(8,128)S(1)}, f32[3,256,256]{2,1,0:T(8,128)S(1)}, f32[6,256]{1,0:T(8,128)S(1)}, f32[6,256]{1,0:T(8,128)S(1)}, f32[6,256]{1,0:T(8,128)S(1)}, /*index=5*/f32[6,256]{1,0:T(8,128)S(1)}) custom-call(s32[128,1,128]{2,1,0:T(1,128)S(1)} %all_to_all.15.asked_ref, f32[3072,128]{1,0:T(8,128)S(1)} %bitcast.9, ...), custom_call_target="tpu_custom_call" | custom-call | tf_op jit(solution)/shard_map/master_sweep/pallas_call | solution.py:482
  105.6 0.1 collective-permute-start.4
  105.7 5.1 %collective-permute-start.5 = (f32[6,256]{1,0:T(8,128)S(1)}, f32[6,256]{1,0:T(8,128)S(1)}, u32[]{:S(2)}, u32[]{:S(2)}) collective-permute-start(f32[6,256]{1,0:T(8,128)S(1)} %get-tuple-element.37), channel_id=1, source_target_pairs={{4,0},{8,4},{12,8},{16,12},{20,16},{24,20},{28,24},{32,28},{36,32}... | collective-permute-start | bytes 18440 | tf_op jit(solution)/shard_map/ppermute | solution.py:538
  110.7 1.9 %collective-permute-start.6 = (f32[6,256]{1,0:T(8,128)S(1)}, f32[6,256]{1,0:T(8,128)S(1)}, u32[]{:S(2)}, u32[]{:S(2)}) collective-permute-start(f32[6,256]{1,0:T(8,128)S(1)} %get-tuple-element.38), channel_id=1, source_target_pairs={{0,1},{1,2},{2,3},{3,0},{4,5},{5,6},{6,7},{7,4},{8,9},{9,10},{10,1... | collective-permute-start | bytes 18440 | tf_op jit(solution)/shard_map/ppermute | solution.py:539
  112.6 0.1 collective-permute-start.7
  112.7 0.0 collective-permute-done.4.ha
  112.7 0.0 collective-permute-done.5.hb
  112.7 1.6 %collective-permute-done.6.hl = f32[6,256]{1,0:T(8,128)S(1)} collective-permute-done((f32[6,256]{1,0:T(8,128)S(1)}, f32[6,256]{1,0:T(8,128)S(1)}, u32[]{:S(2)}, u32[]{:S(2)}) %collective-permute-start.6) | collective-permute-done | bytes 6176 | tf_op jit(solution)/shard_map/ppermute | solution.py:539
  114.4 3.1 %collective-permute-done.7.hr = f32[6,256]{1,0:T(8,128)S(1)} collective-permute-done((f32[6,256]{1,0:T(8,128)S(1)}, f32[6,256]{1,0:T(8,128)S(1)}, u32[]{:S(2)}, u32[]{:S(2)}) %collective-permute-start.7) | collective-permute-done | bytes 6176 | tf_op jit(solution)/shard_map/ppermute | solution.py:540
  117.5 0.0 copy-done.1
  117.5 0.0 copy-done.2
  117.5 2.0 %last_sweep.1 = f32[6,256,256]{2,1,0:T(8,128)} custom-call(f32[6,256,256]{2,1,0:T(8,128)S(1)} %get-tuple-element.33.u_ref, f32[6,256,256]{2,1,0:T(8,128)S(1)} %copy-done.1, f32[3,256,256]{2,1,0:T(8,128)S(1)} %get-tuple-element.35.added_ref, f32[256,256]{1,0:T(8,128)S(1)} %copy-done.2, f32[6,256]{1,0:T(8,128)S(1)} %collective-permute-done.4.ha, ...), custom_call_target="tpu_custom_call" | custom-call | tf_op jit(solution)/shard_map/last_sweep/pallas_call | solution.py:521
Async XLA Ops:
  24.3 6.0 %copy-start.5 = (s32[128]{0:T(128)S(1)}, s32[128]{0:T(128)}, u32[]{:S(2)}) copy-start(s32[128]{0:T(128)} %seg_ref.1) | copy-start | bytes 1540
  24.3 29.7 %all-to-all-start.1 = ((f32[128,24,128]{2,1,0:T(8,128)}), f32[128,24,128]{2,1,0:T(8,128)S(1)}, u32[]{:S(2)}, u32[]{:S(2)}) async-start(f32[128,24,128]{2,1,0:T(8,128)} %serve.1), calls=%async_computation.1 | async-start | bytes 3145728 | tf_op jit(solution)/shard_map/all_to_all | solution.py:545
  30.3 23.7 %copy-start.3 = (s32[128]{0:T(128)S(1)}, s32[128]{0:T(128)}, u32[]{:S(2)}) copy-start(s32[128]{0:T(128)} %row_ref.1) | copy-start | bytes 1540
  30.3 23.7 %copy-start.4 = (s32[1,128]{1,0:T(1,128)S(1)}, s32[1,128]{1,0:T(1,128)}, u32[]{:S(2)}) copy-start(s32[1,128]{1,0:T(1,128)} %get-tuple-element.22) | copy-start | bytes 1540
  69.2 9.8 %copy-start = (f32[6,256,256]{2,1,0:T(8,128)S(1)}, f32[6,256,256]{2,1,0:T(8,128)}, u32[]{:S(2)}) copy-start(f32[6,256,256]{2,1,0:T(8,128)} %u_ref.3) | copy-start | bytes 4718596
  69.3 33.2 %all-to-all-start.2 = ((f32[128,24,128]{2,1,0:T(8,128)}), f32[128,24,128]{2,1,0:T(8,128)S(1)}, u32[]{:S(2)}, u32[]{:S(2)}) async-start(f32[128,24,128]{2,1,0:T(8,128)} %bitcast.14), calls=%async_computation.2 | async-start | bytes 3145728 | tf_op jit(solution)/shard_map/all_to_all | solution.py:545
  79.5 21.9 %collective-permute-start = (f32[6,256]{1,0:T(8,128)S(1)}, f32[6,256]{1,0:T(8,128)S(1)}, u32[]{:S(2)}, u32[]{:S(2)}) collective-permute-start(f32[6,256]{1,0:T(8,128)S(1)} %get-tuple-element.29), channel_id=1, source_target_pairs={{0,4},{4,8},{8,12},{12,16},{16,20},{20,24},{24,28},{28,32},{32,36}... | collective-permute-start | bytes 18440 | tf_op jit(solution)/shard_map/ppermute | solution.py:537
  79.7 21.7 %collective-permute-start.1 = (f32[6,256]{1,0:T(8,128)S(1)}, f32[6,256]{1,0:T(8,128)S(1)}, u32[]{:S(2)}, u32[]{:S(2)}) collective-permute-start(f32[6,256]{1,0:T(8,128)S(1)} %get-tuple-element.30), channel_id=1, source_target_pairs={{4,0},{8,4},{12,8},{16,12},{20,16},{24,20},{28,24},{32,28},{36,32}... | collective-permute-start | bytes 18440 | tf_op jit(solution)/shard_map/ppermute | solution.py:538
  85.0 16.4 %collective-permute-start.2 = (f32[6,256]{1,0:T(8,128)S(1)}, f32[6,256]{1,0:T(8,128)S(1)}, u32[]{:S(2)}, u32[]{:S(2)}) collective-permute-start(f32[6,256]{1,0:T(8,128)S(1)} %get-tuple-element.31), channel_id=1, source_target_pairs={{0,1},{1,2},{2,3},{3,0},{4,5},{5,6},{6,7},{7,4},{8,9},{9,10},{10,1... | collective-permute-start | bytes 18440 | tf_op jit(solution)/shard_map/ppermute | solution.py:539
  85.7 15.8 %collective-permute-start.3 = (f32[6,256]{1,0:T(8,128)S(1)}, f32[6,256]{1,0:T(8,128)S(1)}, u32[]{:S(2)}, u32[]{:S(2)}) collective-permute-start(f32[6,256]{1,0:T(8,128)S(1)} %get-tuple-element.32), channel_id=1, source_target_pairs={{1,0},{2,1},{3,2},{0,3},{5,4},{6,5},{7,6},{4,7},{9,8},{10,9},{11,1... | collective-permute-start | bytes 18440 | tf_op jit(solution)/shard_map/ppermute | solution.py:540
  102.5 15.0 %copy-start.1 = (f32[6,256,256]{2,1,0:T(8,128)S(1)}, f32[6,256,256]{2,1,0:T(8,128)}, u32[]{:S(2)}) copy-start(f32[6,256,256]{2,1,0:T(8,128)} %get-tuple-element.34.right_ref) | copy-start | bytes 4718596
  102.5 15.0 %copy-start.2 = (f32[256,256]{1,0:T(8,128)S(1)}, f32[256,256]{1,0:T(8,128)}, u32[]{:S(2)}) copy-start(f32[256,256]{1,0:T(8,128)} %get-tuple-element.28.gain_ref) | copy-start | bytes 786436
  105.6 7.2 %collective-permute-start.4 = (f32[6,256]{1,0:T(8,128)S(1)}, f32[6,256]{1,0:T(8,128)S(1)}, u32[]{:S(2)}, u32[]{:S(2)}) collective-permute-start(f32[6,256]{1,0:T(8,128)S(1)} %get-tuple-element.36), channel_id=1, source_target_pairs={{0,4},{4,8},{8,12},{12,16},{16,20},{20,24},{24,28},{28,32},{32,36}... | collective-permute-start | bytes 18440 | tf_op jit(solution)/shard_map/ppermute | solution.py:537
  105.7 7.1 %collective-permute-start.5 = (f32[6,256]{1,0:T(8,128)S(1)}, f32[6,256]{1,0:T(8,128)S(1)}, u32[]{:S(2)}, u32[]{:S(2)}) collective-permute-start(f32[6,256]{1,0:T(8,128)S(1)} %get-tuple-element.37), channel_id=1, source_target_pairs={{4,0},{8,4},{12,8},{16,12},{20,16},{24,20},{28,24},{32,28},{36,32}... | collective-permute-start | bytes 18440 | tf_op jit(solution)/shard_map/ppermute | solution.py:538
  110.7 3.7 %collective-permute-start.6 = (f32[6,256]{1,0:T(8,128)S(1)}, f32[6,256]{1,0:T(8,128)S(1)}, u32[]{:S(2)}, u32[]{:S(2)}) collective-permute-start(f32[6,256]{1,0:T(8,128)S(1)} %get-tuple-element.38), channel_id=1, source_target_pairs={{0,1},{1,2},{2,3},{3,0},{4,5},{5,6},{6,7},{7,4},{8,9},{9,10},{10,1... | collective-permute-start | bytes 18440 | tf_op jit(solution)/shard_map/ppermute | solution.py:539
  112.6 4.9 %collective-permute-start.7 = (f32[6,256]{1,0:T(8,128)S(1)}, f32[6,256]{1,0:T(8,128)S(1)}, u32[]{:S(2)}, u32[]{:S(2)}) collective-permute-start(f32[6,256]{1,0:T(8,128)S(1)} %get-tuple-element.39), channel_id=1, source_target_pairs={{1,0},{2,1},{3,2},{0,3},{5,4},{6,5},{7,6},{4,7},{9,8},{10,9},{11,1... | collective-permute-start | bytes 18440 | tf_op jit(solution)/shard_map/ppermute | solution.py:540
